TPU v7x, 128 devices: a whole 4x4x4 slice. The times are simulated.
128 devices in a mesh: dp: 4 (over y_hi, core), fsdp: 32 (over x, z, y_lo).
Axes of the slice: x: 4, y: 4 (y_hi: 2, y_lo: 2; y = y_hi * 2 + y_lo), z: 4, core: 2. Of those that a mesh axis runs over, the one named last changes fastest.
Arguments:
- tokens: bfloat16 [2048, 4096], P('dp', 'fsdp'), may hold values from -6 to 6
- gate_weight: bfloat16 [4096, 16384], P(None, 'fsdp'), may hold values from -0.09375 to 0.09375
- up_weight: bfloat16 [4096, 16384], P(None, 'fsdp'), may hold values from -0.09375 to 0.09375
- down_weight: bfloat16 [16384, 4096], P('fsdp'), may hold values from -0.09375 to 0.09375
- curvature: float32 [2048, 4096], P('dp', 'fsdp'), may hold values from 0.5 to 4
- start: float32 [4096, 16384], P('dp', 'fsdp'), may hold values from -18 to 18
Outputs:
- coefficients: float32 [4], replicated
- next_vector: float32 [4096, 16384], P('dp', 'fsdp')
All inputs are finite; a program needn't handle non-finite values.
Results may differ from a plain program's by a relative error of at most 0.039.
Values may be sent and summed in bfloat16 or wider, within the bound.
No kernel may reach another device: no remote copies, remote signals or barrier semaphores. Data moves between devices by JAX's collectives and lax.ppermute only.
A program may use at most 128 MiB of HBM per device.

v0:
```python
import jax
import jax.numpy as jnp
from jax import lax
from jax.sharding import PartitionSpec as P

D = 4096
FF = 16384


EPS = 1e-06


def shards(tokens, gate_weight, up_weight, down_weight, curvature, start):
    dp_count = lax.axis_size("dp")
    total_tokens = tokens.shape[0] * dp_count
    scale_inv = 1.0 / (D * FF)
    features = lax.all_gather(tokens, "fsdp", axis=1, tiled=True)
    gate = jnp.dot(features, gate_weight, preferred_element_type=jnp.float32)
    up = jnp.dot(features, up_weight, preferred_element_type=jnp.float32)
    sigma = jax.nn.sigmoid(gate)
    slope = sigma * (1.0 + gate * (1.0 - sigma)) * up

    def add_tangent(segment):
        return jnp.dot(features, segment, preferred_element_type=jnp.float32)

    def add_back(segment):
        return lax.dot_general(
            segment, down_weight, (((1,), (1,)), ((), ())), preferred_element_type=jnp.float32
        )

    def curvature_product(vector):
        vector_b = vector.astype(jnp.bfloat16)
        tangent = add_tangent(lax.all_gather(vector_b, "dp", axis=0, tiled=True))
        pushed = (slope * tangent).astype(jnp.bfloat16)
        partial_out = jnp.dot(pushed, down_weight, preferred_element_type=jnp.float32)
        moved = lax.psum_scatter(
            partial_out.astype(jnp.bfloat16), "fsdp", scatter_dimension=1, tiled=True
        ).astype(jnp.float32)
        weighted = (curvature * moved / total_tokens).astype(jnp.bfloat16)
        back = add_back(lax.all_gather(weighted, "fsdp", axis=1, tiled=True))
        delta = (back * slope).astype(jnp.bfloat16)
        return lax.psum_scatter(
            lax.dot_general(
                features, delta, (((0,), (0,)), ((), ())), preferred_element_type=jnp.float32
            ).astype(jnp.bfloat16),
            "dp",
            scatter_dimension=0,
            tiled=True,
        ).astype(jnp.float32)

    def lanczos_update(vectors, image):
        local_proj = jnp.stack([jnp.sum(basis * image) for basis in vectors])
        coeffs = lax.psum(local_proj, ("dp", "fsdp")) * scale_inv
        residual = image
        for index, basis in enumerate(vectors):
            residual = residual - coeffs[index] * basis
        squared = lax.psum(jnp.sum(residual * residual), ("dp", "fsdp")) * scale_inv
        return (coeffs, residual, jnp.sqrt(squared + EPS))

    start_squares = lax.psum(jnp.sum(start * start), ("dp", "fsdp")) * scale_inv
    first = start / jnp.sqrt(start_squares + EPS)
    image_one = curvature_product(first)
    coeffs_one, resid_one, beta_one = lanczos_update([first], image_one)
    second = resid_one / beta_one
    image_two = curvature_product(second)
    coeffs_two, resid_two, beta_two = lanczos_update([second, first], image_two)
    next_vector = resid_two / beta_two
    coefficients = jnp.stack([coeffs_one[0], beta_one, coeffs_two[0], beta_two])
    return (coefficients, next_vector)


def solution(mesh):
    in_specs = (
        P("dp", "fsdp"),
        P(None, "fsdp"),
        P(None, "fsdp"),
        P("fsdp", None),
        P("dp", "fsdp"),
        P("dp", "fsdp"),
    )
    out_specs = (P(), P("dp", "fsdp"))
    return jax.shard_map(shards, mesh=mesh, in_specs=in_specs, out_specs=out_specs, check_vma=False)
```

profile of v0, /device:TPU:1, one launch (start us, length us, event | category | flops | bytes accessed | tf_op | source)
XLA Modules:
  0.0 1322.4 jit_solution(15456304822452983833)
XLA Ops:
  7.2 0.0 all-gather.6.cloned.1.call-start
  7.2 0.7 all-gather.6.cloned.1.call-update
  7.9 0.0 all-gather.8.cloned.1.call-start
  7.9 2.7 multiply_reduce_fusion.2
  10.7 70.5 %psum.35 = f32[]{:T(128)} all-reduce(f32[]{:T(128)} %multiply_reduce_fusion.2), channel_id=1, replica_groups=mesh['dp'=4,'fsdp'=32] {'dp','fsdp'}, use_global_device_ids=true, to_apply=%region_1.0 | all-reduce | flops 1 | bytes 8 | tf_op jit(solution)/shard_map/psum | solution.py:60
  81.2 1.9 copy.10
  83.8 1.3 fusion.14
  85.2 0.0 all-gather.8.cloned.1.call-update
  85.2 0.0 reduce-scatter.13.cloned.1.call-start
  85.2 59.0 %all-gather.6.cloned.1.call-done = bf16[512,4096]{1,0:T(8,128)(2,1)} async-done(((bf16[512,128]{1,0:T(8,128)(2,1)}), bf16[512,4096]{1,0:T(8,128)(2,1)}) %all-gather.6.cloned.1.call-update) | async-done | bytes 4194320 | tf_op jit(solution)/shard_map/all_gather | solution.py:17
  144.2 0.0 copy-start.2
  144.2 5.9 fusion.16
  150.2 0.0 copy-done.2
  150.2 0.0 copy-done.3
  150.2 2.5 convolution_multiply_fusion.2
  152.7 0.0 copy-start.4
  152.7 50.9 %all-gather.8.cloned.1.call-done = bf16[4096,512]{0,1:T(8,128)(2,1)} async-done(((bf16[1024,512]{0,1:T(8,128)(2,1)}), bf16[4096,512]{0,1:T(8,128)(2,1)}) %all-gather.8.cloned.1.call-update) | async-done | bytes 4194320 | tf_op jit(solution)/shard_map/all_gather | solution.py:33
  203.6 11.2 convolution_convert_fusion.3
  214.8 0.0 copy-done.4
  214.8 6.5 copy.12
  221.3 0.0 reduce-scatter.13.cloned.1.call-update
  221.3 0.0 all-gather.10.cloned.1.call-start
  221.4 145.8 %reduce-scatter.13.cloned.1.call-done = bf16[128,512]{1,0:T(8,128)(2,1)} async-done(((bf16[4096,512]{1,0:T(8,128)(2,1)}), bf16[128,512]{1,0:T(8,128)(2,1)}) %reduce-scatter.13.cloned.1.call-update) | async-done | bytes 131088
  367.2 1.0 copy.13
  368.2 0.0 copy-done.1
  368.2 0.7 multiply_convert_fusion.1
  368.9 0.0 all-gather.10.cloned.1.call-update
  368.9 0.2 reduce-scatter.9.cloned.1.call-start
  369.1 149.5 %all-gather.10.cloned.1.call-done = bf16[512,4096]{1,0:T(8,128)(2,1)} async-done(((bf16[512,128]{1,0:T(8,128)(2,1)}), bf16[512,4096]{1,0:T(8,128)(2,1)}) %all-gather.10.cloned.1.call-update) | async-done | bytes 4194320 | tf_op jit(solution)/shard_map/all_gather | solution.py:40
  518.6 11.6 fusion
  530.2 0.0 reduce-scatter.9.cloned.1.call-update
  530.2 0.0 all-gather.12.cloned.1.call-start
  530.3 70.0 %reduce-scatter.9.cloned.1.call-done = bf16[1024,512]{0,1:T(8,128)(2,1)} async-done(((bf16[4096,512]{0,1:T(8,128)(2,1)}), bf16[1024,512]{0,1:T(8,128)(2,1)}) %reduce-scatter.9.cloned.1.call-update) | async-done | bytes 1048592 | tf_op jit(solution)/shard_map/reduce_scatter | solution.py:42
  600.3 2.5 fusion.2
  602.8 65.0 %psum.36 = f32[1]{0:T(128)} all-reduce(f32[1]{0:T(128)} %bitcast.2), channel_id=1, replica_groups=mesh['dp'=4,'fsdp'=32] {'dp','fsdp'}, use_global_device_ids=true, to_apply=%region_5.0 | all-reduce | flops 1 | bytes 8 | tf_op jit(solution)/shard_map/psum | solution.py:53
  668.4 2.4 multiply_reduce_fusion.1
  670.8 63.8 %psum.37 = f32[]{:T(128)} all-reduce(f32[]{:T(128)} %multiply_reduce_fusion.1), channel_id=1, replica_groups=mesh['dp'=4,'fsdp'=32] {'dp','fsdp'}, use_global_device_ids=true, to_apply=%region_7.0 | all-reduce | flops 1 | bytes 8 | tf_op jit(solution)/shard_map/psum | solution.py:57
  735.3 0.0 copy-done
  735.4 1.5 fusion.13
  736.8 0.0 all-gather.12.cloned.1.call-update
  736.9 0.3 reduce-scatter.15.cloned.1.call-start
  737.1 35.2 %all-gather.12.cloned.1.call-done = bf16[4096,512]{0,1:T(8,128)(2,1)} async-done(((bf16[1024,512]{0,1:T(8,128)(2,1)}), bf16[4096,512]{0,1:T(8,128)(2,1)}) %all-gather.12.cloned.1.call-update) | async-done | bytes 4194320 | tf_op jit(solution)/shard_map/all_gather | solution.py:33
  772.3 11.5 convolution_convert_fusion.1
  783.8 6.5 copy.14
  790.3 0.0 reduce-scatter.15.cloned.1.call-update
  790.4 0.0 all-gather.14.cloned.1.call-start
  790.4 143.6 %reduce-scatter.15.cloned.1.call-done = bf16[128,512]{1,0:T(8,128)(2,1)} async-done(((bf16[4096,512]{1,0:T(8,128)(2,1)}), bf16[128,512]{1,0:T(8,128)(2,1)}) %reduce-scatter.15.cloned.1.call-update) | async-done | bytes 131088
  934.0 1.0 copy.15
  935.1 0.7 multiply_convert_fusion
  935.8 0.0 all-gather.14.cloned.1.call-update
  935.8 0.0 reduce-scatter.11.cloned.1.call-start
  935.8 151.7 %all-gather.14.cloned.1.call-done = bf16[512,4096]{1,0:T(8,128)(2,1)} async-done(((bf16[512,128]{1,0:T(8,128)(2,1)}), bf16[512,4096]{1,0:T(8,128)(2,1)}) %all-gather.14.cloned.1.call-update) | async-done | bytes 4194320 | tf_op jit(solution)/shard_map/all_gather | solution.py:40
  1087.5 11.6 fusion.1
  1099.1 0.0 reduce-scatter.11.cloned.1.call-update
  1099.1 70.5 %reduce-scatter.11.cloned.1.call-done = bf16[1024,512]{0,1:T(8,128)(2,1)} async-done(((bf16[4096,512]{0,1:T(8,128)(2,1)}), bf16[1024,512]{0,1:T(8,128)(2,1)}) %reduce-scatter.11.cloned.1.call-update) | async-done | bytes 1048592 | tf_op jit(solution)/shard_map/reduce_scatter | solution.py:42
  1169.6 2.5 fusion.3
  1172.1 1.4 pad_maximum_fusion
  1173.4 65.0 %psum.38 = f32[2]{0:T(128)S(1)} all-reduce(f32[2]{0:T(128)S(1)} %pad_maximum_fusion), channel_id=1, replica_groups=mesh['dp'=4,'fsdp'=32] {'dp','fsdp'}, use_global_device_ids=true, to_apply=%region_12.0 | all-reduce | flops 2 | bytes 16 | tf_op jit(solution)/shard_map/psum | solution.py:53
  1238.4 0.6 fusion.15
  1239.0 3.8 multiply_reduce_fusion
  1242.8 63.8 %psum.39 = f32[]{:T(128)} all-reduce(f32[]{:T(128)} %multiply_reduce_fusion), channel_id=1, replica_groups=mesh['dp'=4,'fsdp'=32] {'dp','fsdp'}, use_global_device_ids=true, to_apply=%region_14.0 | all-reduce | flops 1 | bytes 8 | tf_op jit(solution)/shard_map/psum | solution.py:57
  1307.3 4.5 broadcast_divide_fusion
  1311.8 2.9 copy.11
  1314.7 1.1 pad_maximum_fusion.1
  (4 shorter events, 0.0 us)
Async XLA Ops:
  7.2 137.1 %all-gather.6.cloned.1.call-start = ((), (), s32[]{:S(2)}) async-start(), calls=%async_computation.4 | async-start | bytes 4325376 | tf_op jit(solution)/shard_map/all_gather | solution.py:17
  7.9 195.7 %all-gather.8.cloned.1.call-start = ((), (), s32[]{:S(2)}) async-start(), calls=%async_computation.5 | async-start | bytes 5242880 | tf_op jit(solution)/shard_map/all_gather | solution.py:33
  85.2 282.0 %reduce-scatter.13.cloned.1.call-start = ((), (), s32[]{:S(2)}) async-start(), calls=%async_computation.11 | async-start | bytes 4325376
  144.2 5.9 copy-start.2
  144.2 5.9 copy-start.3
  152.7 62.1 %copy-start.4 = (f32[512,512]{1,0:T(8,128)}, f32[512,512]{1,0:T(8,128)S(1)}, u32[]{:S(2)}) copy-start(f32[512,512]{1,0:T(8,128)S(1)} %convolution_multiply_fusion.2) | copy-start | bytes 3145732
  221.3 146.9 %copy-start.1 = (f32[512,128]{1,0:T(8,128)S(1)}, f32[512,128]{1,0:T(8,128)}, u32[]{:S(2)}) copy-start(f32[512,128]{1,0:T(8,128)} %param.10) | copy-start | bytes 786436
  221.3 297.3 %all-gather.10.cloned.1.call-start = ((), (), s32[]{:S(2)}) async-start(), calls=%async_computation.6 | async-start | bytes 4325376 | tf_op jit(solution)/shard_map/all_gather | solution.py:40
  368.9 231.4 %reduce-scatter.9.cloned.1.call-start = ((), (), s32[]{:S(2)}) async-start(), calls=%async_computation.7 | async-start | bytes 5242880 | tf_op jit(solution)/shard_map/reduce_scatter | solution.py:42
  530.2 242.1 %all-gather.12.cloned.1.call-start = ((), (), s32[]{:S(2)}) async-start(), calls=%async_computation.8 | async-start | bytes 5242880 | tf_op jit(solution)/shard_map/all_gather | solution.py:33
  600.3 135.0 %copy-start = (bf16[1024,512]{0,1:T(8,128)(2,1)S(1)}, bf16[1024,512]{0,1:T(8,128)(2,1)}, u32[]{:S(2)}) copy-start(bf16[1024,512]{0,1:T(8,128)(2,1)} %reduce-scatter.9.cloned.1.call-done) | copy-start | bytes 3145732
  736.9 197.2 %reduce-scatter.15.cloned.1.call-start = ((), (), s32[]{:S(2)}) async-start(), calls=%async_computation.12 | async-start | bytes 4325376
  790.4 297.1 %all-gather.14.cloned.1.call-start = ((), (), s32[]{:S(2)}) async-start(), calls=%async_computation.9 | async-start | bytes 4325376 | tf_op jit(solution)/shard_map/all_gather | solution.py:40
  935.8 233.8 %reduce-scatter.11.cloned.1.call-start = ((), (), s32[]{:S(2)}) async-start(), calls=%async_computation.10 | async-start | bytes 5242880 | tf_op jit(solution)/shard_map/reduce_scatter | solution.py:42
Sparse Core Ops, SparseCore 0:
  9.6 134.6 all-gather.5
  145.9 57.6 all-gather.7
  221.4 145.6 reduce-scatter.12
  369.0 149.5 all-gather.9
  530.3 69.9 reduce-scatter.8
  737.0 35.2 all-gather.11
  790.5 143.4 reduce-scatter.14
  935.9 151.5 all-gather.13
  1099.2 70.2 reduce-scatter.10
where the time goes:
time: 1320 us
  waiting for transfers between devices  877 us (66%)
  blocking collectives  328 us (25%)
  matrix products  54.3 us (4%)
  other arithmetic  25.1 us (2%)
  local copies, waits for them, and re-layouts  20.5 us (2%)
  between operations  16.7 us (1%)
    all_gather x2, waiting for transfers between devices, curvature_product(): back = add_back(lax.all_gather(weighted, 'fsdp', axis=1, tiled=True))  301 us
    unnamed x11, waiting for transfers between devices  290 us
    reduce_scatter x2, waiting for transfers between devices, curvature_product(): lax.psum_scatter(lax.dot_general(features, delta, (((0,), (0,)), ((), ())...  140 us
    psum x2, blocking collectives, lanczos_update(): coeffs = lax.psum(local_proj, ('dp', 'fsdp')) * scale_inv  130 us
    psum x2, blocking collectives, lanczos_update(): squared = lax.psum(jnp.sum(residual * residual), ('dp', 'fsdp')) * scale_inv  128 us
    all_gather x2, waiting for transfers between devices, curvature_product(): tangent = add_tangent(lax.all_gather(vector_b, 'dp', axis=0, tiled=True))  86.1 us
    psum x1, blocking collectives, shards(): start_squares = lax.psum(jnp.sum(start * start), ('dp', 'fsdp')) * scale_inv  70.5 us
    all_gather x1, waiting for transfers between devices, shards(): features = lax.all_gather(tokens, 'fsdp', axis=1, tiled=True)  59 us
  transfers between devices with their start and end apart: 9, of which 9 were waited for; matrix products, arithmetic and copies ran while one was open for 1% of the time, Pallas kernels for 0%

commit v1 on v0

v1 whole, which is shorter than its diff:
```python
import functools
import jax
import jax.numpy as jnp
from jax import lax
from jax.experimental import pallas as pl
from jax.experimental.pallas import tpu as pltpu
from jax.sharding import Mesh
from jax.sharding import PartitionSpec as P

D = 4096
FF = 16384
EPS = 1e-06
SCALE_INV = 1.0 / (D * FF)
AXES = (("yh", 2), ("c", 2), ("x", 4), ("z", 4), ("yl", 2))
NAMES = tuple(name for name, _ in AXES)
SIZES = dict(AXES)
BF = jnp.bfloat16
F32 = jnp.float32
PARAMS = pltpu.CompilerParams(vmem_limit_bytes=40 * 1024 * 1024)
VM = pl.BlockSpec(memory_space=pltpu.VMEM)
SM = pl.BlockSpec(memory_space=pltpu.SMEM)


def shift(value, axis, by):
    n = SIZES[axis]
    return lax.ppermute(value, axis, [((i + by) % n, i) for i in range(n)])


def ring_pair(jobs):
    up = [shift(v, a, 1) for v, a in jobs]
    down = [shift(v, a, -1) for v, a in jobs]
    out = []
    for (v, a), p, m in zip(jobs, up, down):
        h = v.shape[-2] // 2
        far = [shift(p[..., :h, :], a, 1), shift(m[..., h:, :], a, -1)]
        out.append([v, p, jnp.concatenate(far, axis=-2), m])
    return out


def ring_direct(v, a):
    return [v, shift(v, a, 1), shift(v, a, 2), shift(v, a, 3)]


def assemble_tokens_kernel(pos, *refs):
    a, b, out = refs[:4], refs[4:8], refs[8]
    x, z = pos[0], pos[1]
    h = out.shape[0] // 2
    for i in range(4):
        for j in range(4):
            col = (lax.rem(x + j, 4) * 4 + lax.rem(z + i, 4)) * 256
            out[:h, pl.ds(pl.multiple_of(col, 256), 256)] = a[i][j]
            col = (lax.rem(x + i, 4) * 4 + lax.rem(z + j, 4)) * 256
            out[h:, pl.ds(pl.multiple_of(col, 256), 256)] = b[i][j]


def gather_tokens(pair, pos):
    h = pair.shape[0] // 2
    a, b = ring_pair([(pair[:h], "x"), (pair[h:], "z")])
    a, b = ring_pair([(jnp.stack(a), "z"), (jnp.stack(b), "x")])
    return pl.pallas_call(
        assemble_tokens_kernel,
        out_shape=jax.ShapeDtypeStruct((2 * h, D), BF),
        in_specs=[SM] + [VM] * 8,
        out_specs=VM,
        compiler_params=PARAMS,
        name="assemble",
    )(pos, *a, *b)


def nt(a, b):
    return lax.dot_general(a, b, (((1,), (1,)), ((), ())), preferred_element_type=F32)


def tn(a, b):
    return lax.dot_general(a, b, (((0,), (0,)), ((), ())), preferred_element_type=F32)


def nn(a, b):
    return jnp.dot(a, b, preferred_element_type=F32)


def split_kernel(pos, down, keep, send):
    yl = pos[2]
    for b in range(16):
        keep[:, b * 128:(b + 1) * 128] = down[:, pl.ds(pl.multiple_of((2 * b + yl) * 128, 128), 128)]
        send[:, b * 128:(b + 1) * 128] = down[:, pl.ds(pl.multiple_of((2 * b + 1 - yl) * 128, 128), 128)]


def tangent_kernel(pos, feats, *refs):
    out = refs[4]
    acc = jnp.zeros(out.shape, F32)
    for k in range(4):
        rows = pl.multiple_of(pos[4 + k] * 1024, 1024)
        acc = acc + nn(feats[:, pl.ds(rows, 1024)], refs[k][...])
    out[...] = acc


def partial_kernel(own, other, keep, recv, extra, out):
    h = own.shape[0]
    r = nn(own[...], keep[...]) + nn(other[...], recv[...])
    r = r.astype(BF)
    for i in range(2):
        out[i, :h, :] = r[:, i * 128:(i + 1) * 128]
        if out.shape[1] > h:
            out[i, h:, :] = extra[...]


def push_down(own, other, keep, recv, extra, with_extra):
    rows = own.shape[0] + (16 if with_extra else 0)
    whole = lambda s: pl.BlockSpec(s, lambda i: (0, 0))
    return pl.pallas_call(
        partial_kernel,
        grid=(8,),
        out_shape=jax.ShapeDtypeStruct((16, rows, 128), BF),
        in_specs=[
            whole(own.shape),
            whole(other.shape),
            pl.BlockSpec((keep.shape[0], 256), lambda i: (0, i)),
            pl.BlockSpec((recv.shape[0], 256), lambda i: (0, i)),
            whole(extra.shape),
        ],
        out_specs=pl.BlockSpec((2, rows, 128), lambda i: (i, 0, 0)),
        compiler_params=PARAMS,
        name="push_down",
    )(own, other, keep, recv, extra)


def back_kernel(pos, p0, p1, p2, p3, recv, full, send):
    x, z = pos[0], pos[1]
    for i, p in enumerate((p0, p1, p2, p3)):
        for j in range(4):
            col = (lax.rem(x + j, 4) * 4 + lax.rem(z + i, 4)) * 128
            full[:, pl.ds(pl.multiple_of(col, 128), 128)] = p[j]
    send[...] = nt(full[...], recv[...]).astype(BF)


def pull_back(weighted, pos, keep, recv):
    pieces = ring_direct(jnp.stack(ring_direct(weighted, "x")), "z")
    rows, hid = weighted.shape[0], recv.shape[0]
    full, send = pl.pallas_call(
        back_kernel,
        out_shape=(jax.ShapeDtypeStruct((rows, 2048), BF), jax.ShapeDtypeStruct((rows, hid), BF)),
        in_specs=[SM] + [VM] * 5,
        out_specs=(VM, VM),
        compiler_params=PARAMS,
        name="back_other",
    )(pos, *pieces, recv)
    got = shift(send, "yl", 1)
    return nt(full, keep) + got.astype(F32)


def round_bf(v):
    return lax.reduce_precision(v, 8, 7)


def sum_all(values):
    block = jnp.concatenate([jnp.broadcast_to(v, (1, 128)) for v in values] + [jnp.zeros((8 - len(values), 128), F32)])
    block = jnp.broadcast_to(block[None], (128, 8, 128))
    got = lax.all_to_all(block, NAMES, 0, 0, tiled=True)
    total = jnp.sum(got, axis=0)
    return [total[i, 0] for i in range(len(values))]


def shards(tokens, gate_weight, up_weight, down_weight, curvature, start):
    yh, c, x, z, yl = [lax.axis_index(n).astype(jnp.int32) for n in NAMES]
    dp = yh * 2 + c
    order = [dp, yh * 2 + 1 - c, (1 - yh) * 2 + c, (1 - yh) * 2 + 1 - c]
    pos = jnp.stack([x, z, yl, dp] + order)
    total_tokens = tokens.shape[0] * 4

    def over_dp(v):
        far = shift(v, "yh", 1)
        return [v, shift(v, "c", 1), far, shift(far, "c", 1)]

    other = shift(tokens, "yl", 1)
    pair = jnp.where(
        yl == 0, jnp.concatenate([tokens, other], axis=1), jnp.concatenate([other, tokens], axis=1)
    )
    start_b = over_dp(start.astype(BF))
    keep, send = pl.pallas_call(
        split_kernel,
        out_shape=(jax.ShapeDtypeStruct((512, 2048), BF),) * 2,
        in_specs=[SM, VM],
        out_specs=(VM, VM),
        compiler_params=PARAMS,
        name="split_down",
    )(pos, down_weight)
    recv = shift(send, "yl", 1)
    feats = gather_tokens(pair, pos)

    gate = nn(feats, gate_weight)
    up = nn(feats, up_weight)
    sigma = jax.nn.sigmoid(gate)
    slope = sigma * (1.0 + gate * (1.0 - sigma)) * up
    tan_start = pl.pallas_call(
        tangent_kernel,
        out_shape=jax.ShapeDtypeStruct((512, 512), F32),
        in_specs=[SM] + [VM] * 5,
        out_specs=VM,
        compiler_params=PARAMS,
        name="tangent",
    )(pos, feats, *start_b)
    start_squares = jnp.sum(start * start)

    def spread(tangent, extra, with_extra):
        pushed = (slope * tangent).astype(BF)
        parts = push_down(pushed, shift(pushed, "yl", 1), keep, recv, extra, with_extra)
        got = lax.all_to_all(parts, ("x", "z"), 0, 0, tiled=True)
        return jnp.sum(got.astype(F32), axis=0)

    moved_one = spread(tan_start, jnp.zeros((16, 128), BF), False)
    weighted = (curvature * moved_one / total_tokens).astype(BF)
    delta = (pull_back(weighted, pos, keep, recv) * slope).astype(BF)
    deltas_one = over_dp(delta)

    feats_all = over_dp(feats)
    tan_image = 0.0
    for f, d in zip(feats_all, deltas_one):
        gram = nt(feats, f)
        high = round_bf(gram)
        low = round_bf(gram - high)
        tan_image = tan_image + nn(high.astype(BF), d) + nn(low.astype(BF), d)
    rows_all = [lax.dynamic_slice_in_dim(f, dp * 1024, 1024, axis=1) for f in feats_all]

    def image_of(deltas):
        out = tn(rows_all[0], deltas[0])
        for r, d in zip(rows_all[1:], deltas[1:]):
            out = out + tn(r, d)
        return out

    sums = [start_squares, jnp.sum(tan_start * delta.astype(F32)), jnp.sum(tan_image * delta.astype(F32))]
    sums = jnp.stack([jnp.broadcast_to(v * SCALE_INV, (128,)) for v in sums] + [jnp.zeros((128,), F32)] * 5)
    for axis in ("c", "yh", "yl"):
        sums = sums + shift(sums, axis, 1)
    digits = []
    rest = sums[:4]
    for _ in range(3):
        digit = round_bf(rest)
        digits.append(digit)
        rest = rest - digit
    extra = jnp.concatenate(digits + [jnp.zeros((4, 128), F32)]).astype(BF)

    moved = spread(tan_image, extra, True)
    moved_two = moved[:512]
    tail = moved[512:, 0]
    ss, sw, ww = [tail[i] + tail[4 + i] + tail[8 + i] for i in range(3)]
    norm_sq = ss + EPS
    inv_norm = lax.rsqrt(norm_sq)
    alpha_one = sw / norm_sq
    one_one = ss / norm_sq
    resid_sq = jnp.maximum(ww / norm_sq - alpha_one * alpha_one * (2.0 - one_one), 0.0)
    beta_one = jnp.sqrt(resid_sq + EPS)
    scale_two = inv_norm / beta_one

    weighted = (curvature * ((moved_two - alpha_one * moved_one) * scale_two) / total_tokens).astype(BF)
    delta = (pull_back(weighted, pos, keep, recv) * slope).astype(BF)
    deltas_two = over_dp(delta)
    image_one = image_of(deltas_one)
    image_two = image_of(deltas_two)
    delta_f = delta.astype(F32)
    tan_two = (tan_image - alpha_one * tan_start) * scale_two
    alpha_two, cross, image_sq = [
        v * SCALE_INV
        for v in sum_all(
            [jnp.sum(tan_two * delta_f), jnp.sum(tan_start * delta_f) * inv_norm, jnp.sum(image_two * image_two)]
        )
    ]
    two_two = resid_sq / (resid_sq + EPS)
    one_two = alpha_one * (1.0 - one_one) / beta_one
    resid_two_sq = (
        image_sq
        - alpha_two * alpha_two * (2.0 - two_two)
        - cross * cross * (2.0 - one_one)
        + 2.0 * alpha_two * cross * one_two
    )
    beta_two = jnp.sqrt(jnp.maximum(resid_two_sq, 0.0) + EPS)
    first = start * inv_norm
    second = image_one * scale_two - (alpha_one / beta_one) * first
    next_vector = (image_two - alpha_two * second - cross * first) / beta_two
    coefficients = jnp.stack([alpha_one, beta_one, alpha_two, beta_two])
    return (coefficients, next_vector)


def solution(mesh):
    inner = Mesh(mesh.devices.reshape([n for _, n in AXES]), NAMES)
    dp, fsdp = ("yh", "c"), ("x", "z", "yl")
    in_specs = (P(dp, fsdp), P(None, fsdp), P(None, fsdp), P(fsdp, None), P(dp, fsdp), P(dp, fsdp))
    out_specs = (P(), P(dp, fsdp))
    return jax.shard_map(shards, mesh=inner, in_specs=in_specs, out_specs=out_specs, check_vma=False)
```

time: 1320 us -> 506 us (0.38)
  waiting for transfers between devices: 877 us -> 242 us
  blocking collectives: 328 us -> 60.6 us
  starting transfers between devices: 0.77 us -> 78.3 us
  Pallas kernels: 0 us -> 22.3 us
  other arithmetic: 25.1 us -> 10.9 us
    all_gather x5 -> x0, waiting for transfers between devices: 446 us -> none  [the longest x2 301 us: curvature_product(): back = add_back(lax.all_gather(weighted, 'fsdp', axis=1, tiled=True))]
    psum x5 -> x0, blocking collectives: 328 us -> none  [the longest x2 130 us: lanczos_update(): coeffs = lax.psum(local_proj, ('dp', 'fsdp')) * scale_inv]
    unnamed x11 -> x0, waiting for transfers between devices: 290 us -> none
    ppermute x0 -> x49, waiting for transfers between devices: none -> 235 us  [shift(): return lax.ppermute(value, axis, [((i + by) % n, i) for i in range(n)])]
    reduce_scatter x2 -> x0, waiting for transfers between devices: 140 us -> none  [curvature_product(): lax.psum_scatter(lax.dot_general(features, delta, (((0,), (0,)), ((), ())...]
    ppermute x0 -> x49, starting transfers between devices: none -> 70.4 us  [shift(): return lax.ppermute(value, axis, [((i + by) % n, i) for i in range(n)])]
    all_to_all x0 -> x2, blocking collectives: none -> 60.6 us  [spread(): got = lax.all_to_all(parts, ('x', 'z'), 0, 0, tiled=True)]
    pallas_call x0 -> x7, Pallas kernels: none -> 22.3 us  [the longest x2 9.57 us: push_down(): pl.pallas_call(partial_kernel, grid=(8,), out_shape=jax.ShapeDtypeStruct(...]
  transfers between devices with their start and end apart: 9 -> 50, of which waited for: 9 -> 24; matrix products, arithmetic and copies ran while one was open for 1% -> 9% of each run, Pallas kernels for 0% -> 3%
where the time goes in v1:
time: 506 us; the launch traced here: 498 us
  waiting for transfers between devices  242 us (48%)
  starting transfers between devices  78.3 us (15%)
  blocking collectives  60.6 us (12%)
  matrix products  55.8 us (11%)
  Pallas kernels  22.3 us (4%)
  between operations  16.1 us (3%)
  local copies, waits for them, and re-layouts  12 us (2%)
  other arithmetic  10.9 us (2%)
    ppermute x49, waiting for transfers between devices, shift(): return lax.ppermute(value, axis, [((i + by) % n, i) for i in range(n)])  235 us
    ppermute x49, starting transfers between devices, shift(): return lax.ppermute(value, axis, [((i + by) % n, i) for i in range(n)])  70.4 us
    all_to_all x2, blocking collectives, spread(): got = lax.all_to_all(parts, ('x', 'z'), 0, 0, tiled=True)  60.6 us
    dot_general x8, matrix products, tn(): lax.dot_general(a, b, (((0,), (0,)), ((), ())), preferred_element_type=F32)  25.2 us
    dot_general x6, matrix products, nt(): lax.dot_general(a, b, (((1,), (1,)), ((), ())), preferred_element_type=F32)  18 us
    dot_general x10, matrix products, nn(): return jnp.dot(a, b, preferred_element_type=F32)  12.6 us
  transfers between devices with their start and end apart: 50, of which 24 were waited for; matrix products, arithmetic and copies ran while one was open for 9% of the time, Pallas kernels for 3%

profile of v1, /device:TPU:1, one launch (start us, length us, event | category | flops | bytes accessed | tf_op | source)
XLA Modules:
  0.0 497.8 jit_solution(14108601595833588608)
XLA Ops:
  0.6 2.2 collective-permute-start
  2.8 3.0 collective-permute-done
  7.0 4.1 collective-permute-start.9
  11.0 2.5 collective-permute-start.1
  13.5 2.7 collective-permute-start.10
  16.4 3.4 multiply_reduce_fusion.1
  19.8 2.9 collective-permute-start.18
  22.7 2.7 collective-permute-start.2
  25.7 2.7 collective-permute-start.13
  28.4 1.9 collective-permute-done.4
  30.4 2.7 collective-permute-start.5
  33.1 4.1 collective-permute-done.13.refs_5_
  37.2 3.6 collective-permute-start.14
  41.0 2.4 collective-permute-start.6
  45.0 6.7 %collective-permute-start.17 = (bf16[1024,512]{1,0:T(8,128)(2,1)S(1)}, bf16[1024,512]{1,0:T(8,128)(2,1)}, u32[]{:S(2)}, u32[]{:S(2)}) collective-permute-start(bf16[1024,512]{1,0:T(8,128)(2,1)S(1)} %get-tuple-element.21.refs_0_), channel_id=1, source_target_pairs={{32,0},{0,32},{33,1},{1,33},{34,2},{2,34},{35,3},{3,35},{36,4},{4,... | collective-permute-start | bytes 3145736 | tf_op jit(solution)/shard_map/ppermute | solution.py:26
  52.6 2.2 copy-done.5
  54.8 1.7 split_down.1
  62.7 3.3 fusion.59
  66.1 4.3 tangent.1
  70.4 3.8 multiply_convert_fusion.1
  76.0 28.0 %collective-permute-done.21.recv = bf16[512,2048]{1,0:T(8,128)(2,1)S(1)} collective-permute-done((bf16[512,2048]{1,0:T(8,128)(2,1)S(1)}, bf16[512,2048]{1,0:T(8,128)(2,1)S(1)}, u32[]{:S(2)}, u32[]{:S(2)}) %collective-permute-start.21) | collective-permute-done | bytes 2097184 | tf_op jit(solution)/shard_map/ppermute | solution.py:26
  104.0 101.1 %collective-permute-done.20.other = bf16[512,512]{1,0:T(8,128)(2,1)S(1)} collective-permute-done((bf16[512,512]{1,0:T(8,128)(2,1)S(1)}, bf16[512,512]{1,0:T(8,128)(2,1)S(1)}, u32[]{:S(2)}, u32[]{:S(2)}) %collective-permute-start.20) | collective-permute-done | bytes 524320 | tf_op jit(solution)/shard_map/ppermute | solution.py:26
  205.1 4.2 push_down.2
  209.3 30.6 %all_to_all.15 = bf16[16,512,128]{2,1,0:T(8,128)(2,1)S(1)} all-to-all(bf16[16,512,128]{2,1,0:T(8,128)(2,1)S(1)} %push_down.2), channel_id=1, replica_groups=mesh['yh'=2,'c'=2,'x'=4,'z'=4,'yl'=2] {'x','z'}, dimensions={0} | all-to-all | bytes 4194304 | tf_op jit(solution)/shard_map/all_to_all | solution.py:208
  240.9 2.0 collective-permute-start.22
  243.6 2.6 collective-permute-done.22
  246.2 2.1 collective-permute-done.23
  249.5 2.5 collective-permute-start.26
  252.5 4.1 collective-permute-start.33
  256.6 2.4 fusion.60
  260.0 15.8 %collective-permute-done.27.p3 = bf16[4,512,128]{2,1,0:T(8,128)(2,1)S(1)} collective-permute-done((bf16[4,512,128]{2,1,0:T(8,128)(2,1)S(1)}, bf16[4,512,128]{2,1,0:T(8,128)(2,1)S(1)}, u32[]{:S(2)}, u32[]{:S(2)}) %collective-permute-start.27) | collective-permute-done | bytes 524320 | tf_op jit(solution)/shard_map/ppermute | solution.py:26
  275.8 2.4 back_other.2
  278.9 2.4 fusion.62
  281.3 2.4 fusion.61
  283.6 7.4 %collective-permute-done.28 = bf16[512,512]{1,0:T(8,128)(2,1)S(1)} collective-permute-done((bf16[512,512]{1,0:T(8,128)(2,1)S(1)}, bf16[512,512]{1,0:T(8,128)(2,1)S(1)}, u32[]{:S(2)}, u32[]{:S(2)}) %collective-permute-start.28) | collective-permute-done | bytes 524320 | tf_op jit(solution)/shard_map/ppermute | solution.py:26
  292.3 1.9 collective-permute-start.30
  296.5 12.6 %collective-permute-done.32 = bf16[512,512]{1,0:T(8,128)(2,1)S(1)} collective-permute-done((bf16[512,512]{1,0:T(8,128)(2,1)S(1)}, bf16[512,512]{1,0:T(8,128)(2,1)S(1)}, u32[]{:S(2)}, u32[]{:S(2)}) %collective-permute-start.32) | collective-permute-done | bytes 524320 | tf_op jit(solution)/shard_map/ppermute | solution.py:26
  311.9 4.5 fusion.63
  317.0 2.5 fusion.9
  324.7 8.8 %collective-permute-done.37 = f32[8,128]{1,0:T(8,128)S(1)} collective-permute-done((f32[8,128]{1,0:T(8,128)S(1)}, f32[8,128]{1,0:T(8,128)S(1)}, u32[]{:S(2)}, u32[]{:S(2)}) %collective-permute-start.37) | collective-permute-done | bytes 4128 | tf_op jit(solution)/shard_map/ppermute | solution.py:26
  334.3 2.0 collective-permute-done.38
  338.0 5.4 %push_down.3 = bf16[16,528,128]{2,1,0:T(8,128)(2,1)S(1)} custom-call(bf16[512,512]{1,0:T(8,128)(2,1)} %get-tuple-element.22.own, bf16[512,512]{1,0:T(8,128)(2,1)} %collective-permute-done.35.other, bf16[512,2048]{1,0:T(8,128)(2,1)S(1)} %copy-done.2, bf16[512,2048]{1,0:T(8,128)(2,1)S(1)} %collective-permute-done.21.recv, ...), custom_call_target="tpu_custom_call" | custom-call | tf_op jit(solution)/shard_map/push_down/pallas_call | solution.py:111
  343.4 30.0 %all_to_all.16 = bf16[16,528,128]{2,1,0:T(8,128)(2,1)S(1)} all-to-all(bf16[16,528,128]{2,1,0:T(8,128)(2,1)S(1)} %push_down.3), channel_id=1, replica_groups=mesh['yh'=2,'c'=2,'x'=4,'z'=4,'yl'=2] {'x','z'}, dimensions={0} | all-to-all | bytes 4325376 | tf_op jit(solution)/shard_map/all_to_all | solution.py:208
  384.3 1.7 collective-permute-done.39
  386.0 2.7 collective-permute-done.40
  390.5 1.6 collective-permute-start.43
  392.1 6.7 %collective-permute-done.42.p1 = bf16[4,512,128]{2,1,0:T(8,128)(2,1)S(1)} collective-permute-done((bf16[4,512,128]{2,1,0:T(8,128)(2,1)S(1)}, bf16[4,512,128]{2,1,0:T(8,128)(2,1)S(1)}, u32[]{:S(2)}, u32[]{:S(2)}) %collective-permute-start.42) | collective-permute-done | bytes 524320 | tf_op jit(solution)/shard_map/ppermute | solution.py:26
  400.1 15.9 %collective-permute-done.44.p3 = bf16[4,512,128]{2,1,0:T(8,128)(2,1)S(1)} collective-permute-done((bf16[4,512,128]{2,1,0:T(8,128)(2,1)S(1)}, bf16[4,512,128]{2,1,0:T(8,128)(2,1)S(1)}, u32[]{:S(2)}, u32[]{:S(2)}) %collective-permute-start.44) | collective-permute-done | bytes 524320 | tf_op jit(solution)/shard_map/ppermute | solution.py:26
  416.0 3.2 back_other.3
  420.7 11.9 %collective-permute-done.45 = bf16[512,512]{1,0:T(8,128)(2,1)S(1)} collective-permute-done((bf16[512,512]{1,0:T(8,128)(2,1)}, bf16[512,512]{1,0:T(8,128)(2,1)S(1)}, u32[]{:S(2)}, u32[]{:S(2)}) %collective-permute-start.45) | collective-permute-done | bytes 524320 | tf_op jit(solution)/shard_map/ppermute | solution.py:26
  432.6 5.1 %fusion.10 = (f32[]{:T(128)}, f32[]{:T(128)}, bf16[512,512]{1,0:T(8,128)(2,1)S(1)}) fusion(f32[512,512]{1,0:T(8,128)} %get-tuple-element.42, f32[512,512]{1,0:T(8,128)S(1)} %tangent.1, f32[]{:T(128)S(6)} %div.41, f32[]{:T(128)} %div.38, f32[512,512]{1,0:T(8,128)} %copy-done.28, bf16[512,512]{1,0:T(8,128)(2,1)S(1)} %collective-permute-done.45, ...), kind=kOutput, calls=%fused_computation.33 | convolution fusion | flops 1076887552 | bytes 8388624 | tf_op jit(solution)/shard_map/dot_general | solution.py:71
  437.7 3.0 collective-permute-start.47
  440.7 3.3 fusion.30
  444.0 2.4 collective-permute-start.46
  447.0 2.0 fusion.32
  450.3 3.3 collective-permute-start.48
  453.6 2.0 fusion.24
  455.6 2.0 fusion.28
  457.5 2.9 multiply_reduce_fusion
  462.7 7.9 %all-to-all-start.2 = ((f32[128,8,128]{2,1,0:T(8,128)}), f32[128,8,128]{2,1,0:T(8,128)S(1)}, u32[]{:S(2)}, u32[]{:S(2)}) async-start(f32[128,8,128]{2,1,0:T(8,128)} %broadcast_in_dim.26), calls=%async_computation.2 | async-start | bytes 1048576 | tf_op jit(solution)/shard_map/all_to_all | solution.py:159
  470.7 3.3 fusion.22
  474.0 3.4 fusion.26
  477.6 6.6 %all-to-all-done.2 = f32[128,8,128]{2,1,0:T(8,128)S(1)} async-done(((f32[128,8,128]{2,1,0:T(8,128)}), f32[128,8,128]{2,1,0:T(8,128)S(1)}, u32[]{:S(2)}, u32[]{:S(2)}) %all-to-all-start.2) | async-done | bytes 524320 | tf_op jit(solution)/shard_map/all_to_all | solution.py:159
  491.2 6.4 %subtract_divide_fusion = f32[1024,512]{1,0:T(8,128)} fusion(f32[1024,512]{1,0:T(8,128)S(1)} %get-tuple-element.44, f32[1024,512]{1,0:T(8,128)} %param.11, f32[1024,512]{1,0:T(8,128)} %fusion.22, f32[1024,512]{1,0:T(8,128)} %fusion.30, f32[1024,512]{1,0:T(8,128)} %fusion.26, bf16[512,512]{1,0:T(8,128)(2,1)S(1)} %copy-done.26, f32[]{:T(128)} %sqrt.7, ...), kind=kOutput, calls=%fused_computation.2 | convolution fusion | flops 543162368 | bytes 14157328 | tf_op jit(solution)/shard_map/dot_general | solution.py:75
  (188 shorter events, 43.9 us)
Async XLA Ops:
  0.6 5.2 %collective-permute-start = (bf16[512,128]{1,0:T(8,128)(2,1)}, bf16[512,128]{1,0:T(8,128)(2,1)S(1)}, u32[]{:S(2)}, u32[]{:S(2)}) collective-permute-start(bf16[512,128]{1,0:T(8,128)(2,1)} %param.6), channel_id=1, source_target_pairs={{1,0},{0,1},{3,2},{2,3},{5,4},{4,5},{7,6},{6,7},{9,8},{8,9},{11,10... | collective-permute-start | bytes 393224 | tf_op jit(solution)/shard_map/ppermute | solution.py:26
  7.0 6.6 %collective-permute-start.9 = (bf16[256,256]{1,0:T(8,128)(2,1)S(1)}, bf16[256,256]{1,0:T(8,128)(2,1)S(1)}, u32[]{:S(2)}, u32[]{:S(2)}) collective-permute-start(bf16[256,256]{1,0:T(8,128)(2,1)S(1)} %get-tuple-element.34), channel_id=1, source_target_pairs={{2,0},{4,2},{6,4},{0,6},{3,1},{5,3},{7,5},{1,7},{10,8},{12,10},{14... | collective-permute-start | bytes 393224 | tf_op jit(solution)/shard_map/ppermute | solution.py:26
  11.0 5.2 %collective-permute-start.11 = (bf16[256,256]{1,0:T(8,128)(2,1)S(1)}, bf16[256,256]{1,0:T(8,128)(2,1)S(1)}, u32[]{:S(2)}, u32[]{:S(2)}) collective-permute-start(bf16[256,256]{1,0:T(8,128)(2,1)S(1)} %get-tuple-element.34), channel_id=1, source_target_pairs={{6,0},{0,2},{2,4},{4,6},{7,1},{1,3},{3,5},{5,7},{14,8},{8,10},{10,... | collective-permute-start | bytes 393224 | tf_op jit(solution)/shard_map/ppermute | solution.py:26
  11.0 11.7 %collective-permute-start.1 = (bf16[256,256]{1,0:T(8,128)(2,1)S(1)}, bf16[256,256]{1,0:T(8,128)(2,1)S(1)}, u32[]{:S(2)}, u32[]{:S(2)}) collective-permute-start(bf16[256,256]{1,0:T(8,128)(2,1)S(1)} %get-tuple-element.35), channel_id=1, source_target_pairs={{8,0},{16,8},{24,16},{0,24},{9,1},{17,9},{25,17},{1,25},{10,2},{18... | collective-permute-start | bytes 393224 | tf_op jit(solution)/shard_map/ppermute | solution.py:26
  13.5 11.9 %collective-permute-start.3 = (bf16[256,256]{1,0:T(8,128)(2,1)S(1)}, bf16[256,256]{1,0:T(8,128)(2,1)S(1)}, u32[]{:S(2)}, u32[]{:S(2)}) collective-permute-start(bf16[256,256]{1,0:T(8,128)(2,1)S(1)} %get-tuple-element.35), channel_id=1, source_target_pairs={{24,0},{0,8},{8,16},{16,24},{25,1},{1,9},{9,17},{17,25},{26,2},{2,... | collective-permute-start | bytes 393224 | tf_op jit(solution)/shard_map/ppermute | solution.py:26
  13.5 12.0 %collective-permute-start.10 = (bf16[128,256]{1,0:T(8,128)(2,1)S(1)}, bf16[128,256]{1,0:T(8,128)(2,1)S(1)}, u32[]{:S(2)}, u32[]{:S(2)}) collective-permute-start(bf16[128,256]{1,0:T(8,128)(2,1)S(1)} %slice.121), channel_id=1, source_target_pairs={{2,0},{4,2},{6,4},{0,6},{3,1},{5,3},{7,5},{1,7},{10,8},{12,10},{14... | collective-permute-start | bytes 196616 | tf_op jit(solution)/shard_map/ppermute | solution.py:26
  16.3 9.3 %collective-permute-start.12 = (bf16[128,256]{1,0:T(8,128)(2,1)S(1)}, bf16[128,256]{1,0:T(8,128)(2,1)S(1)}, u32[]{:S(2)}, u32[]{:S(2)}) collective-permute-start(bf16[128,256]{1,0:T(8,128)(2,1)S(1)} %slice.122), channel_id=1, source_target_pairs={{6,0},{0,2},{2,4},{4,6},{7,1},{1,3},{3,5},{5,7},{14,8},{8,10},{10,... | collective-permute-start | bytes 196616 | tf_op jit(solution)/shard_map/ppermute | solution.py:26
  19.8 25.2 %copy-start.3 = (bf16[1024,512]{1,0:T(8,128)(2,1)}, bf16[1024,512]{1,0:T(8,128)(2,1)S(1)}, u32[]{:S(2)}) copy-start(bf16[1024,512]{1,0:T(8,128)(2,1)S(1)} %get-tuple-element.21.refs_0_) | copy-start | bytes 3145732
  19.8 25.2 %collective-permute-start.18 = (bf16[1024,512]{1,0:T(8,128)(2,1)S(1)}, bf16[1024,512]{1,0:T(8,128)(2,1)}, u32[]{:S(2)}, u32[]{:S(2)}) collective-permute-start(bf16[1024,512]{1,0:T(8,128)(2,1)S(1)} %get-tuple-element.21.refs_0_), channel_id=1, source_target_pairs={{64,0},{0,64},{65,1},{1,65},{66,2},{2,66},{67,3},{3,67},{68,4},{4,... | collective-permute-start | bytes 3145736 | tf_op jit(solution)/shard_map/ppermute | solution.py:26
  22.7 5.7 %collective-permute-start.2 = (bf16[128,256]{1,0:T(8,128)(2,1)S(1)}, bf16[128,256]{1,0:T(8,128)(2,1)S(1)}, u32[]{:S(2)}, u32[]{:S(2)}) collective-permute-start(bf16[128,256]{1,0:T(8,128)(2,1)S(1)} %slice.116), channel_id=1, source_target_pairs={{8,0},{16,8},{24,16},{0,24},{9,1},{17,9},{25,17},{1,25},{10,2},{18... | collective-permute-start | bytes 196616 | tf_op jit(solution)/shard_map/ppermute | solution.py:26
  25.5 4.8 collective-permute-start.4
  25.7 26.1 %copy-start.6 = (bf16[4,256,256]{2,1,0:T(8,128)(2,1)}, bf16[4,256,256]{2,1,0:T(8,128)(2,1)S(1)}, u32[]{:S(2)}) copy-start(bf16[4,256,256]{2,1,0:T(8,128)(2,1)S(1)} %pad_maximum_fusion.2.refs_4_) | copy-start | bytes 1572868
  25.7 11.5 %collective-permute-start.13 = (bf16[4,256,256]{2,1,0:T(8,128)(2,1)S(1)}, bf16[4,256,256]{2,1,0:T(8,128)(2,1)S(1)}, u32[]{:S(2)}, u32[]{:S(2)}) collective-permute-start(bf16[4,256,256]{2,1,0:T(8,128)(2,1)S(1)} %pad_maximum_fusion.2.refs_4_), channel_id=1, source_target_pairs={{8,0},{16,8},{24,16},{0,24},{9,1},{17,9},{25,17},{1,25},{10,2},{18... | collective-permute-start | bytes 1572872 | tf_op jit(solution)/shard_map/ppermute | solution.py:26
  28.4 12.4 %collective-permute-start.15 = (bf16[4,256,256]{2,1,0:T(8,128)(2,1)S(1)}, bf16[4,256,256]{2,1,0:T(8,128)(2,1)S(1)}, u32[]{:S(2)}, u32[]{:S(2)}) collective-permute-start(bf16[4,256,256]{2,1,0:T(8,128)(2,1)S(1)} %pad_maximum_fusion.2.refs_4_), channel_id=1, source_target_pairs={{24,0},{0,8},{8,16},{16,24},{25,1},{1,9},{9,17},{17,25},{26,2},{2,... | collective-permute-start | bytes 1572872 | tf_op jit(solution)/shard_map/ppermute | solution.py:26
  30.3 21.4 %copy-start.8 = (bf16[4,256,256]{2,1,0:T(8,128)(2,1)}, bf16[4,256,256]{2,1,0:T(8,128)(2,1)S(1)}, u32[]{:S(2)}) copy-start(bf16[4,256,256]{2,1,0:T(8,128)(2,1)S(1)} %pad_maximum_fusion.refs_0_) | copy-start | bytes 1572868
  30.4 10.6 %collective-permute-start.5 = (bf16[4,256,256]{2,1,0:T(8,128)(2,1)S(1)}, bf16[4,256,256]{2,1,0:T(8,128)(2,1)S(1)}, u32[]{:S(2)}, u32[]{:S(2)}) collective-permute-start(bf16[4,256,256]{2,1,0:T(8,128)(2,1)S(1)} %pad_maximum_fusion.refs_0_), channel_id=1, source_target_pairs={{2,0},{4,2},{6,4},{0,6},{3,1},{5,3},{7,5},{1,7},{10,8},{12,10},{14... | collective-permute-start | bytes 1572872 | tf_op jit(solution)/shard_map/ppermute | solution.py:26
  33.1 10.3 %collective-permute-start.7 = (bf16[4,256,256]{2,1,0:T(8,128)(2,1)S(1)}, bf16[4,256,256]{2,1,0:T(8,128)(2,1)S(1)}, u32[]{:S(2)}, u32[]{:S(2)}) collective-permute-start(bf16[4,256,256]{2,1,0:T(8,128)(2,1)S(1)} %pad_maximum_fusion.refs_0_), channel_id=1, source_target_pairs={{6,0},{0,2},{2,4},{4,6},{7,1},{1,3},{3,5},{5,7},{14,8},{8,10},{10,... | collective-permute-start | bytes 1572872 | tf_op jit(solution)/shard_map/ppermute | solution.py:26
  37.2 14.6 %copy-start.10 = (bf16[4,256,256]{2,1,0:T(8,128)(2,1)}, bf16[4,256,256]{2,1,0:T(8,128)(2,1)S(1)}, u32[]{:S(2)}) copy-start(bf16[4,256,256]{2,1,0:T(8,128)(2,1)S(1)} %collective-permute-done.13.refs_5_) | copy-start | bytes 1572868
  37.2 14.5 %collective-permute-start.14 = (bf16[4,128,256]{2,1,0:T(8,128)(2,1)S(1)}, bf16[4,128,256]{2,1,0:T(8,128)(2,1)S(1)}, u32[]{:S(2)}, u32[]{:S(2)}) collective-permute-start(bf16[4,128,256]{2,1,0:T(8,128)(2,1)S(1)} %slice.123), channel_id=1, source_target_pairs={{8,0},{16,8},{24,16},{0,24},{9,1},{17,9},{25,17},{1,25},{10,2},{18... | collective-permute-start | bytes 786440 | tf_op jit(solution)/shard_map/ppermute | solution.py:26
  40.8 11.0 %copy-start.12 = (bf16[4,256,256]{2,1,0:T(8,128)(2,1)}, bf16[4,256,256]{2,1,0:T(8,128)(2,1)S(1)}, u32[]{:S(2)}) copy-start(bf16[4,256,256]{2,1,0:T(8,128)(2,1)S(1)} %collective-permute-done.15.refs_7_) | copy-start | bytes 1572868
  40.9 15.7 %collective-permute-start.16 = (bf16[4,128,256]{2,1,0:T(8,128)(2,1)S(1)}, bf16[4,128,256]{2,1,0:T(8,128)(2,1)S(1)}, u32[]{:S(2)}, u32[]{:S(2)}) collective-permute-start(bf16[4,128,256]{2,1,0:T(8,128)(2,1)S(1)} %slice.124), channel_id=1, source_target_pairs={{24,0},{0,8},{8,16},{16,24},{25,1},{1,9},{9,17},{17,25},{26,2},{2,... | collective-permute-start | bytes 786440 | tf_op jit(solution)/shard_map/ppermute | solution.py:26
  40.9 10.9 %copy-start.14 = (bf16[4,256,256]{2,1,0:T(8,128)(2,1)}, bf16[4,256,256]{2,1,0:T(8,128)(2,1)S(1)}, u32[]{:S(2)}) copy-start(bf16[4,256,256]{2,1,0:T(8,128)(2,1)S(1)} %collective-permute-done.5.refs_1_) | copy-start | bytes 1572868
  41.0 18.0 %collective-permute-start.6 = (bf16[4,128,256]{2,1,0:T(8,128)(2,1)S(1)}, bf16[4,128,256]{2,1,0:T(8,128)(2,1)}, u32[]{:S(2)}, u32[]{:S(2)}) collective-permute-start(bf16[4,128,256]{2,1,0:T(8,128)(2,1)S(1)} %slice.118), channel_id=1, source_target_pairs={{2,0},{4,2},{6,4},{0,6},{3,1},{5,3},{7,5},{1,7},{10,8},{12,10},{14... | collective-permute-start | bytes 786440 | tf_op jit(solution)/shard_map/ppermute | solution.py:26
  45.0 14.0 %collective-permute-start.8 = (bf16[4,128,256]{2,1,0:T(8,128)(2,1)}, bf16[4,128,256]{2,1,0:T(8,128)(2,1)}, u32[]{:S(2)}, u32[]{:S(2)}) collective-permute-start(bf16[4,128,256]{2,1,0:T(8,128)(2,1)} %slice.119), channel_id=1, source_target_pairs={{6,0},{0,2},{2,4},{4,6},{7,1},{1,3},{3,5},{5,7},{14,8},{8,10},{10,... | collective-permute-start | bytes 786440 | tf_op jit(solution)/shard_map/ppermute | solution.py:26
  45.0 21.0 %collective-permute-start.17 = (bf16[1024,512]{1,0:T(8,128)(2,1)S(1)}, bf16[1024,512]{1,0:T(8,128)(2,1)}, u32[]{:S(2)}, u32[]{:S(2)}) collective-permute-start(bf16[1024,512]{1,0:T(8,128)(2,1)S(1)} %get-tuple-element.21.refs_0_), channel_id=1, source_target_pairs={{32,0},{0,32},{33,1},{1,33},{34,2},{2,34},{35,3},{3,35},{36,4},{4,... | collective-permute-start | bytes 3145736 | tf_op jit(solution)/shard_map/ppermute | solution.py:26
  52.5 13.5 %collective-permute-start.19 = (bf16[1024,512]{1,0:T(8,128)(2,1)}, bf16[1024,512]{1,0:T(8,128)(2,1)}, u32[]{:S(2)}, u32[]{:S(2)}) collective-permute-start(bf16[1024,512]{1,0:T(8,128)(2,1)} %collective-permute-done.18.refs_2_), channel_id=1, source_target_pairs={{32,0},{0,32},{33,1},{1,33},{34,2},{2,34},{35,3},{3,35},{36,4},{4,... | collective-permute-start | bytes 3145736 | tf_op jit(solution)/shard_map/ppermute | solution.py:26
  56.5 234.5 %copy-start.1 = (bf16[512,2048]{1,0:T(8,128)(2,1)}, bf16[512,2048]{1,0:T(8,128)(2,1)S(1)}, u32[]{:S(2)}) copy-start(bf16[512,2048]{1,0:T(8,128)(2,1)S(1)} %get-tuple-element.8.keep) | copy-start | bytes 6291460
  57.3 46.7 %collective-permute-start.21 = (bf16[512,2048]{1,0:T(8,128)(2,1)S(1)}, bf16[512,2048]{1,0:T(8,128)(2,1)S(1)}, u32[]{:S(2)}, u32[]{:S(2)}) collective-permute-start(bf16[512,2048]{1,0:T(8,128)(2,1)S(1)} %get-tuple-element.9), channel_id=1, source_target_pairs={{1,0},{0,1},{3,2},{2,3},{5,4},{4,5},{7,6},{6,7},{9,8},{8,9},{11,10... | collective-permute-start | bytes 6291464 | tf_op jit(solution)/shard_map/ppermute | solution.py:26
  61.2 250.7 %copy-start = (bf16[512,4096]{1,0:T(8,128)(2,1)}, bf16[512,4096]{1,0:T(8,128)(2,1)S(1)}, u32[]{:S(2)}) copy-start(bf16[512,4096]{1,0:T(8,128)(2,1)S(1)} %assemble.1.feats) | copy-start | bytes 12582916
  61.3 191.3 %collective-permute-start.31 = (bf16[512,4096]{1,0:T(8,128)(2,1)S(1)}, bf16[512,4096]{1,0:T(8,128)(2,1)S(1)}, u32[]{:S(2)}, u32[]{:S(2)}) collective-permute-start(bf16[512,4096]{1,0:T(8,128)(2,1)S(1)} %assemble.1.feats), channel_id=1, source_target_pairs={{64,0},{0,64},{65,1},{1,65},{66,2},{2,66},{67,3},{3,67},{68,4},{4,... | collective-permute-start | bytes 12582920 | tf_op jit(solution)/shard_map/ppermute | solution.py:26
  74.2 242.8 %copy-start.28 = (f32[512,512]{1,0:T(8,128)}, f32[512,512]{1,0:T(8,128)S(1)}, u32[]{:S(2)}) copy-start(f32[512,512]{1,0:T(8,128)S(1)} %get-tuple-element.19) | copy-start | bytes 3145732
  74.2 130.9 %collective-permute-start.20 = (bf16[512,512]{1,0:T(8,128)(2,1)S(1)}, bf16[512,512]{1,0:T(8,128)(2,1)S(1)}, u32[]{:S(2)}, u32[]{:S(2)}) collective-permute-start(bf16[512,512]{1,0:T(8,128)(2,1)S(1)} %get-tuple-element.18.own), channel_id=1, source_target_pairs={{1,0},{0,1},{3,2},{2,3},{5,4},{4,5},{7,6},{6,7},{9,8},{8,9},{11,10... | collective-permute-start | bytes 1572872 | tf_op jit(solution)/shard_map/ppermute | solution.py:26
  74.9 206.3 %collective-permute-start.29 = (bf16[512,4096]{1,0:T(8,128)(2,1)S(1)}, bf16[512,4096]{1,0:T(8,128)(2,1)S(1)}, u32[]{:S(2)}, u32[]{:S(2)}) collective-permute-start(bf16[512,4096]{1,0:T(8,128)(2,1)S(1)} %assemble.1.feats), channel_id=1, source_target_pairs={{32,0},{0,32},{33,1},{1,33},{34,2},{2,34},{35,3},{3,35},{36,4},{4,... | collective-permute-start | bytes 12582920 | tf_op jit(solution)/shard_map/ppermute | solution.py:26
  240.9 5.3 %collective-permute-start.22 = (bf16[512,128]{1,0:T(8,128)(2,1)S(1)}, bf16[512,128]{1,0:T(8,128)(2,1)S(1)}, u32[]{:S(2)}, u32[]{:S(2)}) collective-permute-start(bf16[512,128]{1,0:T(8,128)(2,1)S(1)} %multiply_convert_fusion.2), channel_id=1, source_target_pairs={{8,0},{16,8},{24,16},{0,24},{9,1},{17,9},{25,17},{1,25},{10,2},{18... | collective-permute-start | bytes 393224 | tf_op jit(solution)/shard_map/ppermute | solution.py:26
  242.9 5.4 %collective-permute-start.23 = (bf16[512,128]{1,0:T(8,128)(2,1)S(1)}, bf16[512,128]{1,0:T(8,128)(2,1)S(1)}, u32[]{:S(2)}, u32[]{:S(2)}) collective-permute-start(bf16[512,128]{1,0:T(8,128)(2,1)S(1)} %multiply_convert_fusion.2), channel_id=1, source_target_pairs={{16,0},{24,8},{0,16},{8,24},{17,1},{25,9},{1,17},{9,25},{18,2},{26... | collective-permute-start | bytes 393224 | tf_op jit(solution)/shard_map/ppermute | solution.py:26
  242.9 6.4 %collective-permute-start.24 = (bf16[512,128]{1,0:T(8,128)(2,1)S(1)}, bf16[512,128]{1,0:T(8,128)(2,1)S(1)}, u32[]{:S(2)}, u32[]{:S(2)}) collective-permute-start(bf16[512,128]{1,0:T(8,128)(2,1)S(1)} %multiply_convert_fusion.2), channel_id=1, source_target_pairs={{24,0},{0,8},{8,16},{16,24},{25,1},{1,9},{9,17},{17,25},{26,2},{2,... | collective-permute-start | bytes 393224 | tf_op jit(solution)/shard_map/ppermute | solution.py:26
  249.4 9.6 %collective-permute-start.25 = (bf16[4,512,128]{2,1,0:T(8,128)(2,1)S(1)}, bf16[4,512,128]{2,1,0:T(8,128)(2,1)S(1)}, u32[]{:S(2)}, u32[]{:S(2)}) collective-permute-start(bf16[4,512,128]{2,1,0:T(8,128)(2,1)S(1)} %pad_maximum_fusion.4.p0), channel_id=1, source_target_pairs={{2,0},{4,2},{6,4},{0,6},{3,1},{5,3},{7,5},{1,7},{10,8},{12,10},{14... | collective-permute-start | bytes 1572872 | tf_op jit(solution)/shard_map/ppermute | solution.py:26
  249.5 10.5 %collective-permute-start.26 = (bf16[4,512,128]{2,1,0:T(8,128)(2,1)S(1)}, bf16[4,512,128]{2,1,0:T(8,128)(2,1)S(1)}, u32[]{:S(2)}, u32[]{:S(2)}) collective-permute-start(bf16[4,512,128]{2,1,0:T(8,128)(2,1)S(1)} %pad_maximum_fusion.4.p0), channel_id=1, source_target_pairs={{4,0},{6,2},{0,4},{2,6},{5,1},{7,3},{1,5},{3,7},{12,8},{14,10},{8,... | collective-permute-start | bytes 1572872 | tf_op jit(solution)/shard_map/ppermute | solution.py:26
  252.0 23.8 %collective-permute-start.27 = (bf16[4,512,128]{2,1,0:T(8,128)(2,1)S(1)}, bf16[4,512,128]{2,1,0:T(8,128)(2,1)S(1)}, u32[]{:S(2)}, u32[]{:S(2)}) collective-permute-start(bf16[4,512,128]{2,1,0:T(8,128)(2,1)S(1)} %pad_maximum_fusion.4.p0), channel_id=1, source_target_pairs={{6,0},{0,2},{2,4},{4,6},{7,1},{1,3},{3,5},{5,7},{14,8},{8,10},{10,... | collective-permute-start | bytes 1572872 | tf_op jit(solution)/shard_map/ppermute | solution.py:26
  252.5 26.4 %copy-start.30 = (bf16[512,4096]{1,0:T(8,128)(2,1)}, bf16[512,4096]{1,0:T(8,128)(2,1)S(1)}, u32[]{:S(2)}) copy-start(bf16[512,4096]{1,0:T(8,128)(2,1)S(1)} %collective-permute-done.31) | copy-start | bytes 12582916
  252.5 59.4 %collective-permute-start.33 = (bf16[512,4096]{1,0:T(8,128)(2,1)S(1)}, bf16[512,4096]{1,0:T(8,128)(2,1)}, u32[]{:S(2)}, u32[]{:S(2)}) collective-permute-start(bf16[512,4096]{1,0:T(8,128)(2,1)S(1)} %collective-permute-done.31), channel_id=1, source_target_pairs={{32,0},{0,32},{33,1},{1,33},{34,2},{2,34},{35,3},{3,35},{36,4},{4,... | collective-permute-start | bytes 12582920 | tf_op jit(solution)/shard_map/ppermute | solution.py:26
  278.2 12.8 %collective-permute-start.28 = (bf16[512,512]{1,0:T(8,128)(2,1)S(1)}, bf16[512,512]{1,0:T(8,128)(2,1)S(1)}, u32[]{:S(2)}, u32[]{:S(2)}) collective-permute-start(bf16[512,512]{1,0:T(8,128)(2,1)S(1)} %get-tuple-element.11), channel_id=1, source_target_pairs={{1,0},{0,1},{3,2},{2,3},{5,4},{4,5},{7,6},{6,7},{9,8},{8,9},{11,10... | collective-permute-start | bytes 1572872 | tf_op jit(solution)/shard_map/ppermute | solution.py:26
  292.3 24.7 %copy-start.19 = (bf16[512,512]{1,0:T(8,128)(2,1)}, bf16[512,512]{1,0:T(8,128)(2,1)S(1)}, u32[]{:S(2)}) copy-start(bf16[512,512]{1,0:T(8,128)(2,1)S(1)} %fusion.6) | copy-start | bytes 1572868
  292.3 18.6 %collective-permute-start.30 = (bf16[512,512]{1,0:T(8,128)(2,1)S(1)}, bf16[512,512]{1,0:T(8,128)(2,1)S(1)}, u32[]{:S(2)}, u32[]{:S(2)}) collective-permute-start(bf16[512,512]{1,0:T(8,128)(2,1)S(1)} %fusion.6), channel_id=1, source_target_pairs={{32,0},{0,32},{33,1},{1,33},{34,2},{2,34},{35,3},{3,35},{36,4},{4,... | collective-permute-start | bytes 1572872 | tf_op jit(solution)/shard_map/ppermute | solution.py:26
  294.2 15.0 %collective-permute-start.32 = (bf16[512,512]{1,0:T(8,128)(2,1)S(1)}, bf16[512,512]{1,0:T(8,128)(2,1)S(1)}, u32[]{:S(2)}, u32[]{:S(2)}) collective-permute-start(bf16[512,512]{1,0:T(8,128)(2,1)S(1)} %fusion.6), channel_id=1, source_target_pairs={{64,0},{0,64},{65,1},{1,65},{66,2},{2,66},{67,3},{3,67},{68,4},{4,... | collective-permute-start | bytes 1572872 | tf_op jit(solution)/shard_map/ppermute | solution.py:26
  309.2 7.3 %collective-permute-start.34 = (bf16[512,512]{1,0:T(8,128)(2,1)S(1)}, bf16[512,512]{1,0:T(8,128)(2,1)S(1)}, u32[]{:S(2)}, u32[]{:S(2)}) collective-permute-start(bf16[512,512]{1,0:T(8,128)(2,1)S(1)} %collective-permute-done.32), channel_id=1, source_target_pairs={{32,0},{0,32},{33,1},{1,33},{34,2},{2,34},{35,3},{3,35},{36,4},{4,... | collective-permute-start | bytes 1572872 | tf_op jit(solution)/shard_map/ppermute | solution.py:26
  319.4 17.0 %collective-permute-start.35 = (bf16[512,512]{1,0:T(8,128)(2,1)}, bf16[512,512]{1,0:T(8,128)(2,1)}, u32[]{:S(2)}, u32[]{:S(2)}) collective-permute-start(bf16[512,512]{1,0:T(8,128)(2,1)} %get-tuple-element.22.own), channel_id=1, source_target_pairs={{1,0},{0,1},{3,2},{2,3},{5,4},{4,5},{7,6},{6,7},{9,8},{8,9},{11,10... | collective-permute-start | bytes 1572872 | tf_op jit(solution)/shard_map/ppermute | solution.py:26
  321.9 1.2 collective-permute-start.36
  323.1 10.3 %collective-permute-start.37 = (f32[8,128]{1,0:T(8,128)S(1)}, f32[8,128]{1,0:T(8,128)S(1)}, u32[]{:S(2)}, u32[]{:S(2)}) collective-permute-start(f32[8,128]{1,0:T(8,128)S(1)} %add.135), channel_id=1, source_target_pairs={{64,0},{0,64},{65,1},{1,65},{66,2},{2,66},{67,3},{3,67},{68,4},{4,... | collective-permute-start | bytes 12296 | tf_op jit(solution)/shard_map/ppermute | solution.py:26
  333.5 2.8 collective-permute-start.38
  382.1 3.9 collective-permute-start.39
  383.3 5.4 %collective-permute-start.40 = (bf16[512,128]{1,0:T(8,128)(2,1)S(1)}, bf16[512,128]{1,0:T(8,128)(2,1)S(1)}, u32[]{:S(2)}, u32[]{:S(2)}) collective-permute-start(bf16[512,128]{1,0:T(8,128)(2,1)S(1)} %fusion.46), channel_id=1, source_target_pairs={{16,0},{24,8},{0,16},{8,24},{17,1},{25,9},{1,17},{9,25},{18,2},{26... | collective-permute-start | bytes 393224 | tf_op jit(solution)/shard_map/ppermute | solution.py:26
  384.3 5.7 %collective-permute-start.41 = (bf16[512,128]{1,0:T(8,128)(2,1)S(1)}, bf16[512,128]{1,0:T(8,128)(2,1)S(1)}, u32[]{:S(2)}, u32[]{:S(2)}) collective-permute-start(bf16[512,128]{1,0:T(8,128)(2,1)S(1)} %fusion.46), channel_id=1, source_target_pairs={{24,0},{0,8},{8,16},{16,24},{25,1},{1,9},{9,17},{17,25},{26,2},{2,... | collective-permute-start | bytes 393224 | tf_op jit(solution)/shard_map/ppermute | solution.py:26
  390.1 8.7 %collective-permute-start.42 = (bf16[4,512,128]{2,1,0:T(8,128)(2,1)S(1)}, bf16[4,512,128]{2,1,0:T(8,128)(2,1)S(1)}, u32[]{:S(2)}, u32[]{:S(2)}) collective-permute-start(bf16[4,512,128]{2,1,0:T(8,128)(2,1)S(1)} %pad_maximum_fusion.5.p0), channel_id=1, source_target_pairs={{2,0},{4,2},{6,4},{0,6},{3,1},{5,3},{7,5},{1,7},{10,8},{12,10},{14... | collective-permute-start | bytes 1572872 | tf_op jit(solution)/shard_map/ppermute | solution.py:26
  390.5 9.6 %collective-permute-start.43 = (bf16[4,512,128]{2,1,0:T(8,128)(2,1)S(1)}, bf16[4,512,128]{2,1,0:T(8,128)(2,1)S(1)}, u32[]{:S(2)}, u32[]{:S(2)}) collective-permute-start(bf16[4,512,128]{2,1,0:T(8,128)(2,1)S(1)} %pad_maximum_fusion.5.p0), channel_id=1, source_target_pairs={{4,0},{6,2},{0,4},{2,6},{5,1},{7,3},{1,5},{3,7},{12,8},{14,10},{8,... | collective-permute-start | bytes 1572872 | tf_op jit(solution)/shard_map/ppermute | solution.py:26
  392.1 23.9 %collective-permute-start.44 = (bf16[4,512,128]{2,1,0:T(8,128)(2,1)S(1)}, bf16[4,512,128]{2,1,0:T(8,128)(2,1)S(1)}, u32[]{:S(2)}, u32[]{:S(2)}) collective-permute-start(bf16[4,512,128]{2,1,0:T(8,128)(2,1)S(1)} %pad_maximum_fusion.5.p0), channel_id=1, source_target_pairs={{6,0},{0,2},{2,4},{4,6},{7,1},{1,3},{3,5},{5,7},{14,8},{8,10},{10,... | collective-permute-start | bytes 1572872 | tf_op jit(solution)/shard_map/ppermute | solution.py:26
  420.5 12.1 %collective-permute-start.45 = (bf16[512,512]{1,0:T(8,128)(2,1)}, bf16[512,512]{1,0:T(8,128)(2,1)S(1)}, u32[]{:S(2)}, u32[]{:S(2)}) collective-permute-start(bf16[512,512]{1,0:T(8,128)(2,1)} %get-tuple-element.13), channel_id=1, source_target_pairs={{1,0},{0,1},{3,2},{2,3},{5,4},{4,5},{7,6},{6,7},{9,8},{8,9},{11,10... | collective-permute-start | bytes 1572872 | tf_op jit(solution)/shard_map/ppermute | solution.py:26
  432.6 8.1 %copy-start.20 = (bf16[512,512]{1,0:T(8,128)(2,1)S(1)}, bf16[512,512]{1,0:T(8,128)(2,1)}, u32[]{:S(2)}) copy-start(bf16[512,512]{1,0:T(8,128)(2,1)} %copy-done.19) | copy-start | bytes 1572868
  437.7 12.6 %collective-permute-start.47 = (bf16[512,512]{1,0:T(8,128)(2,1)S(1)}, bf16[512,512]{1,0:T(8,128)(2,1)S(1)}, u32[]{:S(2)}, u32[]{:S(2)}) collective-permute-start(bf16[512,512]{1,0:T(8,128)(2,1)S(1)} %get-tuple-element.45), channel_id=1, source_target_pairs={{64,0},{0,64},{65,1},{1,65},{66,2},{2,66},{67,3},{3,67},{68,4},{4,... | collective-permute-start | bytes 1572872 | tf_op jit(solution)/shard_map/ppermute | solution.py:26
  444.0 11.5 %collective-permute-start.46 = (bf16[512,512]{1,0:T(8,128)(2,1)S(1)}, bf16[512,512]{1,0:T(8,128)(2,1)S(1)}, u32[]{:S(2)}, u32[]{:S(2)}) collective-permute-start(bf16[512,512]{1,0:T(8,128)(2,1)S(1)} %get-tuple-element.45), channel_id=1, source_target_pairs={{32,0},{0,32},{33,1},{1,33},{34,2},{2,34},{35,3},{3,35},{36,4},{4,... | collective-permute-start | bytes 1572872 | tf_op jit(solution)/shard_map/ppermute | solution.py:26
  450.3 7.3 %collective-permute-start.48 = (bf16[512,512]{1,0:T(8,128)(2,1)S(1)}, bf16[512,512]{1,0:T(8,128)(2,1)S(1)}, u32[]{:S(2)}, u32[]{:S(2)}) collective-permute-start(bf16[512,512]{1,0:T(8,128)(2,1)S(1)} %collective-permute-done.47), channel_id=1, source_target_pairs={{32,0},{0,32},{33,1},{1,33},{34,2},{2,34},{35,3},{3,35},{36,4},{4,... | collective-permute-start | bytes 1572872 | tf_op jit(solution)/shard_map/ppermute | solution.py:26
  457.5 13.1 %copy-start.22 = (bf16[512,512]{1,0:T(8,128)(2,1)S(1)}, bf16[512,512]{1,0:T(8,128)(2,1)}, u32[]{:S(2)}) copy-start(bf16[512,512]{1,0:T(8,128)(2,1)} %copy-done.21) | copy-start | bytes 1572868
  462.7 21.4 %all-to-all-start.2 = ((f32[128,8,128]{2,1,0:T(8,128)}), f32[128,8,128]{2,1,0:T(8,128)S(1)}, u32[]{:S(2)}, u32[]{:S(2)}) async-start(f32[128,8,128]{2,1,0:T(8,128)} %broadcast_in_dim.26), calls=%async_computation.2 | async-start | bytes 1048576 | tf_op jit(solution)/shard_map/all_to_all | solution.py:159
  474.0 17.2 %copy-start.26 = (bf16[512,512]{1,0:T(8,128)(2,1)S(1)}, bf16[512,512]{1,0:T(8,128)(2,1)}, u32[]{:S(2)}) copy-start(bf16[512,512]{1,0:T(8,128)(2,1)} %copy-done.25) | copy-start | bytes 1572868
  (23 other events, 60.0 us)

commit v2 on v0

v2 whole, which is shorter than its diff:
```python
import jax
import jax.numpy as jnp
from jax import lax
from jax.experimental import pallas as pl
from jax.experimental.pallas import tpu as pltpu
from jax.sharding import Mesh
from jax.sharding import PartitionSpec as P

D = 4096
FF = 16384
EPS = 1e-06
TOKENS = 2048
SCALE_INV = 1.0 / (D * FF)
AXES = (("yh", 2), ("c", 2), ("x", 4), ("z", 4), ("yl", 2))
NAMES = tuple(name for name, _ in AXES)
SIZES = dict(AXES)
BF = jnp.bfloat16
F32 = jnp.float32
MIB = 1024 * 1024
VM = pl.BlockSpec(memory_space=pltpu.VMEM)
SM = pl.BlockSpec(memory_space=pltpu.SMEM)


def shift(value, axis, by):
    n = SIZES[axis]
    return lax.ppermute(value, axis, [((i + by) % n, i) for i in range(n)])


def ring_pair(jobs):
    up = [shift(v, a, 1) for v, a in jobs]
    down = [shift(v, a, -1) for v, a in jobs]
    out = []
    for (v, a), p, m in zip(jobs, up, down):
        h = v.shape[-2] // 2
        far = [shift(p[..., :h, :], a, 1), shift(m[..., h:, :], a, -1)]
        out.append([v, p, jnp.concatenate(far, axis=-2), m])
    return out


def ring_direct(v, a):
    return [v, shift(v, a, 1), shift(v, a, 2), shift(v, a, 3)]


def after(value, *others):
    return lax.optimization_barrier((value, *others))[0]


def call(kernel, name, out, *operands, mib=16):
    specs = [SM if v.dtype == jnp.int32 else VM for v in operands]
    shapes = [jax.ShapeDtypeStruct(s, t) for s, t in out]
    got = pl.pallas_call(
        kernel,
        out_shape=shapes,
        in_specs=specs,
        out_specs=[VM] * len(shapes),
        compiler_params=pltpu.CompilerParams(vmem_limit_bytes=mib * MIB),
        name=name,
    )(*operands)
    return got if len(got) > 1 else got[0]


def nt(a, b):
    return lax.dot_general(a, b, (((1,), (1,)), ((), ())), preferred_element_type=F32)


def nn(a, b):
    return jnp.dot(a, b, preferred_element_type=F32)


def place(pos, i, j, width):
    return pl.multiple_of((lax.rem(pos[0] + i, 4) * 4 + lax.rem(pos[1] + j, 4)) * width, width)


def total(v):
    return jnp.sum(v, axis=(0, 1), keepdims=True) * SCALE_INV


def row_of(values, rows, width):
    index = lax.broadcasted_iota(jnp.int32, (rows, width), 0)
    out = jnp.zeros((rows, width), F32)
    for i, v in enumerate(values):
        out = jnp.where(index == i, jnp.broadcast_to(v, (rows, width)), out)
    return out


def digits(values, width):
    rows = []
    for v in values:
        for _ in range(3):
            d = v.astype(BF).astype(F32)
            rows.append(d)
            v = v - d
    return row_of(rows, 16, width).astype(BF)


def undigit(rows):
    return [rows[3 * i:3 * i + 1] + rows[3 * i + 1:3 * i + 2] + rows[3 * i + 2:3 * i + 3] for i in range(3)]


def cast_kernel(start, out, squares):
    acc = jnp.zeros((8, 512), F32)
    for i in range(0, 1024, 8):
        v = start[i:i + 8, :]
        acc = acc + v * v
    out[...] = start[...].astype(BF)
    squares[...] = acc


def split_kernel(pos, down, keep, send):
    yl = pos[2]
    for b in range(16):
        keep[:, b * 128:(b + 1) * 128] = down[:, pl.ds(pl.multiple_of((2 * b + yl) * 128, 128), 128)]
        send[:, b * 128:(b + 1) * 128] = down[:, pl.ds(pl.multiple_of((2 * b + 1 - yl) * 128, 128), 128)]


def front_kernel(pos, *refs):
    a, b = refs[:4], refs[4:8]
    gate_w, up_w = refs[8:10]
    rows = refs[10:14]
    feats, slope, tangent, pushed = refs[14:]
    h = feats.shape[0] // 2
    for i in range(4):
        for j in range(4):
            feats[:h, pl.ds(place(pos, j, i, 256), 256)] = a[i][j]
            feats[h:, pl.ds(place(pos, i, j, 256), 256)] = b[i][j]
    gate = nn(feats[...], gate_w[...])
    sigma = 1.0 / (1.0 + jnp.exp(-gate))
    slope[...] = sigma * (1.0 + gate * (1.0 - sigma)) * nn(feats[...], up_w[...])
    acc = jnp.zeros(tangent.shape, F32)
    for k in range(4):
        cols = pl.multiple_of(pos[4 + k] * 1024, 1024)
        acc = acc + nn(feats[:, pl.ds(cols, 1024)], rows[k][...])
    tangent[...] = acc
    pushed[...] = (slope[...] * acc).astype(BF)


def push_kernel(own, other, keep, recv, out):
    for b in range(0, 16, 4):
        cols = slice(b * 128, (b + 4) * 128)
        r = (nn(own[:512], keep[:, cols]) + nn(other[:512], recv[:, cols])).astype(BF)
        for i in range(4):
            out[b + i, :512, :] = r[:, i * 128:(i + 1) * 128]
    if out.shape[1] > 512:
        sums = undigit(own[512:].astype(F32) + other[512:].astype(F32))
        extra = digits(sums, 512)[:, :128]
        for b in range(16):
            out[b, 512:, :] = extra


def weigh_first_kernel(got, curvature, moved, weighted):
    acc = got[0].astype(F32)
    for i in range(1, 16):
        acc = acc + got[i].astype(F32)
    moved[...] = acc
    weighted[...] = (curvature[...] * acc / TOKENS).astype(BF)


def weigh_second_kernel(got, curvature, moved, weighted, scalars):
    acc = got[0, :512, :].astype(F32)
    tail = got[0, 512:, :].astype(F32)
    for i in range(1, 16):
        acc = acc + got[i, :512, :].astype(F32)
        tail = tail + got[i, 512:, :].astype(F32)
    ss, sw, dd = undigit(tail)
    alpha = sw / (ss + EPS)
    scale = lax.rsqrt(dd + 1e-30) * (1.0 / 1024.0)
    weighted[...] = (curvature[...] * ((acc - alpha * moved[...]) * scale) / TOKENS).astype(BF)
    scalars[...] = row_of([ss, sw, scale], 8, 128)


def back_kernel(pos, p0, p1, p2, p3, recv, full, send):
    for i, p in enumerate((p0, p1, p2, p3)):
        for j in range(4):
            full[:, pl.ds(place(pos, j, i, 128), 128)] = p[j]
    send[...] = nt(full[...], recv[...]).astype(BF)


def own_back_kernel(full, keep, out):
    out[...] = nt(full[...], keep[...])


def delta_first_kernel(own, got, slope, tangent, squares, out):
    delta = ((own[...] + got[...].astype(F32)) * slope[...]).astype(BF)
    out[:512, :] = delta
    delta = delta.astype(F32)
    sums = [total(squares[...]), total(tangent[...] * delta), total(delta * (delta * 1.0))]
    out[512:, :] = digits([jnp.broadcast_to(v, (1, 512)) for v in sums], 512)


def delta_second_kernel(own, got, slope, tan_start, tan_image, delta_one, out, sums):
    delta = ((own[...] + got[...].astype(F32)) * slope[...]).astype(BF)
    out[...] = delta
    delta = delta.astype(F32)
    ww = total(tan_image[...] * delta_one[:512].astype(F32))
    sums[...] = row_of([ww, total(tan_start[...] * delta), total(tan_image[...] * delta)], 8, 128)


def gram_kernel(feats, others, out):
    out[...] = nt(feats[...], others[...])


def gram_split_kernel(pos, near, p0, p1, p2, p3, high, low):
    def put(cols, v):
        top = v.astype(BF)
        high[:, cols] = top
        low[:, cols] = (v - top.astype(F32)).astype(BF)

    put(slice(0, 1024), near[...])
    for i, p in enumerate((p0, p1, p2, p3)):
        q = lax.rem(pos[0] + i, 4) * 128
        put(pl.ds(pl.multiple_of(1024 + q, 128), 128), p[:, :128])
        put(pl.ds(pl.multiple_of(1536 + q, 128), 128), p[:, 128:])


def near_tangent_kernel(high, low, d0, d1, out):
    acc = nn(high[:, :512], d0[:512]) + nn(low[:, :512], d0[:512])
    out[...] = acc + nn(high[:, 512:1024], d1[:512]) + nn(low[:, 512:1024], d1[:512])


def far_tangent_kernel(near, high, low, d0, d1, d2, d3, slope, tangent, pushed):
    acc = near[...] + nn(high[:, 1024:1536], d2[:512]) + nn(low[:, 1024:1536], d2[:512])
    acc = acc + nn(high[:, 1536:], d3[:512]) + nn(low[:, 1536:], d3[:512])
    tangent[...] = acc
    pushed[:512, :] = (slope[...] * acc).astype(BF)
    rows = d0[512:].astype(F32) + d1[512:].astype(F32) + d2[512:].astype(F32) + d3[512:].astype(F32)
    pushed[512:, :] = digits(undigit(rows), 512)


def near_image_kernel(r0, r1, d0, d1, out):
    out[...] = nn(r0[...], d0[:512]) + nn(r1[...], d1[:512])


def far_image_kernel(near, r2, r3, d2, d3, out):
    out[...] = near[...] + nn(r2[...], d2[:512]) + nn(r3[...], d3[:512])


def last_image_kernel(near, r2, r3, d2, d3, sums, out, block):
    acc = near[...] + nn(r2[...], d2[...]) + nn(r3[...], d3[...])
    out[...] = acc
    index = lax.broadcasted_iota(jnp.int32, (8, 128), 0)
    block[...] = jnp.where(index == 3, jnp.broadcast_to(total(acc * acc), (8, 128)), sums[...])


def final_kernel(got, scalars, start, image_one, image_two, out, coefficients):
    acc = got[0]
    for i in range(1, 128):
        acc = acc + got[i]
    ss, sw, scale = scalars[0:1], scalars[1:2], scalars[2:3]
    ww, uz, wz, zz = acc[0:1], acc[1:2], acc[2:3], acc[3:4]
    norm_sq = ss + EPS
    norm = jnp.sqrt(norm_sq)
    alpha_one = sw / norm_sq
    one_one = ss / norm_sq
    resid_sq = jnp.maximum(ww / norm_sq - alpha_one * alpha_one * (2.0 - one_one), 0.0)
    beta_one = jnp.sqrt(resid_sq + EPS)
    second = 1.0 / (norm * beta_one)
    image = second / scale
    alpha_two = image * second * (wz - alpha_one * uz)
    cross = image * uz / norm
    two_two = resid_sq / (resid_sq + EPS)
    one_two = alpha_one * (1.0 - one_one) / beta_one
    last_sq = (
        image * image * zz
        - alpha_two * alpha_two * (2.0 - two_two)
        - cross * cross * (2.0 - one_one)
        + 2.0 * alpha_two * cross * one_two
    )
    beta_two = jnp.sqrt(jnp.maximum(last_sq, 0.0) + EPS)
    index = lax.broadcasted_iota(jnp.int32, (1, 128), 1)
    row = jnp.zeros((1, 128), F32)
    for i, v in enumerate((alpha_one, beta_one, alpha_two, beta_two)):
        row = jnp.where(index == i, v, row)
    coefficients[...] = row
    f_two = image / beta_two
    f_one = -alpha_two * second / beta_two
    f_start = (alpha_two * alpha_one / beta_one - cross) / (norm * beta_two)
    for k in range(4):
        cols = slice(k * 128, (k + 1) * 128)
        out[:, cols] = f_two * image_two[:, cols] + f_one * image_one[:, cols] + f_start * start[:, cols]


def pull_back(weighted, pos, keep, recv):
    pieces = ring_direct(jnp.stack(ring_direct(weighted, "x")), "z")
    full, send = call(back_kernel, "back_other", [((512, 2048), BF), ((512, 512), BF)], pos, *pieces, recv)
    got = shift(send, "yl", 1)
    own = call(own_back_kernel, "back_own", [((512, 512), F32)], full, keep)
    return own, got, full


def over_dp(v):
    far = shift(v, "yh", 1)
    return [v, shift(v, "c", 1), far, shift(far, "c", 1)]


def shards(tokens, gate_weight, up_weight, down_weight, curvature, start):
    yh, c, x, z, yl = [lax.axis_index(n).astype(jnp.int32) for n in NAMES]
    dp = yh * 2 + c
    pos = jnp.stack([x, z, yl, dp, dp, yh * 2 + 1 - c, (1 - yh) * 2 + c, (1 - yh) * 2 + 1 - c])

    other = shift(tokens, "yl", 1)
    start_b, squares = call(cast_kernel, "cast_start", [((1024, 512), BF), ((8, 512), F32)], start)
    pair = jnp.where(
        yl == 0, jnp.concatenate([tokens, other], axis=1), jnp.concatenate([other, tokens], axis=1)
    )
    keep, send = call(split_kernel, "split_down", [((512, 2048), BF)] * 2, pos, down_weight)
    a, b = ring_pair([(pair[:256], "x"), (pair[256:], "z")])
    starts = over_dp(start_b)
    recv = shift(after(send, starts[2]), "yl", 1)
    a, b = ring_pair([(jnp.stack(a), "z"), (jnp.stack(b), "x")])
    feats, slope, tan_start, pushed = call(
        front_kernel,
        "front",
        [((512, D), BF), ((512, 512), F32), ((512, 512), F32), ((512, 512), BF)],
        pos, *a, *b, gate_weight, up_weight, *starts,
        mib=32,
    )

    other = shift(pushed, "yl", 1)
    feats_c = shift(feats, "c", 1)
    near_gram = call(
        gram_kernel, "near_gram", [((512, 1024), F32)], after(feats, pushed), jnp.concatenate([feats, feats_c])
    )
    other, near_gram = lax.optimization_barrier((other, near_gram))
    parts = call(push_kernel, "push", [((16, 512, 128), BF)], pushed, other, keep, recv)
    quarter = lax.dynamic_slice_in_dim(feats, x * 128, 128, axis=0)
    quarter = shift(after(quarter, other), "yh", 1)
    quarter_c = shift(quarter, "c", 1)
    got = lax.all_to_all(parts, ("x", "z"), 0, 0, tiled=True)
    moved, weighted = call(weigh_first_kernel, "weigh", [((512, 128), F32), ((512, 128), BF)], got, curvature)
    own, got, full = pull_back(weighted, pos, keep, recv)
    far_gram = call(
        gram_kernel, "far_gram", [((512, 256), F32)], after(feats, own), jnp.concatenate([quarter, quarter_c])
    )
    delta = call(
        delta_first_kernel, "delta", [((528, 512), BF)], own, got, slope, tan_start, squares
    )
    deltas = over_dp(delta)
    high, low = call(
        gram_split_kernel, "gram_split", [((512, 2048), BF)] * 2, pos, near_gram, *ring_direct(far_gram, "x")
    )
    near = call(near_tangent_kernel, "near_tangent", [((512, 512), F32)], high, low, *deltas[:2])
    tan_image, pushed = call(
        far_tangent_kernel,
        "far_tangent",
        [((512, 512), F32), ((528, 512), BF)],
        near, high, low, *deltas, slope,
    )

    other = shift(pushed, "yl", 1)
    parts = call(push_kernel, "push", [((16, 528, 128), BF)], pushed, other, keep, recv)
    theirs = lax.dynamic_slice_in_dim(feats, (1 - yh) * 2048, 2048, axis=1)
    far_rows = shift(after(theirs, other), "yh", 1)
    got = lax.all_to_all(parts, ("x", "z"), 0, 0, tiled=True)
    weighted, scalars = call(
        weigh_second_kernel, "weigh", [((512, 128), BF), ((8, 128), F32)], got, curvature, moved
    )
    own, got, full = pull_back(weighted, pos, keep, recv)
    mine = lambda v, at: lax.dynamic_slice_in_dim(v, at * 1024, 1024, axis=1)
    rows = [mine(feats, dp), mine(feats_c, dp), mine(far_rows, c), shift(mine(far_rows, 1 - c), "c", 1)]
    rows = [after(r, own).T for r in rows]
    first_deltas = deltas
    near = call(near_image_kernel, "near_image", [((1024, 512), F32)], *rows[:2], *first_deltas[:2])
    image_one = call(far_image_kernel, "far_image", [((1024, 512), F32)], near, *rows[2:], *first_deltas[2:])
    delta, sums = call(
        delta_second_kernel,
        "delta",
        [((512, 512), BF), ((8, 128), F32)],
        own, got, slope, tan_start, tan_image, delta,
    )
    deltas = over_dp(delta)
    near = call(near_image_kernel, "near_image", [((1024, 512), F32)], *rows[:2], *deltas[:2])
    image_two, block = call(
        last_image_kernel, "last_image", [((1024, 512), F32), ((8, 128), F32)], near, *rows[2:], *deltas[2:], sums
    )
    got = lax.all_to_all(jnp.broadcast_to(block[None], (128, 8, 128)), NAMES, 0, 0, tiled=True)
    whole = lambda *s: pl.BlockSpec(s, lambda i: (0,) * len(s))
    band = pl.BlockSpec((256, 512), lambda i: (i, 0))
    next_vector, coefficients = pl.pallas_call(
        final_kernel,
        grid=(4,),
        out_shape=[jax.ShapeDtypeStruct((1024, 512), F32), jax.ShapeDtypeStruct((1, 128), F32)],
        in_specs=[whole(128, 8, 128), whole(8, 128), band, band, band],
        out_specs=[band, whole(1, 128)],
        compiler_params=pltpu.CompilerParams(vmem_limit_bytes=16 * MIB),
        name="final",
    )(got, scalars, start, image_one, image_two)
    return (coefficients[0, :4], next_vector)


def solution(mesh):
    inner = Mesh(mesh.devices.reshape([n for _, n in AXES]), NAMES)
    dp, fsdp = ("yh", "c"), ("x", "z", "yl")
    in_specs = (P(dp, fsdp), P(None, fsdp), P(None, fsdp), P(fsdp, None), P(dp, fsdp), P(dp, fsdp))
    out_specs = (P(), P(dp, fsdp))
    return jax.shard_map(shards, mesh=inner, in_specs=in_specs, out_specs=out_specs, check_vma=False)
```

time: 1320 us -> 478 us (0.36)
  waiting for transfers between devices: 877 us -> 246 us
  blocking collectives: 328 us -> 0 us
  starting transfers between devices: 0.77 us -> 86.2 us
  Pallas kernels: 0 us -> 62.7 us
  matrix products: 54.3 us -> 0 us
  local copies, waits for them, and re-layouts: 20.5 us -> 61.5 us
  between operations: 16.7 us -> 1.43 us
  other arithmetic: 25.1 us -> 11.9 us
    all_gather x5 -> x0, waiting for transfers between devices: 446 us -> none  [the longest x2 301 us: curvature_product(): back = add_back(lax.all_gather(weighted, 'fsdp', axis=1, tiled=True))]
    psum x5 -> x0, blocking collectives: 328 us -> none  [the longest x2 130 us: lanczos_update(): coeffs = lax.psum(local_proj, ('dp', 'fsdp')) * scale_inv]
    unnamed x11 -> x0, waiting for transfers between devices: 290 us -> none
    ppermute x0 -> x51, waiting for transfers between devices: none -> 190 us  [shift(): return lax.ppermute(value, axis, [((i + by) % n, i) for i in range(n)])]
    reduce_scatter x2 -> x0, waiting for transfers between devices: 140 us -> none  [curvature_product(): lax.psum_scatter(lax.dot_general(features, delta, (((0,), (0,)), ((), ())...]
    ppermute x0 -> x51, starting transfers between devices: none -> 72.5 us  [shift(): return lax.ppermute(value, axis, [((i + by) % n, i) for i in range(n)])]
    pallas_call x0 -> x23, Pallas kernels: none -> 62.7 us  [the longest x22 59 us: call(): pl.pallas_call(kernel, out_shape=shapes, in_specs=specs, out_specs=[VM] *...]
    all_to_all x0 -> x3, waiting for transfers between devices: none -> 56.3 us  [the longest x2 47.1 us: shards(): got = lax.all_to_all(parts, ('x', 'z'), 0, 0, tiled=True)]
  transfers between devices with their start and end apart: 9 -> 54, of which waited for: 9 -> 32; matrix products, arithmetic and copies ran while one was open for 1% -> 8% of each run, Pallas kernels for 0% -> 8%
where the time goes in v2:
time: 478 us; the launch traced here: 470 us
  waiting for transfers between devices  246 us (51%)
  starting transfers between devices  86.2 us (18%)
  Pallas kernels  62.7 us (13%)
  local copies, waits for them, and re-layouts  61.5 us (13%)
  other arithmetic  11.9 us (2%)
    ppermute x51, waiting for transfers between devices, shift(): return lax.ppermute(value, axis, [((i + by) % n, i) for i in range(n)])  190 us
    ppermute x51, starting transfers between devices, shift(): return lax.ppermute(value, axis, [((i + by) % n, i) for i in range(n)])  72.5 us
    pallas_call x22, Pallas kernels, call(): pl.pallas_call(kernel, out_shape=shapes, in_specs=specs, out_specs=[VM] *...  59 us
    all_to_all x2, waiting for transfers between devices, shards(): got = lax.all_to_all(parts, ('x', 'z'), 0, 0, tiled=True)  47.1 us
    unnamed x74, local copies, waits for them, and re-layouts  29.1 us
    concatenate x1, local copies, waits for them, and re-layouts, shards(): jnp.concatenate([feats, feats_c])  11.8 us
  transfers between devices with their start and end apart: 54, of which 32 were waited for; matrix products, arithmetic and copies ran while one was open for 8% of the time, Pallas kernels for 8%

profile of v2, /device:TPU:1, one launch (start us, length us, event | category | flops | bytes accessed | tf_op | source)
XLA Modules:
  0.0 470.1 jit_solution(15580804126413888485)
XLA Ops:
  0.6 2.2 collective-permute-start
  5.6 2.6 collective-permute-start.18
  8.4 3.8 collective-permute-start.9
  14.2 3.5 collective-permute-start.10
  17.7 2.5 collective-permute-start.1
  20.3 2.2 collective-permute-done.12
  22.6 2.5 collective-permute-start.13
  26.7 3.9 collective-permute-start.17
  30.6 4.1 collective-permute-done.2
  35.7 4.3 collective-permute-start.19
  41.6 4.8 %collective-permute-done.15.refs_7_ = bf16[4,256,256]{2,1,0:T(8,128)(2,1)S(1)} collective-permute-done((bf16[4,256,256]{2,1,0:T(8,128)(2,1)S(1)}, bf16[4,256,256]{2,1,0:T(8,128)(2,1)S(1)}, u32[]{:S(2)}, u32[]{:S(2)}) %collective-permute-start.15) | collective-permute-done | bytes 524320 | tf_op jit(solution)/shard_map/ppermute | solution.py:26
  47.6 6.0 %collective-permute-done.5.refs_1_ = bf16[4,256,256]{2,1,0:T(8,128)(2,1)S(1)} collective-permute-done((bf16[4,256,256]{2,1,0:T(8,128)(2,1)S(1)}, bf16[4,256,256]{2,1,0:T(8,128)(2,1)S(1)}, u32[]{:S(2)}, u32[]{:S(2)}) %collective-permute-start.5) | collective-permute-done | bytes 524320 | tf_op jit(solution)/shard_map/ppermute | solution.py:26
  55.9 2.4 collective-permute-start.6
  63.1 4.7 %collective-permute-done.8 = bf16[4,128,256]{2,1,0:T(8,128)(2,1)} collective-permute-done((bf16[4,128,256]{2,1,0:T(8,128)(2,1)}, bf16[4,128,256]{2,1,0:T(8,128)(2,1)}, u32[]{:S(2)}, u32[]{:S(2)}) %collective-permute-start.8) | collective-permute-done | bytes 262176 | tf_op jit(solution)/shard_map/ppermute | solution.py:26
  69.0 2.2 copy-done.15
  71.1 10.6 %front.1 = (bf16[512,4096]{1,0:T(8,128)(2,1)S(1)}, f32[512,512]{1,0:T(8,128)S(1)}, f32[512,512]{1,0:T(8,128)S(1)}, bf16[512,512]{1,0:T(8,128)(2,1)S(1)}) custom-call(s32[8]{0:T(128)S(1)} %stack.92.pos, bf16[4,256,256]{2,1,0:T(8,128)(2,1)S(1)} %pad_maximum_fusion.2.refs_0_, bf16[4,256,256]{2,1,0:T(8,128)(2,1)S(1)} %collective-permute-done.5.refs_1_, ...), custom_call_target="tpu_custom_call" | custom-call | tf_op jit(solution)/shard_map/front/pallas_call | solution.py:51
  81.7 2.0 copy-done
  86.5 6.5 %copy.8 = bf16[512,4096]{0,1:T(8,128)(2,1)} copy(bf16[512,4096]{1,0:T(8,128)(2,1)} %copy-done) | data formatting | bytes 8388608 | tf_op jit(solution)/shard_map/front/pallas_call | solution.py:51
  93.0 2.3 collective-permute-start.21
  95.2 2.2 copy-done.16
  97.4 3.0 split_down.1
  102.4 8.0 %pad_maximum_fusion = bf16[1024,4096]{0,1:T(8,128)(2,1)} fusion(bf16[512,4096]{0,1:T(8,128)(2,1)} %collective-permute-done.21, bf16[512,4096]{0,1:T(8,128)(2,1)} %copy.8), kind=kLoop, calls=%fused_computation | loop fusion | flops 16777216 | bytes 16777216 | tf_op jit(solution)/shard_map/concatenate | solution.py:321
  110.3 11.8 %copy.11.others = bf16[1024,4096]{1,0:T(8,128)(2,1)} copy(bf16[1024,4096]{0,1:T(8,128)(2,1)} %pad_maximum_fusion) | data formatting | bytes 16777216 | tf_op jit(solution)/shard_map/concatenate | solution.py:321
  122.1 2.2 copy-done.1
  124.3 3.4 copy-done.3
  127.7 4.5 near_gram.1.near
  133.5 25.6 %collective-permute-done.20.other = bf16[512,512]{1,0:T(8,128)(2,1)S(1)} collective-permute-done((bf16[512,512]{1,0:T(8,128)(2,1)S(1)}, bf16[512,512]{1,0:T(8,128)(2,1)S(1)}, u32[]{:S(2)}, u32[]{:S(2)}) %collective-permute-start.20) | collective-permute-done | bytes 524320 | tf_op jit(solution)/shard_map/ppermute | solution.py:26
  159.1 4.0 push.2
  164.4 4.6 all-to-all-start
  169.0 2.3 constant_dynamic-slice_fusion.4
  171.9 24.1 %all-to-all-done.got = bf16[16,512,128]{2,1,0:T(8,128)(2,1)} async-done(((bf16[16,512,128]{2,1,0:T(8,128)(2,1)}), bf16[16,512,128]{2,1,0:T(8,128)(2,1)}, u32[]{:S(2)}, u32[]{:S(2)}) %all-to-all-start) | async-done | bytes 2097184 | tf_op jit(solution)/shard_map/all_to_all | solution.py:328
  201.9 2.7 collective-permute-done.24
  205.8 5.8 %collective-permute-start.26 = (bf16[4,512,128]{2,1,0:T(8,128)(2,1)S(1)}, bf16[4,512,128]{2,1,0:T(8,128)(2,1)S(1)}, u32[]{:S(2)}, u32[]{:S(2)}) collective-permute-start(bf16[4,512,128]{2,1,0:T(8,128)(2,1)S(1)} %pad_maximum_fusion.6.p0), channel_id=1, source_target_pairs={{2,0},{4,2},{6,4},{0,6},{3,1},{5,3},{7,5},{1,7},{10,8},{12,10},{14... | collective-permute-start | bytes 1572872 | tf_op jit(solution)/shard_map/ppermute | solution.py:26
  212.2 20.7 %collective-permute-done.26.p1 = bf16[4,512,128]{2,1,0:T(8,128)(2,1)S(1)} collective-permute-done((bf16[4,512,128]{2,1,0:T(8,128)(2,1)S(1)}, bf16[4,512,128]{2,1,0:T(8,128)(2,1)S(1)}, u32[]{:S(2)}, u32[]{:S(2)}) %collective-permute-start.26) | collective-permute-done | bytes 524320 | tf_op jit(solution)/shard_map/ppermute | solution.py:26
  232.9 4.6 collective-permute-done.28.p3
  237.5 3.5 back_other.2
  244.6 9.1 %collective-permute-done.34.got = bf16[512,512]{1,0:T(8,128)(2,1)S(1)} collective-permute-done((bf16[512,512]{1,0:T(8,128)(2,1)S(1)}, bf16[512,512]{1,0:T(8,128)(2,1)S(1)}, u32[]{:S(2)}, u32[]{:S(2)}) %collective-permute-start.34) | collective-permute-done | bytes 524320 | tf_op jit(solution)/shard_map/ppermute | solution.py:26
  255.0 2.0 collective-permute-start.35
  257.0 10.9 %collective-permute-done.36.d2 = bf16[528,512]{1,0:T(8,128)(2,1)S(1)} collective-permute-done((bf16[528,512]{1,0:T(8,128)(2,1)S(1)}, bf16[528,512]{1,0:T(8,128)(2,1)S(1)}, u32[]{:S(2)}, u32[]{:S(2)}) %collective-permute-start.36) | collective-permute-done | bytes 540704 | tf_op jit(solution)/shard_map/ppermute | solution.py:26
  267.9 2.7 collective-permute-start.37
  275.3 11.4 %collective-permute-done.31.p1 = f32[512,256]{1,0:T(8,128)S(1)} collective-permute-done((f32[512,256]{1,0:T(8,128)S(1)}, f32[512,256]{1,0:T(8,128)S(1)}, u32[]{:S(2)}, u32[]{:S(2)}) %collective-permute-start.31) | collective-permute-done | bytes 524320 | tf_op jit(solution)/shard_map/ppermute | solution.py:26
  288.3 11.7 %collective-permute-done.33.p3 = f32[512,256]{1,0:T(8,128)S(1)} collective-permute-done((f32[512,256]{1,0:T(8,128)S(1)}, f32[512,256]{1,0:T(8,128)S(1)}, u32[]{:S(2)}, u32[]{:S(2)}) %collective-permute-start.33) | collective-permute-done | bytes 524320 | tf_op jit(solution)/shard_map/ppermute | solution.py:26
  306.1 12.4 %collective-permute-done.38.other = bf16[528,512]{1,0:T(8,128)(2,1)S(1)} collective-permute-done((bf16[528,512]{1,0:T(8,128)(2,1)S(1)}, bf16[528,512]{1,0:T(8,128)(2,1)S(1)}, u32[]{:S(2)}, u32[]{:S(2)}) %collective-permute-start.38) | collective-permute-done | bytes 540704 | tf_op jit(solution)/shard_map/ppermute | solution.py:26
  318.5 3.9 push.3
  323.8 4.4 all-to-all-start.1
  328.3 3.1 constant_dynamic-slice_fusion.2
  332.0 23.0 %all-to-all-done.1.got = bf16[16,528,128]{2,1,0:T(8,128)(2,1)} async-done(((bf16[16,528,128]{2,1,0:T(8,128)(2,1)}), bf16[16,528,128]{2,1,0:T(8,128)(2,1)}, u32[]{:S(2)}, u32[]{:S(2)}) %all-to-all-start.1) | async-done | bytes 2162720 | tf_op jit(solution)/shard_map/all_to_all | solution.py:353
  360.6 2.5 collective-permute-done.39
  363.1 2.5 collective-permute-done.40
  366.8 3.3 collective-permute-start.42
  371.8 12.5 %collective-permute-done.42.p1 = bf16[4,512,128]{2,1,0:T(8,128)(2,1)S(1)} collective-permute-done((bf16[4,512,128]{2,1,0:T(8,128)(2,1)S(1)}, bf16[4,512,128]{2,1,0:T(8,128)(2,1)S(1)}, u32[]{:S(2)}, u32[]{:S(2)}) %collective-permute-start.42) | collective-permute-done | bytes 524320 | tf_op jit(solution)/shard_map/ppermute | solution.py:26
  384.3 12.3 %collective-permute-done.44.p3 = bf16[4,512,128]{2,1,0:T(8,128)(2,1)S(1)} collective-permute-done((bf16[4,512,128]{2,1,0:T(8,128)(2,1)S(1)}, bf16[4,512,128]{2,1,0:T(8,128)(2,1)S(1)}, u32[]{:S(2)}, u32[]{:S(2)}) %collective-permute-start.44) | collective-permute-done | bytes 524320 | tf_op jit(solution)/shard_map/ppermute | solution.py:26
  396.6 4.3 back_other.3
  403.0 3.2 constant_dynamic-slice_fusion
  408.3 7.3 %collective-permute-done.45.got = bf16[512,512]{1,0:T(8,128)(2,1)} collective-permute-done((bf16[512,512]{1,0:T(8,128)(2,1)}, bf16[512,512]{1,0:T(8,128)(2,1)}, u32[]{:S(2)}, u32[]{:S(2)}) %collective-permute-start.45) | collective-permute-done | bytes 524320 | tf_op jit(solution)/shard_map/ppermute | solution.py:26
  415.5 2.5 delta.3
  420.1 11.8 %collective-permute-done.49.d2 = bf16[512,512]{1,0:T(8,128)(2,1)} collective-permute-done((bf16[512,512]{1,0:T(8,128)(2,1)}, bf16[512,512]{1,0:T(8,128)(2,1)}, u32[]{:S(2)}, u32[]{:S(2)}) %collective-permute-start.49) | collective-permute-done | bytes 524320 | tf_op jit(solution)/shard_map/ppermute | solution.py:26
  431.9 2.3 collective-permute-start.50
  436.8 2.5 near_image.2.near
  439.4 3.2 last_image.1
  444.7 4.7 all-to-all-start.2
  450.9 2.5 far_image.1.image_one
  453.4 9.2 %all-to-all-done.2.got = f32[128,8,128]{2,1,0:T(8,128)} async-done(((f32[128,8,128]{2,1,0:T(8,128)}), f32[128,8,128]{2,1,0:T(8,128)}, u32[]{:S(2)}, u32[]{:S(2)}) %all-to-all-start.2) | async-done | bytes 524320 | tf_op jit(solution)/shard_map/all_to_all | solution.py:375
  465.7 3.7 final.1
  (171 shorter events, 78.0 us)
Async XLA Ops:
  0.6 7.6 %collective-permute-start = (bf16[512,128]{1,0:T(8,128)(2,1)}, bf16[512,128]{1,0:T(8,128)(2,1)S(1)}, u32[]{:S(2)}, u32[]{:S(2)}) collective-permute-start(bf16[512,128]{1,0:T(8,128)(2,1)} %param.6), channel_id=1, source_target_pairs={{1,0},{0,1},{3,2},{2,3},{5,4},{4,5},{7,6},{6,7},{9,8},{8,9},{11,10... | collective-permute-start | bytes 393224 | tf_op jit(solution)/shard_map/ppermute | solution.py:26
  5.6 30.0 %collective-permute-start.18 = (bf16[1024,512]{1,0:T(8,128)(2,1)}, bf16[1024,512]{1,0:T(8,128)(2,1)}, u32[]{:S(2)}, u32[]{:S(2)}) collective-permute-start(bf16[1024,512]{1,0:T(8,128)(2,1)} %get-tuple-element.39.refs_10_), channel_id=1, source_target_pairs={{64,0},{0,64},{65,1},{1,65},{66,2},{2,66},{67,3},{3,67},{68,4},{4,... | collective-permute-start | bytes 3145736 | tf_op jit(solution)/shard_map/ppermute | solution.py:26
  8.4 5.8 %collective-permute-start.9 = (bf16[256,256]{1,0:T(8,128)(2,1)S(1)}, bf16[256,256]{1,0:T(8,128)(2,1)S(1)}, u32[]{:S(2)}, u32[]{:S(2)}) collective-permute-start(bf16[256,256]{1,0:T(8,128)(2,1)S(1)} %get-tuple-element.80), channel_id=1, source_target_pairs={{2,0},{4,2},{6,4},{0,6},{3,1},{5,3},{7,5},{1,7},{10,8},{12,10},{14... | collective-permute-start | bytes 393224 | tf_op jit(solution)/shard_map/ppermute | solution.py:26
  12.2 5.4 %collective-permute-start.11 = (bf16[256,256]{1,0:T(8,128)(2,1)S(1)}, bf16[256,256]{1,0:T(8,128)(2,1)S(1)}, u32[]{:S(2)}, u32[]{:S(2)}) collective-permute-start(bf16[256,256]{1,0:T(8,128)(2,1)S(1)} %get-tuple-element.80), channel_id=1, source_target_pairs={{6,0},{0,2},{2,4},{4,6},{7,1},{1,3},{3,5},{5,7},{14,8},{8,10},{10,... | collective-permute-start | bytes 393224 | tf_op jit(solution)/shard_map/ppermute | solution.py:26
  14.2 6.1 %collective-permute-start.10 = (bf16[128,256]{1,0:T(8,128)(2,1)S(1)}, bf16[128,256]{1,0:T(8,128)(2,1)S(1)}, u32[]{:S(2)}, u32[]{:S(2)}) collective-permute-start(bf16[128,256]{1,0:T(8,128)(2,1)S(1)} %slice.50), channel_id=1, source_target_pairs={{2,0},{4,2},{6,4},{0,6},{3,1},{5,3},{7,5},{1,7},{10,8},{12,10},{14... | collective-permute-start | bytes 196616 | tf_op jit(solution)/shard_map/ppermute | solution.py:26
  17.7 4.8 %collective-permute-start.12 = (bf16[128,256]{1,0:T(8,128)(2,1)S(1)}, bf16[128,256]{1,0:T(8,128)(2,1)S(1)}, u32[]{:S(2)}, u32[]{:S(2)}) collective-permute-start(bf16[128,256]{1,0:T(8,128)(2,1)S(1)} %slice.51), channel_id=1, source_target_pairs={{6,0},{0,2},{2,4},{4,6},{7,1},{1,3},{3,5},{5,7},{14,8},{8,10},{10,... | collective-permute-start | bytes 196616 | tf_op jit(solution)/shard_map/ppermute | solution.py:26
  17.7 7.4 %collective-permute-start.1 = (bf16[256,256]{1,0:T(8,128)(2,1)S(1)}, bf16[256,256]{1,0:T(8,128)(2,1)S(1)}, u32[]{:S(2)}, u32[]{:S(2)}) collective-permute-start(bf16[256,256]{1,0:T(8,128)(2,1)S(1)} %get-tuple-element.81), channel_id=1, source_target_pairs={{8,0},{16,8},{24,16},{0,24},{9,1},{17,9},{25,17},{1,25},{10,2},{18... | collective-permute-start | bytes 393224 | tf_op jit(solution)/shard_map/ppermute | solution.py:26
  20.3 5.5 %collective-permute-start.3 = (bf16[256,256]{1,0:T(8,128)(2,1)S(1)}, bf16[256,256]{1,0:T(8,128)(2,1)S(1)}, u32[]{:S(2)}, u32[]{:S(2)}) collective-permute-start(bf16[256,256]{1,0:T(8,128)(2,1)S(1)} %get-tuple-element.81), channel_id=1, source_target_pairs={{24,0},{0,8},{8,16},{16,24},{25,1},{1,9},{9,17},{17,25},{26,2},{2,... | collective-permute-start | bytes 393224 | tf_op jit(solution)/shard_map/ppermute | solution.py:26
  22.6 18.9 %collective-permute-start.13 = (bf16[4,256,256]{2,1,0:T(8,128)(2,1)S(1)}, bf16[4,256,256]{2,1,0:T(8,128)(2,1)S(1)}, u32[]{:S(2)}, u32[]{:S(2)}) collective-permute-start(bf16[4,256,256]{2,1,0:T(8,128)(2,1)S(1)} %pad_maximum_fusion.4.refs_4_), channel_id=1, source_target_pairs={{8,0},{16,8},{24,16},{0,24},{9,1},{17,9},{25,17},{1,25},{10,2},{18... | collective-permute-start | bytes 1572872 | tf_op jit(solution)/shard_map/ppermute | solution.py:26
  25.1 9.6 %collective-permute-start.2 = (bf16[128,256]{1,0:T(8,128)(2,1)S(1)}, bf16[128,256]{1,0:T(8,128)(2,1)S(1)}, u32[]{:S(2)}, u32[]{:S(2)}) collective-permute-start(bf16[128,256]{1,0:T(8,128)(2,1)S(1)} %slice.45), channel_id=1, source_target_pairs={{8,0},{16,8},{24,16},{0,24},{9,1},{17,9},{25,17},{1,25},{10,2},{18... | collective-permute-start | bytes 196616 | tf_op jit(solution)/shard_map/ppermute | solution.py:26
  25.8 9.9 %collective-permute-start.4 = (bf16[128,256]{1,0:T(8,128)(2,1)S(1)}, bf16[128,256]{1,0:T(8,128)(2,1)S(1)}, u32[]{:S(2)}, u32[]{:S(2)}) collective-permute-start(bf16[128,256]{1,0:T(8,128)(2,1)S(1)} %slice.46), channel_id=1, source_target_pairs={{24,0},{0,8},{8,16},{16,24},{25,1},{1,9},{9,17},{17,25},{26,2},{2,... | collective-permute-start | bytes 196616 | tf_op jit(solution)/shard_map/ppermute | solution.py:26
  26.7 42.2 %collective-permute-start.17 = (bf16[1024,512]{1,0:T(8,128)(2,1)}, bf16[1024,512]{1,0:T(8,128)(2,1)}, u32[]{:S(2)}, u32[]{:S(2)}) collective-permute-start(bf16[1024,512]{1,0:T(8,128)(2,1)} %get-tuple-element.39.refs_10_), channel_id=1, source_target_pairs={{32,0},{0,32},{33,1},{1,33},{34,2},{2,34},{35,3},{3,35},{36,4},{4,... | collective-permute-start | bytes 3145736 | tf_op jit(solution)/shard_map/ppermute | solution.py:26
  34.7 11.7 %collective-permute-start.15 = (bf16[4,256,256]{2,1,0:T(8,128)(2,1)S(1)}, bf16[4,256,256]{2,1,0:T(8,128)(2,1)S(1)}, u32[]{:S(2)}, u32[]{:S(2)}) collective-permute-start(bf16[4,256,256]{2,1,0:T(8,128)(2,1)S(1)} %pad_maximum_fusion.4.refs_4_), channel_id=1, source_target_pairs={{24,0},{0,8},{8,16},{16,24},{25,1},{1,9},{9,17},{17,25},{26,2},{2,... | collective-permute-start | bytes 1572872 | tf_op jit(solution)/shard_map/ppermute | solution.py:26
  35.7 33.3 %collective-permute-start.19 = (bf16[1024,512]{1,0:T(8,128)(2,1)}, bf16[1024,512]{1,0:T(8,128)(2,1)}, u32[]{:S(2)}, u32[]{:S(2)}) collective-permute-start(bf16[1024,512]{1,0:T(8,128)(2,1)} %collective-permute-done.18.refs_12_), channel_id=1, source_target_pairs={{32,0},{0,32},{33,1},{1,33},{34,2},{2,34},{35,3},{3,35},{36,4},{4,... | collective-permute-start | bytes 3145736 | tf_op jit(solution)/shard_map/ppermute | solution.py:26
  40.0 13.6 %collective-permute-start.5 = (bf16[4,256,256]{2,1,0:T(8,128)(2,1)S(1)}, bf16[4,256,256]{2,1,0:T(8,128)(2,1)S(1)}, u32[]{:S(2)}, u32[]{:S(2)}) collective-permute-start(bf16[4,256,256]{2,1,0:T(8,128)(2,1)S(1)} %pad_maximum_fusion.2.refs_0_), channel_id=1, source_target_pairs={{2,0},{4,2},{6,4},{0,6},{3,1},{5,3},{7,5},{1,7},{10,8},{12,10},{14... | collective-permute-start | bytes 1572872 | tf_op jit(solution)/shard_map/ppermute | solution.py:26
  41.4 14.4 %collective-permute-start.7 = (bf16[4,256,256]{2,1,0:T(8,128)(2,1)S(1)}, bf16[4,256,256]{2,1,0:T(8,128)(2,1)S(1)}, u32[]{:S(2)}, u32[]{:S(2)}) collective-permute-start(bf16[4,256,256]{2,1,0:T(8,128)(2,1)S(1)} %pad_maximum_fusion.2.refs_0_), channel_id=1, source_target_pairs={{6,0},{0,2},{2,4},{4,6},{7,1},{1,3},{3,5},{5,7},{14,8},{8,10},{10,... | collective-permute-start | bytes 1572872 | tf_op jit(solution)/shard_map/ppermute | solution.py:26
  46.4 12.6 %collective-permute-start.14 = (bf16[4,128,256]{2,1,0:T(8,128)(2,1)S(1)}, bf16[4,128,256]{2,1,0:T(8,128)(2,1)S(1)}, u32[]{:S(2)}, u32[]{:S(2)}) collective-permute-start(bf16[4,128,256]{2,1,0:T(8,128)(2,1)S(1)} %slice.52), channel_id=1, source_target_pairs={{8,0},{16,8},{24,16},{0,24},{9,1},{17,9},{25,17},{1,25},{10,2},{18... | collective-permute-start | bytes 786440 | tf_op jit(solution)/shard_map/ppermute | solution.py:26
  53.6 8.3 %collective-permute-start.16 = (bf16[4,128,256]{2,1,0:T(8,128)(2,1)S(1)}, bf16[4,128,256]{2,1,0:T(8,128)(2,1)}, u32[]{:S(2)}, u32[]{:S(2)}) collective-permute-start(bf16[4,128,256]{2,1,0:T(8,128)(2,1)S(1)} %slice.53), channel_id=1, source_target_pairs={{24,0},{0,8},{8,16},{16,24},{25,1},{1,9},{9,17},{17,25},{26,2},{2,... | collective-permute-start | bytes 786440 | tf_op jit(solution)/shard_map/ppermute | solution.py:26
  55.9 7.2 %collective-permute-start.6 = (bf16[4,128,256]{2,1,0:T(8,128)(2,1)}, bf16[4,128,256]{2,1,0:T(8,128)(2,1)}, u32[]{:S(2)}, u32[]{:S(2)}) collective-permute-start(bf16[4,128,256]{2,1,0:T(8,128)(2,1)} %slice.47), channel_id=1, source_target_pairs={{2,0},{4,2},{6,4},{0,6},{3,1},{5,3},{7,5},{1,7},{10,8},{12,10},{14... | collective-permute-start | bytes 786440 | tf_op jit(solution)/shard_map/ppermute | solution.py:26
  59.7 8.2 %collective-permute-start.8 = (bf16[4,128,256]{2,1,0:T(8,128)(2,1)}, bf16[4,128,256]{2,1,0:T(8,128)(2,1)}, u32[]{:S(2)}, u32[]{:S(2)}) collective-permute-start(bf16[4,128,256]{2,1,0:T(8,128)(2,1)} %slice.48), channel_id=1, source_target_pairs={{6,0},{0,2},{2,4},{4,6},{7,1},{1,3},{3,5},{5,7},{14,8},{8,10},{10,... | collective-permute-start | bytes 786440 | tf_op jit(solution)/shard_map/ppermute | solution.py:26
  93.0 9.4 %collective-permute-start.21 = (bf16[512,4096]{0,1:T(8,128)(2,1)}, bf16[512,4096]{0,1:T(8,128)(2,1)}, u32[]{:S(2)}, u32[]{:S(2)}) collective-permute-start(bf16[512,4096]{0,1:T(8,128)(2,1)} %copy.8), channel_id=1, source_target_pairs={{32,0},{0,32},{33,1},{1,33},{34,2},{2,34},{35,3},{3,35},{36,4},{4,... | collective-permute-start | bytes 12582920 | tf_op jit(solution)/shard_map/ppermute | solution.py:26
  100.4 58.7 %collective-permute-start.22 = (bf16[512,2048]{1,0:T(8,128)(2,1)}, bf16[512,2048]{1,0:T(8,128)(2,1)}, u32[]{:S(2)}, u32[]{:S(2)}) collective-permute-start(bf16[512,2048]{1,0:T(8,128)(2,1)} %get-tuple-element.47), channel_id=1, source_target_pairs={{1,0},{0,1},{3,2},{2,3},{5,4},{4,5},{7,6},{6,7},{9,8},{8,9},{11,10... | collective-permute-start | bytes 6291464 | tf_op jit(solution)/shard_map/ppermute | solution.py:26
  100.4 58.7 %collective-permute-start.20 = (bf16[512,512]{1,0:T(8,128)(2,1)S(1)}, bf16[512,512]{1,0:T(8,128)(2,1)S(1)}, u32[]{:S(2)}, u32[]{:S(2)}) collective-permute-start(bf16[512,512]{1,0:T(8,128)(2,1)S(1)} %copy-done.32), channel_id=1, source_target_pairs={{1,0},{0,1},{3,2},{2,3},{5,4},{4,5},{7,6},{6,7},{9,8},{8,9},{11,10... | collective-permute-start | bytes 1572872 | tf_op jit(solution)/shard_map/ppermute | solution.py:26
  164.4 31.7 %copy-start.30 = (f32[512,128]{1,0:T(8,128)S(1)}, f32[512,128]{1,0:T(8,128)}, u32[]{:S(2)}) copy-start(f32[512,128]{1,0:T(8,128)} %curvature.3) | copy-start | bytes 786436
  164.4 31.7 %all-to-all-start = ((bf16[16,512,128]{2,1,0:T(8,128)(2,1)}), bf16[16,512,128]{2,1,0:T(8,128)(2,1)}, u32[]{:S(2)}, u32[]{:S(2)}) async-start(bf16[16,512,128]{2,1,0:T(8,128)(2,1)} %copy-done.14), calls=%async_computation | async-start | bytes 4194304 | tf_op jit(solution)/shard_map/all_to_all | solution.py:328
  171.3 70.7 %collective-permute-start.29 = (bf16[128,4096]{1,0:T(8,128)(2,1)}, bf16[128,4096]{1,0:T(8,128)(2,1)}, u32[]{:S(2)}, u32[]{:S(2)}) collective-permute-start(bf16[128,4096]{1,0:T(8,128)(2,1)} %constant_dynamic-slice_fusion.4), channel_id=1, source_target_pairs={{64,0},{0,64},{65,1},{1,65},{66,2},{2,66},{67,3},{3,67},{68,4},{4,... | collective-permute-start | bytes 3145736 | tf_op jit(solution)/shard_map/ppermute | solution.py:26
  198.0 43.0 %copy-start.33 = (f32[512,128]{1,0:T(8,128)}, f32[512,128]{1,0:T(8,128)S(1)}, u32[]{:S(2)}) copy-start(f32[512,128]{1,0:T(8,128)S(1)} %get-tuple-element.59.moved) | copy-start | bytes 786436
  198.0 3.9 collective-permute-start.23
  199.1 5.4 %collective-permute-start.24 = (bf16[512,128]{1,0:T(8,128)(2,1)S(1)}, bf16[512,128]{1,0:T(8,128)(2,1)S(1)}, u32[]{:S(2)}, u32[]{:S(2)}) collective-permute-start(bf16[512,128]{1,0:T(8,128)(2,1)S(1)} %get-tuple-element.48), channel_id=1, source_target_pairs={{16,0},{24,8},{0,16},{8,24},{17,1},{25,9},{1,17},{9,25},{18,2},{26... | collective-permute-start | bytes 393224 | tf_op jit(solution)/shard_map/ppermute | solution.py:26
  199.2 6.4 %collective-permute-start.25 = (bf16[512,128]{1,0:T(8,128)(2,1)S(1)}, bf16[512,128]{1,0:T(8,128)(2,1)S(1)}, u32[]{:S(2)}, u32[]{:S(2)}) collective-permute-start(bf16[512,128]{1,0:T(8,128)(2,1)S(1)} %get-tuple-element.48), channel_id=1, source_target_pairs={{24,0},{0,8},{8,16},{16,24},{25,1},{1,9},{9,17},{17,25},{26,2},{2,... | collective-permute-start | bytes 393224 | tf_op jit(solution)/shard_map/ppermute | solution.py:26
  205.8 27.2 %collective-permute-start.26 = (bf16[4,512,128]{2,1,0:T(8,128)(2,1)S(1)}, bf16[4,512,128]{2,1,0:T(8,128)(2,1)S(1)}, u32[]{:S(2)}, u32[]{:S(2)}) collective-permute-start(bf16[4,512,128]{2,1,0:T(8,128)(2,1)S(1)} %pad_maximum_fusion.6.p0), channel_id=1, source_target_pairs={{2,0},{4,2},{6,4},{0,6},{3,1},{5,3},{7,5},{1,7},{10,8},{12,10},{14... | collective-permute-start | bytes 1572872 | tf_op jit(solution)/shard_map/ppermute | solution.py:26
  211.6 21.3 %collective-permute-start.27 = (bf16[4,512,128]{2,1,0:T(8,128)(2,1)S(1)}, bf16[4,512,128]{2,1,0:T(8,128)(2,1)S(1)}, u32[]{:S(2)}, u32[]{:S(2)}) collective-permute-start(bf16[4,512,128]{2,1,0:T(8,128)(2,1)S(1)} %pad_maximum_fusion.6.p0), channel_id=1, source_target_pairs={{4,0},{6,2},{0,4},{2,6},{5,1},{7,3},{1,5},{3,7},{12,8},{14,10},{8,... | collective-permute-start | bytes 1572872 | tf_op jit(solution)/shard_map/ppermute | solution.py:26
  211.6 25.9 %collective-permute-start.28 = (bf16[4,512,128]{2,1,0:T(8,128)(2,1)S(1)}, bf16[4,512,128]{2,1,0:T(8,128)(2,1)S(1)}, u32[]{:S(2)}, u32[]{:S(2)}) collective-permute-start(bf16[4,512,128]{2,1,0:T(8,128)(2,1)S(1)} %pad_maximum_fusion.6.p0), channel_id=1, source_target_pairs={{6,0},{0,2},{2,4},{4,6},{7,1},{1,3},{3,5},{5,7},{14,8},{8,10},{10,... | collective-permute-start | bytes 1572872 | tf_op jit(solution)/shard_map/ppermute | solution.py:26
  241.0 12.7 %collective-permute-start.34 = (bf16[512,512]{1,0:T(8,128)(2,1)S(1)}, bf16[512,512]{1,0:T(8,128)(2,1)S(1)}, u32[]{:S(2)}, u32[]{:S(2)}) collective-permute-start(bf16[512,512]{1,0:T(8,128)(2,1)S(1)} %get-tuple-element.54), channel_id=1, source_target_pairs={{1,0},{0,1},{3,2},{2,3},{5,4},{4,5},{7,6},{6,7},{9,8},{8,9},{11,10... | collective-permute-start | bytes 1572872 | tf_op jit(solution)/shard_map/ppermute | solution.py:26
  242.0 28.6 %collective-permute-start.30 = (bf16[128,4096]{1,0:T(8,128)(2,1)}, bf16[128,4096]{1,0:T(8,128)(2,1)S(1)}, u32[]{:S(2)}, u32[]{:S(2)}) collective-permute-start(bf16[128,4096]{1,0:T(8,128)(2,1)} %collective-permute-done.29), channel_id=1, source_target_pairs={{32,0},{0,32},{33,1},{1,33},{34,2},{2,34},{35,3},{3,35},{36,4},{4,... | collective-permute-start | bytes 3145736 | tf_op jit(solution)/shard_map/ppermute | solution.py:26
  243.3 10.4 %copy-start.7 = (f32[512,512]{1,0:T(8,128)S(1)}, f32[512,512]{1,0:T(8,128)}, u32[]{:S(2)}) copy-start(f32[512,512]{1,0:T(8,128)} %copy-done.6) | copy-start | bytes 3145732
  243.3 10.4 %copy-start.18 = (f32[512,512]{1,0:T(8,128)S(1)}, f32[512,512]{1,0:T(8,128)}, u32[]{:S(2)}) copy-start(f32[512,512]{1,0:T(8,128)} %copy-done.17) | copy-start | bytes 3145732
  254.3 17.7 %copy-start.2 = (bf16[512,4096]{1,0:T(8,128)(2,1)S(1)}, bf16[512,4096]{1,0:T(8,128)(2,1)}, u32[]{:S(2)}) copy-start(bf16[512,4096]{1,0:T(8,128)(2,1)} %copy-done) | copy-start | bytes 12582916
  254.3 13.6 %collective-permute-start.36 = (bf16[528,512]{1,0:T(8,128)(2,1)S(1)}, bf16[528,512]{1,0:T(8,128)(2,1)S(1)}, u32[]{:S(2)}, u32[]{:S(2)}) collective-permute-start(bf16[528,512]{1,0:T(8,128)(2,1)S(1)} %delta.2.d0.delta_one), channel_id=1, source_target_pairs={{64,0},{0,64},{65,1},{1,65},{66,2},{2,66},{67,3},{3,67},{68,4},{4,... | collective-permute-start | bytes 1622024 | tf_op jit(solution)/shard_map/ppermute | solution.py:26
  255.0 46.6 %collective-permute-start.35 = (bf16[528,512]{1,0:T(8,128)(2,1)S(1)}, bf16[528,512]{1,0:T(8,128)(2,1)S(1)}, u32[]{:S(2)}, u32[]{:S(2)}) collective-permute-start(bf16[528,512]{1,0:T(8,128)(2,1)S(1)} %delta.2.d0.delta_one), channel_id=1, source_target_pairs={{32,0},{0,32},{33,1},{1,33},{34,2},{2,34},{35,3},{3,35},{36,4},{4,... | collective-permute-start | bytes 1622024 | tf_op jit(solution)/shard_map/ppermute | solution.py:26
  267.9 34.9 %copy-start.20 = (bf16[528,512]{1,0:T(8,128)(2,1)}, bf16[528,512]{1,0:T(8,128)(2,1)S(1)}, u32[]{:S(2)}) copy-start(bf16[528,512]{1,0:T(8,128)(2,1)S(1)} %collective-permute-done.36.d2) | copy-start | bytes 1622020
  267.9 34.9 %collective-permute-start.37 = (bf16[528,512]{1,0:T(8,128)(2,1)S(1)}, bf16[528,512]{1,0:T(8,128)(2,1)S(1)}, u32[]{:S(2)}, u32[]{:S(2)}) collective-permute-start(bf16[528,512]{1,0:T(8,128)(2,1)S(1)} %collective-permute-done.36.d2), channel_id=1, source_target_pairs={{32,0},{0,32},{33,1},{1,33},{34,2},{2,34},{35,3},{3,35},{36,4},{4,... | collective-permute-start | bytes 1622024 | tf_op jit(solution)/shard_map/ppermute | solution.py:26
  272.0 28.1 %copy-start.13 = (f32[512,1024]{1,0:T(8,128)S(1)}, f32[512,1024]{1,0:T(8,128)}, u32[]{:S(2)}) copy-start(f32[512,1024]{1,0:T(8,128)} %copy-done.12) | copy-start | bytes 6291460
  273.3 13.4 %collective-permute-start.31 = (f32[512,256]{1,0:T(8,128)S(1)}, f32[512,256]{1,0:T(8,128)S(1)}, u32[]{:S(2)}, u32[]{:S(2)}) collective-permute-start(f32[512,256]{1,0:T(8,128)S(1)} %far_gram.1.p0), channel_id=1, source_target_pairs={{8,0},{16,8},{24,16},{0,24},{9,1},{17,9},{25,17},{1,25},{10,2},{18... | collective-permute-start | bytes 1572872 | tf_op jit(solution)/shard_map/ppermute | solution.py:26
  273.4 15.0 %collective-permute-start.32 = (f32[512,256]{1,0:T(8,128)S(1)}, f32[512,256]{1,0:T(8,128)S(1)}, u32[]{:S(2)}, u32[]{:S(2)}) collective-permute-start(f32[512,256]{1,0:T(8,128)S(1)} %far_gram.1.p0), channel_id=1, source_target_pairs={{16,0},{24,8},{0,16},{8,24},{17,1},{25,9},{1,17},{9,25},{18,2},{26... | collective-permute-start | bytes 1572872 | tf_op jit(solution)/shard_map/ppermute | solution.py:26
  274.5 25.5 %collective-permute-start.33 = (f32[512,256]{1,0:T(8,128)S(1)}, f32[512,256]{1,0:T(8,128)S(1)}, u32[]{:S(2)}, u32[]{:S(2)}) collective-permute-start(f32[512,256]{1,0:T(8,128)S(1)} %far_gram.1.p0), channel_id=1, source_target_pairs={{24,0},{0,8},{8,16},{16,24},{25,1},{1,9},{9,17},{17,25},{26,2},{2,... | collective-permute-start | bytes 1572872 | tf_op jit(solution)/shard_map/ppermute | solution.py:26
  305.1 13.4 %collective-permute-start.38 = (bf16[528,512]{1,0:T(8,128)(2,1)S(1)}, bf16[528,512]{1,0:T(8,128)(2,1)S(1)}, u32[]{:S(2)}, u32[]{:S(2)}) collective-permute-start(bf16[528,512]{1,0:T(8,128)(2,1)S(1)} %get-tuple-element.58.own), channel_id=1, source_target_pairs={{1,0},{0,1},{3,2},{2,3},{5,4},{4,5},{7,6},{6,7},{9,8},{8,9},{11,10... | collective-permute-start | bytes 1622024 | tf_op jit(solution)/shard_map/ppermute | solution.py:26
  323.8 31.1 %all-to-all-start.1 = ((bf16[16,528,128]{2,1,0:T(8,128)(2,1)}), bf16[16,528,128]{2,1,0:T(8,128)(2,1)}, u32[]{:S(2)}, u32[]{:S(2)}) async-start(bf16[16,528,128]{2,1,0:T(8,128)(2,1)} %copy-done.9), calls=%async_computation.1 | async-start | bytes 4325376 | tf_op jit(solution)/shard_map/all_to_all | solution.py:353
  331.4 71.6 %collective-permute-start.47 = (bf16[512,2048]{0,1:T(8,128)(2,1)}, bf16[512,2048]{0,1:T(8,128)(2,1)}, u32[]{:S(2)}, u32[]{:S(2)}) collective-permute-start(bf16[512,2048]{0,1:T(8,128)(2,1)} %constant_dynamic-slice_fusion.2), channel_id=1, source_target_pairs={{64,0},{0,64},{65,1},{1,65},{66,2},{2,66},{67,3},{3,67},{68,4},{4,... | collective-permute-start | bytes 6291464 | tf_op jit(solution)/shard_map/ppermute | solution.py:26
  357.8 5.3 %collective-permute-start.39 = (bf16[512,128]{1,0:T(8,128)(2,1)S(1)}, bf16[512,128]{1,0:T(8,128)(2,1)S(1)}, u32[]{:S(2)}, u32[]{:S(2)}) collective-permute-start(bf16[512,128]{1,0:T(8,128)(2,1)S(1)} %get-tuple-element.60), channel_id=1, source_target_pairs={{8,0},{16,8},{24,16},{0,24},{9,1},{17,9},{25,17},{1,25},{10,2},{18... | collective-permute-start | bytes 393224 | tf_op jit(solution)/shard_map/ppermute | solution.py:26
  359.8 5.8 %collective-permute-start.40 = (bf16[512,128]{1,0:T(8,128)(2,1)S(1)}, bf16[512,128]{1,0:T(8,128)(2,1)S(1)}, u32[]{:S(2)}, u32[]{:S(2)}) collective-permute-start(bf16[512,128]{1,0:T(8,128)(2,1)S(1)} %get-tuple-element.60), channel_id=1, source_target_pairs={{16,0},{24,8},{0,16},{8,24},{17,1},{25,9},{1,17},{9,25},{18,2},{26... | collective-permute-start | bytes 393224 | tf_op jit(solution)/shard_map/ppermute | solution.py:26
  359.9 6.8 %collective-permute-start.41 = (bf16[512,128]{1,0:T(8,128)(2,1)S(1)}, bf16[512,128]{1,0:T(8,128)(2,1)S(1)}, u32[]{:S(2)}, u32[]{:S(2)}) collective-permute-start(bf16[512,128]{1,0:T(8,128)(2,1)S(1)} %get-tuple-element.60), channel_id=1, source_target_pairs={{24,0},{0,8},{8,16},{16,24},{25,1},{1,9},{9,17},{17,25},{26,2},{2,... | collective-permute-start | bytes 393224 | tf_op jit(solution)/shard_map/ppermute | solution.py:26
  366.8 17.5 %collective-permute-start.42 = (bf16[4,512,128]{2,1,0:T(8,128)(2,1)S(1)}, bf16[4,512,128]{2,1,0:T(8,128)(2,1)S(1)}, u32[]{:S(2)}, u32[]{:S(2)}) collective-permute-start(bf16[4,512,128]{2,1,0:T(8,128)(2,1)S(1)} %pad_maximum_fusion.7.p0), channel_id=1, source_target_pairs={{2,0},{4,2},{6,4},{0,6},{3,1},{5,3},{7,5},{1,7},{10,8},{12,10},{14... | collective-permute-start | bytes 1572872 | tf_op jit(solution)/shard_map/ppermute | solution.py:26
  370.1 14.2 %collective-permute-start.43 = (bf16[4,512,128]{2,1,0:T(8,128)(2,1)S(1)}, bf16[4,512,128]{2,1,0:T(8,128)(2,1)S(1)}, u32[]{:S(2)}, u32[]{:S(2)}) collective-permute-start(bf16[4,512,128]{2,1,0:T(8,128)(2,1)S(1)} %pad_maximum_fusion.7.p0), channel_id=1, source_target_pairs={{4,0},{6,2},{0,4},{2,6},{5,1},{7,3},{1,5},{3,7},{12,8},{14,10},{8,... | collective-permute-start | bytes 1572872 | tf_op jit(solution)/shard_map/ppermute | solution.py:26
  370.8 25.8 %collective-permute-start.44 = (bf16[4,512,128]{2,1,0:T(8,128)(2,1)S(1)}, bf16[4,512,128]{2,1,0:T(8,128)(2,1)S(1)}, u32[]{:S(2)}, u32[]{:S(2)}) collective-permute-start(bf16[4,512,128]{2,1,0:T(8,128)(2,1)S(1)} %pad_maximum_fusion.7.p0), channel_id=1, source_target_pairs={{6,0},{0,2},{2,4},{4,6},{7,1},{1,3},{3,5},{5,7},{14,8},{8,10},{10,... | collective-permute-start | bytes 1572872 | tf_op jit(solution)/shard_map/ppermute | solution.py:26
  402.2 13.3 %collective-permute-start.45 = (bf16[512,512]{1,0:T(8,128)(2,1)}, bf16[512,512]{1,0:T(8,128)(2,1)}, u32[]{:S(2)}, u32[]{:S(2)}) collective-permute-start(bf16[512,512]{1,0:T(8,128)(2,1)} %get-tuple-element.64), channel_id=1, source_target_pairs={{1,0},{0,1},{3,2},{2,3},{5,4},{4,5},{7,6},{6,7},{9,8},{8,9},{11,10... | collective-permute-start | bytes 1572872 | tf_op jit(solution)/shard_map/ppermute | solution.py:26
  406.2 30.6 %collective-permute-start.48 = (bf16[512,1024]{0,1:T(8,128)(2,1)}, bf16[512,1024]{0,1:T(8,128)(2,1)}, u32[]{:S(2)}, u32[]{:S(2)}) collective-permute-start(bf16[512,1024]{0,1:T(8,128)(2,1)} %get-tuple-element.76), channel_id=1, source_target_pairs={{32,0},{0,32},{33,1},{1,33},{34,2},{2,34},{35,3},{3,35},{36,4},{4,... | collective-permute-start | bytes 3145736 | tf_op jit(solution)/shard_map/ppermute | solution.py:26
  407.0 8.6 %copy-start.8 = (f32[512,512]{1,0:T(8,128)S(1)}, f32[512,512]{1,0:T(8,128)}, u32[]{:S(2)}) copy-start(f32[512,512]{1,0:T(8,128)} %copy-done.6) | copy-start | bytes 3145732
  407.0 8.6 %copy-start.19 = (f32[512,512]{1,0:T(8,128)S(1)}, f32[512,512]{1,0:T(8,128)}, u32[]{:S(2)}) copy-start(f32[512,512]{1,0:T(8,128)} %copy-done.17) | copy-start | bytes 3145732
  407.0 8.6 %copy-start.29 = (f32[512,512]{1,0:T(8,128)S(1)}, f32[512,512]{1,0:T(8,128)}, u32[]{:S(2)}) copy-start(f32[512,512]{1,0:T(8,128)} %copy-done.28) | copy-start | bytes 3145732
  418.0 13.9 %collective-permute-start.49 = (bf16[512,512]{1,0:T(8,128)(2,1)}, bf16[512,512]{1,0:T(8,128)(2,1)}, u32[]{:S(2)}, u32[]{:S(2)}) collective-permute-start(bf16[512,512]{1,0:T(8,128)(2,1)} %get-tuple-element.66.d0), channel_id=1, source_target_pairs={{64,0},{0,64},{65,1},{1,65},{66,2},{2,66},{67,3},{3,67},{68,4},{4,... | collective-permute-start | bytes 1572872 | tf_op jit(solution)/shard_map/ppermute | solution.py:26
  418.5 18.3 %collective-permute-start.46 = (bf16[512,512]{1,0:T(8,128)(2,1)}, bf16[512,512]{1,0:T(8,128)(2,1)}, u32[]{:S(2)}, u32[]{:S(2)}) collective-permute-start(bf16[512,512]{1,0:T(8,128)(2,1)} %get-tuple-element.66.d0), channel_id=1, source_target_pairs={{32,0},{0,32},{33,1},{1,33},{34,2},{2,34},{35,3},{3,35},{36,4},{4,... | collective-permute-start | bytes 1572872 | tf_op jit(solution)/shard_map/ppermute | solution.py:26
  431.9 7.4 %collective-permute-start.50 = (bf16[512,512]{1,0:T(8,128)(2,1)}, bf16[512,512]{1,0:T(8,128)(2,1)}, u32[]{:S(2)}, u32[]{:S(2)}) collective-permute-start(bf16[512,512]{1,0:T(8,128)(2,1)} %collective-permute-done.49.d2), channel_id=1, source_target_pairs={{32,0},{0,32},{33,1},{1,33},{34,2},{2,34},{35,3},{3,35},{36,4},{4,... | collective-permute-start | bytes 1572872 | tf_op jit(solution)/shard_map/ppermute | solution.py:26
  444.7 17.8 %all-to-all-start.2 = ((f32[128,8,128]{2,1,0:T(8,128)}), f32[128,8,128]{2,1,0:T(8,128)}, u32[]{:S(2)}, u32[]{:S(2)}) async-start(f32[128,8,128]{2,1,0:T(8,128)} %broadcast_in_dim.2), calls=%async_computation.2 | async-start | bytes 1048576 | tf_op jit(solution)/shard_map/all_to_all | solution.py:375
  (27 other events, 47.7 us)

commit v3 on v2

--- a/solution.py
+++ b/solution.py
@@ -26,18 +26,7 @@
     return lax.ppermute(value, axis, [((i + by) % n, i) for i in range(n)])
 
 
-def ring_pair(jobs):
-    up = [shift(v, a, 1) for v, a in jobs]
-    down = [shift(v, a, -1) for v, a in jobs]
-    out = []
-    for (v, a), p, m in zip(jobs, up, down):
-        h = v.shape[-2] // 2
-        far = [shift(p[..., :h, :], a, 1), shift(m[..., h:, :], a, -1)]
-        out.append([v, p, jnp.concatenate(far, axis=-2), m])
-    return out
-
-
-def ring_direct(v, a):
+def line(v, a):
     return [v, shift(v, a, 1), shift(v, a, 2), shift(v, a, 3)]
 
 
@@ -59,6 +48,21 @@
     return got if len(got) > 1 else got[0]
 
 
+def gather(v):
+    here, far = lax.optimization_barrier((line(v, "x"), shift(v, "z", 2)))
+    here = jnp.stack(here)
+    return [here, shift(here, "z", 1), *line(far, "x"), shift(here, "z", 3)]
+
+
+def blocks(pos, refs, width):
+    here, nxt, f0, f1, f2, f3, prev = refs
+    for i, f in enumerate((f0, f1, f2, f3)):
+        yield place(pos, i, 0, width), here[i]
+        yield place(pos, i, 1, width), nxt[i]
+        yield place(pos, i, 2, width), f[...]
+        yield place(pos, i, 3, width), prev[i]
+
+
 def nt(a, b):
     return lax.dot_general(a, b, (((1,), (1,)), ((), ())), preferred_element_type=F32)
 
@@ -114,15 +118,11 @@
 
 
 def front_kernel(pos, *refs):
-    a, b = refs[:4], refs[4:8]
-    gate_w, up_w = refs[8:10]
-    rows = refs[10:14]
-    feats, slope, tangent, pushed = refs[14:]
-    h = feats.shape[0] // 2
-    for i in range(4):
-        for j in range(4):
-            feats[:h, pl.ds(place(pos, j, i, 256), 256)] = a[i][j]
-            feats[h:, pl.ds(place(pos, i, j, 256), 256)] = b[i][j]
+    gate_w, up_w = refs[7:9]
+    rows = refs[9:13]
+    feats, slope, tangent, pushed = refs[13:]
+    for col, block in blocks(pos, refs[:7], 256):
+        feats[:, pl.ds(col, 256)] = block
     gate = nn(feats[...], gate_w[...])
     sigma = 1.0 / (1.0 + jnp.exp(-gate))
     slope[...] = sigma * (1.0 + gate * (1.0 - sigma)) * nn(feats[...], up_w[...])
@@ -168,10 +168,10 @@
     scalars[...] = row_of([ss, sw, scale], 8, 128)
 
 
-def back_kernel(pos, p0, p1, p2, p3, recv, full, send):
-    for i, p in enumerate((p0, p1, p2, p3)):
-        for j in range(4):
-            full[:, pl.ds(place(pos, j, i, 128), 128)] = p[j]
+def back_kernel(pos, *refs):
+    recv, full, send = refs[7:]
+    for col, block in blocks(pos, refs[:7], 128):
+        full[:, pl.ds(col, 128)] = block
     send[...] = nt(full[...], recv[...]).astype(BF)
 
 
@@ -195,8 +195,20 @@
     sums[...] = row_of([ww, total(tan_start[...] * delta), total(tan_image[...] * delta)], 8, 128)
 
 
-def gram_kernel(feats, others, out):
-    out[...] = nt(feats[...], others[...])
+def gram_kernel(feats, one, two, out):
+    n = one.shape[0]
+    out[:, :n] = nt(feats[...], one[...])
+    out[:, n:] = nt(feats[...], two[...])
+
+
+def rows_kernel(pos, feats, out):
+    out[...] = feats[:, pl.ds(pl.multiple_of(pos[3] * 1024, 1024), 1024)].T
+
+
+def far_rows_kernel(pos, feats, out, other):
+    c = pos[8]
+    out[...] = feats[:, pl.ds(pl.multiple_of(c * 1024, 1024), 1024)].T
+    other[...] = feats[:, pl.ds(pl.multiple_of((1 - c) * 1024, 1024), 1024)].T
 
 
 def gram_split_kernel(pos, near, p0, p1, p2, p3, high, low):
@@ -279,14 +291,6 @@
         out[:, cols] = f_two * image_two[:, cols] + f_one * image_one[:, cols] + f_start * start[:, cols]
 
 
-def pull_back(weighted, pos, keep, recv):
-    pieces = ring_direct(jnp.stack(ring_direct(weighted, "x")), "z")
-    full, send = call(back_kernel, "back_other", [((512, 2048), BF), ((512, 512), BF)], pos, *pieces, recv)
-    got = shift(send, "yl", 1)
-    own = call(own_back_kernel, "back_own", [((512, 512), F32)], full, keep)
-    return own, got, full
-
-
 def over_dp(v):
     far = shift(v, "yh", 1)
     return [v, shift(v, "c", 1), far, shift(far, "c", 1)]
@@ -295,49 +299,49 @@
 def shards(tokens, gate_weight, up_weight, down_weight, curvature, start):
     yh, c, x, z, yl = [lax.axis_index(n).astype(jnp.int32) for n in NAMES]
     dp = yh * 2 + c
-    pos = jnp.stack([x, z, yl, dp, dp, yh * 2 + 1 - c, (1 - yh) * 2 + c, (1 - yh) * 2 + 1 - c])
+    pos = jnp.stack([x, z, yl, dp, dp, yh * 2 + 1 - c, (1 - yh) * 2 + c, (1 - yh) * 2 + 1 - c, c])
 
     other = shift(tokens, "yl", 1)
     start_b, squares = call(cast_kernel, "cast_start", [((1024, 512), BF), ((8, 512), F32)], start)
+    keep, send = call(
+        split_kernel, "split_down", [((512, 2048), BF)] * 2, pos, after(down_weight, squares)
+    )
     pair = jnp.where(
         yl == 0, jnp.concatenate([tokens, other], axis=1), jnp.concatenate([other, tokens], axis=1)
     )
-    keep, send = call(split_kernel, "split_down", [((512, 2048), BF)] * 2, pos, down_weight)
-    a, b = ring_pair([(pair[:256], "x"), (pair[256:], "z")])
+    start_b, send = lax.optimization_barrier((start_b, send))
     starts = over_dp(start_b)
-    recv = shift(after(send, starts[2]), "yl", 1)
-    a, b = ring_pair([(jnp.stack(a), "z"), (jnp.stack(b), "x")])
+    recv = shift(send, "yl", 1)
     feats, slope, tan_start, pushed = call(
         front_kernel,
         "front",
         [((512, D), BF), ((512, 512), F32), ((512, 512), F32), ((512, 512), BF)],
-        pos, *a, *b, gate_weight, up_weight, *starts,
+        pos, *gather(pair), gate_weight, up_weight, *starts,
         mib=32,
     )
 
     other = shift(pushed, "yl", 1)
     feats_c = shift(feats, "c", 1)
-    near_gram = call(
-        gram_kernel, "near_gram", [((512, 1024), F32)], after(feats, pushed), jnp.concatenate([feats, feats_c])
-    )
+    near_gram = call(gram_kernel, "near_gram", [((512, 1024), F32)], feats, feats, feats_c)
     other, near_gram = lax.optimization_barrier((other, near_gram))
     parts = call(push_kernel, "push", [((16, 512, 128), BF)], pushed, other, keep, recv)
     quarter = lax.dynamic_slice_in_dim(feats, x * 128, 128, axis=0)
-    quarter = shift(after(quarter, other), "yh", 1)
+    quarter = shift(after(quarter, parts), "yh", 1)
     quarter_c = shift(quarter, "c", 1)
     got = lax.all_to_all(parts, ("x", "z"), 0, 0, tiled=True)
+    rows = [call(rows_kernel, "rows", [((1024, 512), BF)], pos, after(f, parts)) for f in (feats, feats_c)]
+    got, rows = lax.optimization_barrier((got, rows))
     moved, weighted = call(weigh_first_kernel, "weigh", [((512, 128), F32), ((512, 128), BF)], got, curvature)
-    own, got, full = pull_back(weighted, pos, keep, recv)
-    far_gram = call(
-        gram_kernel, "far_gram", [((512, 256), F32)], after(feats, own), jnp.concatenate([quarter, quarter_c])
-    )
-    delta = call(
-        delta_first_kernel, "delta", [((528, 512), BF)], own, got, slope, tan_start, squares
-    )
+    pieces = gather(weighted)
+    far_gram = call(gram_kernel, "far_gram", [((512, 256), F32)], after(feats, pieces[0]), quarter, quarter_c)
+    recv_one, far_gram = lax.optimization_barrier((recv, far_gram))
+    full, send = call(back_kernel, "back_other", [((512, 2048), BF), ((512, 512), BF)], pos, *pieces, recv_one)
+    got = shift(send, "yl", 1)
+    own = call(own_back_kernel, "back_own", [((512, 512), F32)], full, keep)
+    far_grams = line(after(far_gram, send), "x")
+    delta = call(delta_first_kernel, "delta", [((528, 512), BF)], own, got, slope, tan_start, squares)
     deltas = over_dp(delta)
-    high, low = call(
-        gram_split_kernel, "gram_split", [((512, 2048), BF)] * 2, pos, near_gram, *ring_direct(far_gram, "x")
-    )
+    high, low = call(gram_split_kernel, "gram_split", [((512, 2048), BF)] * 2, pos, near_gram, *far_grams)
     near = call(near_tangent_kernel, "near_tangent", [((512, 512), F32)], high, low, *deltas[:2])
     tan_image, pushed = call(
         far_tangent_kernel,
@@ -349,18 +353,24 @@
     other = shift(pushed, "yl", 1)
     parts = call(push_kernel, "push", [((16, 528, 128), BF)], pushed, other, keep, recv)
     theirs = lax.dynamic_slice_in_dim(feats, (1 - yh) * 2048, 2048, axis=1)
-    far_rows = shift(after(theirs, other), "yh", 1)
+    far_rows = shift(after(theirs, parts), "yh", 1)
     got = lax.all_to_all(parts, ("x", "z"), 0, 0, tiled=True)
+    first_deltas = deltas
+    near_one = call(
+        near_image_kernel, "near_image", [((1024, 512), F32)], *rows, after(first_deltas[0], parts), first_deltas[1]
+    )
+    got, near_one = lax.optimization_barrier((got, near_one))
     weighted, scalars = call(
         weigh_second_kernel, "weigh", [((512, 128), BF), ((8, 128), F32)], got, curvature, moved
     )
-    own, got, full = pull_back(weighted, pos, keep, recv)
-    mine = lambda v, at: lax.dynamic_slice_in_dim(v, at * 1024, 1024, axis=1)
-    rows = [mine(feats, dp), mine(feats_c, dp), mine(far_rows, c), shift(mine(far_rows, 1 - c), "c", 1)]
-    rows = [after(r, own).T for r in rows]
-    first_deltas = deltas
-    near = call(near_image_kernel, "near_image", [((1024, 512), F32)], *rows[:2], *first_deltas[:2])
-    image_one = call(far_image_kernel, "far_image", [((1024, 512), F32)], near, *rows[2:], *first_deltas[2:])
+    full, send = call(
+        back_kernel, "back_other", [((512, 2048), BF), ((512, 512), BF)], pos, *gather(weighted), recv
+    )
+    got = shift(send, "yl", 1)
+    own = call(own_back_kernel, "back_own", [((512, 512), F32)], full, keep)
+    mine, theirs = call(far_rows_kernel, "far_rows", [((1024, 512), BF)] * 2, pos, after(far_rows, send))
+    got, mine, theirs = lax.optimization_barrier((got, mine, theirs))
+    rows += [mine, shift(theirs, "c", 1)]
     delta, sums = call(
         delta_second_kernel,
         "delta",
@@ -368,7 +378,11 @@
         own, got, slope, tan_start, tan_image, delta,
     )
     deltas = over_dp(delta)
+    image_one = call(
+        far_image_kernel, "far_image", [((1024, 512), F32)], after(near_one, delta), *rows[2:], *first_deltas[2:]
+    )
     near = call(near_image_kernel, "near_image", [((1024, 512), F32)], *rows[:2], *deltas[:2])
+    near, image_one = lax.optimization_barrier((near, image_one))
     image_two, block = call(
         last_image_kernel, "last_image", [((1024, 512), F32), ((8, 128), F32)], near, *rows[2:], *deltas[2:], sums
     )

time: 478 us -> 441 us (0.923)
  local copies, waits for them, and re-layouts: 61.5 us -> 27.7 us
  blocking collectives: 0 us -> 20.8 us
  other arithmetic: 11.9 us -> 1.44 us
  Pallas kernels: 62.7 us -> 52.9 us
    ppermute x51 -> x50, waiting for transfers between devices: 190 us -> 225 us  [shift(): return lax.ppermute(value, axis, [((i + by) % n, i) for i in range(n)])]
    all_to_all x2, waiting for transfers between devices: 47.1 us -> 19.2 us  [shards(): got = lax.all_to_all(parts, ('x', 'z'), 0, 0, tiled=True)]
    all_to_all x0 -> x1, blocking collectives: none -> 20.8 us  [shards(): lax.all_to_all(jnp.broadcast_to(block[None], (128, 8, 128)), NAMES, 0, 0,...]
    concatenate x1 -> x0, local copies, waits for them, and re-layouts: 11.8 us -> none  [shards(): jnp.concatenate([feats, feats_c])]
    concatenate x4 -> x0, other arithmetic: 11.5 us -> none  [the longest x1 7.95 us: shards(): jnp.concatenate([feats, feats_c])]
    all_to_all x1 -> x0, waiting for transfers between devices: 9.17 us -> none  [shards(): lax.all_to_all(jnp.broadcast_to(block[None], (128, 8, 128)), NAMES, 0, 0,...]
    pallas_call x22 -> x25, Pallas kernels: 59 us -> 50.3 us  [call(): pl.pallas_call(kernel, out_shape=shapes, in_specs=specs, out_specs=[VM] *...]
    unnamed x74 -> x84, local copies, waits for them, and re-layouts: 29.1 us -> 22.4 us
  transfers between devices with their start and end apart: 54 -> 52, of which waited for: 32 -> 30; matrix products, arithmetic and copies ran while one was open for 8% -> 1% of each run, Pallas kernels for 8% -> 7%
where the time goes in v3:
time: 441 us; the launch traced here: 432 us
  waiting for transfers between devices  244 us (55%)
  starting transfers between devices  84.1 us (19%)
  Pallas kernels  52.9 us (12%)
  local copies, waits for them, and re-layouts  27.7 us (6%)
  blocking collectives  20.8 us (5%)
    ppermute x50, waiting for transfers between devices, shift(): return lax.ppermute(value, axis, [((i + by) % n, i) for i in range(n)])  225 us
    ppermute x50, starting transfers between devices, shift(): return lax.ppermute(value, axis, [((i + by) % n, i) for i in range(n)])  75.1 us
    pallas_call x25, Pallas kernels, call(): pl.pallas_call(kernel, out_shape=shapes, in_specs=specs, out_specs=[VM] *...  50.3 us
    unnamed x84, local copies, waits for them, and re-layouts  22.4 us
    all_to_all x1, blocking collectives, shards(): lax.all_to_all(jnp.broadcast_to(block[None], (128, 8, 128)), NAMES, 0, 0,...  20.8 us
    all_to_all x2, waiting for transfers between devices, shards(): got = lax.all_to_all(parts, ('x', 'z'), 0, 0, tiled=True)  19.2 us
    all_to_all x2, starting transfers between devices, shards(): got = lax.all_to_all(parts, ('x', 'z'), 0, 0, tiled=True)  8.97 us
  transfers between devices with their start and end apart: 52, of which 30 were waited for; matrix products, arithmetic and copies ran while one was open for 1% of the time, Pallas kernels for 7%

profile of v3, /device:TPU:1, one launch (start us, length us, event | category | flops | bytes accessed | tf_op | source)
XLA Modules:
  0.0 432.4 jit_solution(12666913883486844604)
XLA Ops:
  0.7 1.6 copy-done.18
  2.6 2.2 copy-done.26
  4.8 1.7 split_down.1
  7.8 3.7 collective-permute-start.11
  12.0 25.5 %collective-permute-done = bf16[512,128]{1,0:T(8,128)(2,1)} collective-permute-done((bf16[512,128]{1,0:T(8,128)(2,1)S(1)}, bf16[512,128]{1,0:T(8,128)(2,1)}, u32[]{:S(2)}, u32[]{:S(2)}) %collective-permute-start) | collective-permute-done | bytes 131104 | tf_op jit(solution)/shard_map/ppermute | solution.py:26
  38.6 2.5 collective-permute-start.1
  42.3 3.6 collective-permute-start.4
  46.0 7.3 %collective-permute-start.10 = (bf16[1024,512]{1,0:T(8,128)(2,1)S(1)}, bf16[1024,512]{1,0:T(8,128)(2,1)S(1)}, u32[]{:S(2)}, u32[]{:S(2)}) collective-permute-start(bf16[1024,512]{1,0:T(8,128)(2,1)S(1)} %get-tuple-element.80.refs_9_), channel_id=1, source_target_pairs={{32,0},{0,32},{33,1},{1,33},{34,2},{2,34},{35,3},{3,35},{36,4},{4,... | collective-permute-start | bytes 3145736 | tf_op jit(solution)/shard_map/ppermute | solution.py:26
  53.3 3.2 collective-permute-done.3
  56.7 3.8 collective-permute-start.5
  61.6 7.5 %collective-permute-done.6.refs_3_ = bf16[512,256]{1,0:T(8,128)(2,1)S(1)} collective-permute-done((bf16[512,256]{1,0:T(8,128)(2,1)S(1)}, bf16[512,256]{1,0:T(8,128)(2,1)S(1)}, u32[]{:S(2)}, u32[]{:S(2)}) %collective-permute-start.6) | collective-permute-done | bytes 262176 | tf_op jit(solution)/shard_map/ppermute | solution.py:26
  69.7 8.0 %collective-permute-done.7.refs_4_ = bf16[512,256]{1,0:T(8,128)(2,1)S(1)} collective-permute-done((bf16[512,256]{1,0:T(8,128)(2,1)S(1)}, bf16[512,256]{1,0:T(8,128)(2,1)S(1)}, u32[]{:S(2)}, u32[]{:S(2)}) %collective-permute-start.7) | collective-permute-done | bytes 262176 | tf_op jit(solution)/shard_map/ppermute | solution.py:26
  77.6 7.3 %collective-permute-done.8.refs_5_ = bf16[512,256]{1,0:T(8,128)(2,1)S(1)} collective-permute-done((bf16[512,256]{1,0:T(8,128)(2,1)S(1)}, bf16[512,256]{1,0:T(8,128)(2,1)S(1)}, u32[]{:S(2)}, u32[]{:S(2)}) %collective-permute-start.8) | collective-permute-done | bytes 262176 | tf_op jit(solution)/shard_map/ppermute | solution.py:26
  85.6 2.2 copy-done.25
  87.8 9.7 %front.1 = (bf16[512,4096]{1,0:T(8,128)(2,1)S(1)}, f32[512,512]{1,0:T(8,128)S(1)}, f32[512,512]{1,0:T(8,128)S(1)}, bf16[512,512]{1,0:T(8,128)(2,1)S(1)}) custom-call(s32[9]{0:T(128)S(1)} %stack.81.pos, bf16[4,512,256]{2,1,0:T(8,128)(2,1)S(1)} %pad_maximum_fusion.refs_0_, bf16[4,512,256]{2,1,0:T(8,128)(2,1)S(1)} %collective-permute-done.5.refs_1_, ...), custom_call_target="tpu_custom_call" | custom-call | tf_op jit(solution)/shard_map/front/pallas_call | solution.py:40
  97.5 2.1 collective-permute-start.14
  101.2 5.1 %collective-permute-done.14.two.feats = bf16[512,4096]{1,0:T(8,128)(2,1)S(1)} collective-permute-done((bf16[512,4096]{1,0:T(8,128)(2,1)S(1)}, bf16[512,4096]{1,0:T(8,128)(2,1)S(1)}, u32[]{:S(2)}, u32[]{:S(2)}) %collective-permute-start.14) | collective-permute-done | bytes 4194336 | tf_op jit(solution)/shard_map/ppermute | solution.py:26
  106.4 4.5 %near_gram.1.near = f32[512,1024]{1,0:T(8,128)S(1)} custom-call(bf16[512,4096]{1,0:T(8,128)(2,1)S(1)} %get-tuple-element.97.feats.one, bf16[512,4096]{1,0:T(8,128)(2,1)S(1)} %get-tuple-element.97.feats.one, bf16[512,4096]{1,0:T(8,128)(2,1)S(1)} %collective-permute-done.14.two.feats), custom_call_target="tpu_custom_call" | custom-call | tf_op jit(solution)/shard_map/near_gram/pallas_call | solution.py:40
  112.3 45.8 %collective-permute-done.13.other = bf16[512,512]{1,0:T(8,128)(2,1)S(1)} collective-permute-done((bf16[512,512]{1,0:T(8,128)(2,1)S(1)}, bf16[512,512]{1,0:T(8,128)(2,1)S(1)}, u32[]{:S(2)}, u32[]{:S(2)}) %collective-permute-start.13) | collective-permute-done | bytes 524320 | tf_op jit(solution)/shard_map/ppermute | solution.py:26
  158.0 2.3 push.2
  163.0 4.5 %all-to-all-start = ((bf16[16,512,128]{2,1,0:T(8,128)(2,1)}), bf16[16,512,128]{2,1,0:T(8,128)(2,1)}, u32[]{:S(2)}, u32[]{:S(2)}) async-start(bf16[16,512,128]{2,1,0:T(8,128)(2,1)} %copy-done.24), calls=%async_computation | async-start | bytes 4194304 | tf_op jit(solution)/shard_map/all_to_all | solution.py:331
  168.9 1.6 collective-permute-start.20
  170.5 23.5 %collective-permute-done.20.one = bf16[128,4096]{1,0:T(8,128)(2,1)S(1)} collective-permute-done((bf16[128,4096]{1,0:T(8,128)(2,1)S(1)}, bf16[128,4096]{1,0:T(8,128)(2,1)S(1)}, u32[]{:S(2)}, u32[]{:S(2)}) %collective-permute-start.20) | collective-permute-done | bytes 1048608 | tf_op jit(solution)/shard_map/ppermute | solution.py:26
  194.0 2.1 collective-permute-start.21
  196.0 2.2 copy-done.7
  202.0 1.9 weigh.2
  203.9 2.6 collective-permute-start.16
  207.6 2.7 collective-permute-start.19
  210.3 1.8 collective-permute-done.16
  212.8 3.4 collective-permute-done.18
  216.3 2.5 collective-permute-start.22
  220.5 2.2 copy-done.2
  222.7 3.7 far_gram.1.p0
  227.4 2.1 collective-permute-done.22.refs_1_
  229.5 3.1 collective-permute-done.26.refs_6_
  232.6 2.4 back_other.2
  237.4 9.4 %collective-permute-done.30.got = bf16[512,512]{1,0:T(8,128)(2,1)S(1)} collective-permute-done((bf16[512,512]{1,0:T(8,128)(2,1)S(1)}, bf16[512,512]{1,0:T(8,128)(2,1)S(1)}, u32[]{:S(2)}, u32[]{:S(2)}) %collective-permute-start.30) | collective-permute-done | bytes 524320 | tf_op jit(solution)/shard_map/ppermute | solution.py:26
  247.4 1.6 collective-permute-start.32
  249.1 2.9 collective-permute-start.31
  251.9 8.3 %collective-permute-done.32.d2 = bf16[528,512]{1,0:T(8,128)(2,1)S(1)} collective-permute-done((bf16[528,512]{1,0:T(8,128)(2,1)S(1)}, bf16[528,512]{1,0:T(8,128)(2,1)S(1)}, u32[]{:S(2)}, u32[]{:S(2)}) %collective-permute-start.32) | collective-permute-done | bytes 540704 | tf_op jit(solution)/shard_map/ppermute | solution.py:26
  260.2 3.5 collective-permute-start.33
  265.2 12.1 %collective-permute-done.27.p1 = f32[512,256]{1,0:T(8,128)S(1)} collective-permute-done((f32[512,256]{1,0:T(8,128)S(1)}, f32[512,256]{1,0:T(8,128)S(1)}, u32[]{:S(2)}, u32[]{:S(2)}) %collective-permute-start.27) | collective-permute-done | bytes 524320 | tf_op jit(solution)/shard_map/ppermute | solution.py:26
  278.7 11.6 %collective-permute-done.29.p3 = f32[512,256]{1,0:T(8,128)S(1)} collective-permute-done((f32[512,256]{1,0:T(8,128)S(1)}, f32[512,256]{1,0:T(8,128)S(1)}, u32[]{:S(2)}, u32[]{:S(2)}) %collective-permute-start.29) | collective-permute-done | bytes 524320 | tf_op jit(solution)/shard_map/ppermute | solution.py:26
  296.4 12.3 %collective-permute-done.34.other = bf16[528,512]{1,0:T(8,128)(2,1)S(1)} collective-permute-done((bf16[528,512]{1,0:T(8,128)(2,1)S(1)}, bf16[528,512]{1,0:T(8,128)(2,1)S(1)}, u32[]{:S(2)}, u32[]{:S(2)}) %collective-permute-start.34) | collective-permute-done | bytes 540704 | tf_op jit(solution)/shard_map/ppermute | solution.py:26
  308.7 2.3 push.3
  312.4 4.4 %all-to-all-start.1 = ((bf16[16,528,128]{2,1,0:T(8,128)(2,1)}), bf16[16,528,128]{2,1,0:T(8,128)(2,1)}, u32[]{:S(2)}, u32[]{:S(2)}) async-start(bf16[16,528,128]{2,1,0:T(8,128)(2,1)} %copy-done.17), calls=%async_computation.1 | async-start | bytes 4325376 | tf_op jit(solution)/shard_map/all_to_all | solution.py:357
  316.9 3.3 constant_dynamic-slice_fusion
  324.4 19.2 %all-to-all-done.1.got = bf16[16,528,128]{2,1,0:T(8,128)(2,1)} async-done(((bf16[16,528,128]{2,1,0:T(8,128)(2,1)}), bf16[16,528,128]{2,1,0:T(8,128)(2,1)}, u32[]{:S(2)}, u32[]{:S(2)}) %all-to-all-start.1) | async-done | bytes 2162720 | tf_op jit(solution)/shard_map/all_to_all | solution.py:357
  344.7 1.9 weigh.3
  346.6 1.9 collective-permute-start.35
  349.6 3.1 collective-permute-start.38
  352.7 1.8 collective-permute-done.36
  355.8 3.3 collective-permute-start.39
  360.7 3.3 collective-permute-done.40.refs_3_
  364.0 2.4 collective-permute-done.41.refs_4_
  366.4 3.8 collective-permute-done.42.refs_5_
  370.2 2.4 back_other.3
  373.4 2.2 far_rows.1
  377.0 4.7 %collective-permute-done.44.got = bf16[512,512]{1,0:T(8,128)(2,1)S(1)} collective-permute-done((bf16[512,512]{1,0:T(8,128)(2,1)S(1)}, bf16[512,512]{1,0:T(8,128)(2,1)S(1)}, u32[]{:S(2)}, u32[]{:S(2)}) %collective-permute-start.44) | collective-permute-done | bytes 524320 | tf_op jit(solution)/shard_map/ppermute | solution.py:26
  381.6 5.4 %collective-permute-start.47 = (bf16[1024,512]{1,0:T(8,128)(2,1)S(1)}, bf16[1024,512]{1,0:T(8,128)(2,1)S(1)}, u32[]{:S(2)}, u32[]{:S(2)}) collective-permute-start(bf16[1024,512]{1,0:T(8,128)(2,1)S(1)} %get-tuple-element.131), channel_id=1, source_target_pairs={{32,0},{0,32},{33,1},{1,33},{34,2},{2,34},{35,3},{3,35},{36,4},{4,... | collective-permute-start | bytes 3145736 | tf_op jit(solution)/shard_map/ppermute | solution.py:26
  389.5 13.5 %collective-permute-done.48.d2 = bf16[512,512]{1,0:T(8,128)(2,1)S(1)} collective-permute-done((bf16[512,512]{1,0:T(8,128)(2,1)S(1)}, bf16[512,512]{1,0:T(8,128)(2,1)S(1)}, u32[]{:S(2)}, u32[]{:S(2)}) %collective-permute-start.48) | collective-permute-done | bytes 524320 | tf_op jit(solution)/shard_map/ppermute | solution.py:26
  406.4 1.7 last_image.1
  408.1 20.8 %all_to_all.15.got = f32[128,8,128]{2,1,0:T(8,128)S(1)} all-to-all(f32[128,8,128]{2,1,0:T(8,128)S(1)} %broadcast_in_dim.2), channel_id=1, replica_groups=mesh['yh'=2,'c'=2,'x'=4,'z'=4,'yl'=2] {'yh','c','x','z','yl'}, dimensions={0} | all-to-all | bytes 1048576 | tf_op jit(solution)/shard_map/all_to_all | solution.py:389
  428.9 2.6 final.1
  (160 shorter events, 53.1 us)
Async XLA Ops:
  7.8 52.7 %collective-permute-start.11 = (bf16[1024,512]{1,0:T(8,128)(2,1)S(1)}, bf16[1024,512]{1,0:T(8,128)(2,1)}, u32[]{:S(2)}, u32[]{:S(2)}) collective-permute-start(bf16[1024,512]{1,0:T(8,128)(2,1)S(1)} %get-tuple-element.80.refs_9_), channel_id=1, source_target_pairs={{64,0},{0,64},{65,1},{1,65},{66,2},{2,66},{67,3},{3,67},{68,4},{4,... | collective-permute-start | bytes 3145736 | tf_op jit(solution)/shard_map/ppermute | solution.py:26
  11.6 25.9 %collective-permute-start = (bf16[512,128]{1,0:T(8,128)(2,1)S(1)}, bf16[512,128]{1,0:T(8,128)(2,1)}, u32[]{:S(2)}, u32[]{:S(2)}) collective-permute-start(bf16[512,128]{1,0:T(8,128)(2,1)S(1)} %copy-done.41), channel_id=1, source_target_pairs={{1,0},{0,1},{3,2},{2,3},{5,4},{4,5},{7,6},{6,7},{9,8},{8,9},{11,10... | collective-permute-start | bytes 393224 | tf_op jit(solution)/shard_map/ppermute | solution.py:26
  38.6 7.4 %collective-permute-start.1 = (bf16[512,256]{1,0:T(8,128)(2,1)S(1)}, bf16[512,256]{1,0:T(8,128)(2,1)S(1)}, u32[]{:S(2)}, u32[]{:S(2)}) collective-permute-start(bf16[512,256]{1,0:T(8,128)(2,1)S(1)} %maximum_select_fusion), channel_id=1, source_target_pairs={{8,0},{16,8},{24,16},{0,24},{9,1},{17,9},{25,17},{1,25},{10,2},{18... | collective-permute-start | bytes 786440 | tf_op jit(solution)/shard_map/ppermute | solution.py:26
  41.2 12.2 %collective-permute-start.2 = (bf16[512,256]{1,0:T(8,128)(2,1)S(1)}, bf16[512,256]{1,0:T(8,128)(2,1)S(1)}, u32[]{:S(2)}, u32[]{:S(2)}) collective-permute-start(bf16[512,256]{1,0:T(8,128)(2,1)S(1)} %maximum_select_fusion), channel_id=1, source_target_pairs={{16,0},{24,8},{0,16},{8,24},{17,1},{25,9},{1,17},{9,25},{18,2},{26... | collective-permute-start | bytes 786440 | tf_op jit(solution)/shard_map/ppermute | solution.py:26
  41.7 14.8 %collective-permute-start.3 = (bf16[512,256]{1,0:T(8,128)(2,1)S(1)}, bf16[512,256]{1,0:T(8,128)(2,1)S(1)}, u32[]{:S(2)}, u32[]{:S(2)}) collective-permute-start(bf16[512,256]{1,0:T(8,128)(2,1)S(1)} %maximum_select_fusion), channel_id=1, source_target_pairs={{24,0},{0,8},{8,16},{16,24},{25,1},{1,9},{9,17},{17,25},{26,2},{2,... | collective-permute-start | bytes 786440 | tf_op jit(solution)/shard_map/ppermute | solution.py:26
  42.3 14.2 %collective-permute-start.4 = (bf16[512,256]{1,0:T(8,128)(2,1)S(1)}, bf16[512,256]{1,0:T(8,128)(2,1)S(1)}, u32[]{:S(2)}, u32[]{:S(2)}) collective-permute-start(bf16[512,256]{1,0:T(8,128)(2,1)S(1)} %maximum_select_fusion), channel_id=1, source_target_pairs={{4,0},{6,2},{0,4},{2,6},{5,1},{7,3},{1,5},{3,7},{12,8},{14,10},{8,... | collective-permute-start | bytes 786440 | tf_op jit(solution)/shard_map/ppermute | solution.py:26
  46.0 38.9 %collective-permute-start.10 = (bf16[1024,512]{1,0:T(8,128)(2,1)S(1)}, bf16[1024,512]{1,0:T(8,128)(2,1)S(1)}, u32[]{:S(2)}, u32[]{:S(2)}) collective-permute-start(bf16[1024,512]{1,0:T(8,128)(2,1)S(1)} %get-tuple-element.80.refs_9_), channel_id=1, source_target_pairs={{32,0},{0,32},{33,1},{1,33},{34,2},{2,34},{35,3},{3,35},{36,4},{4,... | collective-permute-start | bytes 3145736 | tf_op jit(solution)/shard_map/ppermute | solution.py:26
  56.5 43.1 %copy-start.40 = (bf16[512,2048]{1,0:T(8,128)(2,1)S(1)}, bf16[512,2048]{1,0:T(8,128)(2,1)}, u32[]{:S(2)}) copy-start(bf16[512,2048]{1,0:T(8,128)(2,1)} %copy-done.39) | copy-start | bytes 6291460
  56.7 28.2 %collective-permute-start.5 = (bf16[4,512,256]{2,1,0:T(8,128)(2,1)S(1)}, bf16[4,512,256]{2,1,0:T(8,128)(2,1)S(1)}, u32[]{:S(2)}, u32[]{:S(2)}) collective-permute-start(bf16[4,512,256]{2,1,0:T(8,128)(2,1)S(1)} %pad_maximum_fusion.refs_0_), channel_id=1, source_target_pairs={{2,0},{4,2},{6,4},{0,6},{3,1},{5,3},{7,5},{1,7},{10,8},{12,10},{14... | collective-permute-start | bytes 3145736 | tf_op jit(solution)/shard_map/ppermute | solution.py:26
  60.5 25.1 %collective-permute-start.9 = (bf16[4,512,256]{2,1,0:T(8,128)(2,1)S(1)}, bf16[4,512,256]{2,1,0:T(8,128)(2,1)S(1)}, u32[]{:S(2)}, u32[]{:S(2)}) collective-permute-start(bf16[4,512,256]{2,1,0:T(8,128)(2,1)S(1)} %pad_maximum_fusion.refs_0_), channel_id=1, source_target_pairs={{6,0},{0,2},{2,4},{4,6},{7,1},{1,3},{3,5},{5,7},{14,8},{8,10},{10,... | collective-permute-start | bytes 3145736 | tf_op jit(solution)/shard_map/ppermute | solution.py:26
  60.5 25.1 %collective-permute-start.12 = (bf16[1024,512]{1,0:T(8,128)(2,1)}, bf16[1024,512]{1,0:T(8,128)(2,1)S(1)}, u32[]{:S(2)}, u32[]{:S(2)}) collective-permute-start(bf16[1024,512]{1,0:T(8,128)(2,1)} %collective-permute-done.11.refs_11_), channel_id=1, source_target_pairs={{32,0},{0,32},{33,1},{1,33},{34,2},{2,34},{35,3},{3,35},{36,4},{4,... | collective-permute-start | bytes 3145736 | tf_op jit(solution)/shard_map/ppermute | solution.py:26
  61.3 7.9 %collective-permute-start.6 = (bf16[512,256]{1,0:T(8,128)(2,1)S(1)}, bf16[512,256]{1,0:T(8,128)(2,1)S(1)}, u32[]{:S(2)}, u32[]{:S(2)}) collective-permute-start(bf16[512,256]{1,0:T(8,128)(2,1)S(1)} %collective-permute-done.4.refs_2_), channel_id=1, source_target_pairs={{8,0},{16,8},{24,16},{0,24},{9,1},{17,9},{25,17},{1,25},{10,2},{18... | collective-permute-start | bytes 786440 | tf_op jit(solution)/shard_map/ppermute | solution.py:26
  69.1 8.5 %collective-permute-start.7 = (bf16[512,256]{1,0:T(8,128)(2,1)S(1)}, bf16[512,256]{1,0:T(8,128)(2,1)S(1)}, u32[]{:S(2)}, u32[]{:S(2)}) collective-permute-start(bf16[512,256]{1,0:T(8,128)(2,1)S(1)} %collective-permute-done.4.refs_2_), channel_id=1, source_target_pairs={{16,0},{24,8},{0,16},{8,24},{17,1},{25,9},{1,17},{9,25},{18,2},{26... | collective-permute-start | bytes 786440 | tf_op jit(solution)/shard_map/ppermute | solution.py:26
  77.6 7.3 %collective-permute-start.8 = (bf16[512,256]{1,0:T(8,128)(2,1)S(1)}, bf16[512,256]{1,0:T(8,128)(2,1)S(1)}, u32[]{:S(2)}, u32[]{:S(2)}) collective-permute-start(bf16[512,256]{1,0:T(8,128)(2,1)S(1)} %collective-permute-done.4.refs_2_), channel_id=1, source_target_pairs={{24,0},{0,8},{8,16},{16,24},{25,1},{1,9},{9,17},{17,25},{26,2},{2,... | collective-permute-start | bytes 786440 | tf_op jit(solution)/shard_map/ppermute | solution.py:26
  97.5 8.8 %collective-permute-start.14 = (bf16[512,4096]{1,0:T(8,128)(2,1)S(1)}, bf16[512,4096]{1,0:T(8,128)(2,1)S(1)}, u32[]{:S(2)}, u32[]{:S(2)}) collective-permute-start(bf16[512,4096]{1,0:T(8,128)(2,1)S(1)} %get-tuple-element.97.feats.one), channel_id=1, source_target_pairs={{32,0},{0,32},{33,1},{1,33},{34,2},{2,34},{35,3},{3,35},{36,4},{4,... | collective-permute-start | bytes 12582920 | tf_op jit(solution)/shard_map/ppermute | solution.py:26
  99.6 58.4 %collective-permute-start.15 = (bf16[512,2048]{1,0:T(8,128)(2,1)S(1)}, bf16[512,2048]{1,0:T(8,128)(2,1)S(1)}, u32[]{:S(2)}, u32[]{:S(2)}) collective-permute-start(bf16[512,2048]{1,0:T(8,128)(2,1)S(1)} %copy-done.40), channel_id=1, source_target_pairs={{1,0},{0,1},{3,2},{2,3},{5,4},{4,5},{7,6},{6,7},{9,8},{8,9},{11,10... | collective-permute-start | bytes 6291464 | tf_op jit(solution)/shard_map/ppermute | solution.py:26
  100.7 57.3 %collective-permute-start.13 = (bf16[512,512]{1,0:T(8,128)(2,1)S(1)}, bf16[512,512]{1,0:T(8,128)(2,1)S(1)}, u32[]{:S(2)}, u32[]{:S(2)}) collective-permute-start(bf16[512,512]{1,0:T(8,128)(2,1)S(1)} %get-tuple-element.81.own), channel_id=1, source_target_pairs={{1,0},{0,1},{3,2},{2,3},{5,4},{4,5},{7,6},{6,7},{9,8},{8,9},{11,10... | collective-permute-start | bytes 1572872 | tf_op jit(solution)/shard_map/ppermute | solution.py:26
  163.0 39.0 %all-to-all-start = ((bf16[16,512,128]{2,1,0:T(8,128)(2,1)}), bf16[16,512,128]{2,1,0:T(8,128)(2,1)}, u32[]{:S(2)}, u32[]{:S(2)}) async-start(bf16[16,512,128]{2,1,0:T(8,128)(2,1)} %copy-done.24), calls=%async_computation | async-start | bytes 4194304 | tf_op jit(solution)/shard_map/all_to_all | solution.py:331
  168.9 31.2 %copy-start.1 = (bf16[512,4096]{1,0:T(8,128)(2,1)S(1)}, bf16[512,4096]{1,0:T(8,128)(2,1)}, u32[]{:S(2)}) copy-start(bf16[512,4096]{1,0:T(8,128)(2,1)} %copy-done) | copy-start | bytes 12582916
  168.9 25.1 %collective-permute-start.20 = (bf16[128,4096]{1,0:T(8,128)(2,1)S(1)}, bf16[128,4096]{1,0:T(8,128)(2,1)S(1)}, u32[]{:S(2)}, u32[]{:S(2)}) collective-permute-start(bf16[128,4096]{1,0:T(8,128)(2,1)S(1)} %constant_dynamic-slice_fusion.1), channel_id=1, source_target_pairs={{64,0},{0,64},{65,1},{1,65},{66,2},{2,66},{67,3},{3,67},{68,4},{4,... | collective-permute-start | bytes 3145736 | tf_op jit(solution)/shard_map/ppermute | solution.py:26
  194.0 25.3 %collective-permute-start.21 = (bf16[128,4096]{1,0:T(8,128)(2,1)S(1)}, bf16[128,4096]{1,0:T(8,128)(2,1)}, u32[]{:S(2)}, u32[]{:S(2)}) collective-permute-start(bf16[128,4096]{1,0:T(8,128)(2,1)S(1)} %collective-permute-done.20.one), channel_id=1, source_target_pairs={{32,0},{0,32},{33,1},{1,33},{34,2},{2,34},{35,3},{3,35},{36,4},{4,... | collective-permute-start | bytes 3145736 | tf_op jit(solution)/shard_map/ppermute | solution.py:26
  203.8 15.5 %copy-start.37 = (f32[512,128]{1,0:T(8,128)}, f32[512,128]{1,0:T(8,128)S(1)}, u32[]{:S(2)}) copy-start(f32[512,128]{1,0:T(8,128)S(1)} %get-tuple-element.112.moved) | copy-start | bytes 786436
  203.9 8.2 %collective-permute-start.16 = (bf16[512,128]{1,0:T(8,128)(2,1)S(1)}, bf16[512,128]{1,0:T(8,128)(2,1)S(1)}, u32[]{:S(2)}, u32[]{:S(2)}) collective-permute-start(bf16[512,128]{1,0:T(8,128)(2,1)S(1)} %get-tuple-element.93), channel_id=1, source_target_pairs={{8,0},{16,8},{24,16},{0,24},{9,1},{17,9},{25,17},{1,25},{10,2},{18... | collective-permute-start | bytes 393224 | tf_op jit(solution)/shard_map/ppermute | solution.py:26
  206.4 6.4 %collective-permute-start.17 = (bf16[512,128]{1,0:T(8,128)(2,1)S(1)}, bf16[512,128]{1,0:T(8,128)(2,1)S(1)}, u32[]{:S(2)}, u32[]{:S(2)}) collective-permute-start(bf16[512,128]{1,0:T(8,128)(2,1)S(1)} %get-tuple-element.93), channel_id=1, source_target_pairs={{16,0},{24,8},{0,16},{8,24},{17,1},{25,9},{1,17},{9,25},{18,2},{26... | collective-permute-start | bytes 393224 | tf_op jit(solution)/shard_map/ppermute | solution.py:26
  207.0 9.2 %collective-permute-start.18 = (bf16[512,128]{1,0:T(8,128)(2,1)S(1)}, bf16[512,128]{1,0:T(8,128)(2,1)S(1)}, u32[]{:S(2)}, u32[]{:S(2)}) collective-permute-start(bf16[512,128]{1,0:T(8,128)(2,1)S(1)} %get-tuple-element.93), channel_id=1, source_target_pairs={{24,0},{0,8},{8,16},{16,24},{25,1},{1,9},{9,17},{17,25},{26,2},{2,... | collective-permute-start | bytes 393224 | tf_op jit(solution)/shard_map/ppermute | solution.py:26
  207.6 8.6 %collective-permute-start.19 = (bf16[512,128]{1,0:T(8,128)(2,1)S(1)}, bf16[512,128]{1,0:T(8,128)(2,1)S(1)}, u32[]{:S(2)}, u32[]{:S(2)}) collective-permute-start(bf16[512,128]{1,0:T(8,128)(2,1)S(1)} %get-tuple-element.93), channel_id=1, source_target_pairs={{4,0},{6,2},{0,4},{2,6},{5,1},{7,3},{1,5},{3,7},{12,8},{14,10},{8,... | collective-permute-start | bytes 393224 | tf_op jit(solution)/shard_map/ppermute | solution.py:26
  216.3 13.3 %collective-permute-start.22 = (bf16[4,512,128]{2,1,0:T(8,128)(2,1)S(1)}, bf16[4,512,128]{2,1,0:T(8,128)(2,1)S(1)}, u32[]{:S(2)}, u32[]{:S(2)}) collective-permute-start(bf16[4,512,128]{2,1,0:T(8,128)(2,1)S(1)} %pad_maximum_fusion.1.refs_0_), channel_id=1, source_target_pairs={{2,0},{4,2},{6,4},{0,6},{3,1},{5,3},{7,5},{1,7},{10,8},{12,10},{14... | collective-permute-start | bytes 1572872 | tf_op jit(solution)/shard_map/ppermute | solution.py:26
  218.7 13.9 %collective-permute-start.26 = (bf16[4,512,128]{2,1,0:T(8,128)(2,1)S(1)}, bf16[4,512,128]{2,1,0:T(8,128)(2,1)S(1)}, u32[]{:S(2)}, u32[]{:S(2)}) collective-permute-start(bf16[4,512,128]{2,1,0:T(8,128)(2,1)S(1)} %pad_maximum_fusion.1.refs_0_), channel_id=1, source_target_pairs={{6,0},{0,2},{2,4},{4,6},{7,1},{1,3},{3,5},{5,7},{14,8},{8,10},{10,... | collective-permute-start | bytes 1572872 | tf_op jit(solution)/shard_map/ppermute | solution.py:26
  218.7 7.7 %collective-permute-start.23 = (bf16[512,128]{1,0:T(8,128)(2,1)S(1)}, bf16[512,128]{1,0:T(8,128)(2,1)S(1)}, u32[]{:S(2)}, u32[]{:S(2)}) collective-permute-start(bf16[512,128]{1,0:T(8,128)(2,1)S(1)} %collective-permute-done.19.refs_2_), channel_id=1, source_target_pairs={{8,0},{16,8},{24,16},{0,24},{9,1},{17,9},{25,17},{1,25},{10,2},{18... | collective-permute-start | bytes 393224 | tf_op jit(solution)/shard_map/ppermute | solution.py:26
  218.7 7.7 %collective-permute-start.24 = (bf16[512,128]{1,0:T(8,128)(2,1)S(1)}, bf16[512,128]{1,0:T(8,128)(2,1)S(1)}, u32[]{:S(2)}, u32[]{:S(2)}) collective-permute-start(bf16[512,128]{1,0:T(8,128)(2,1)S(1)} %collective-permute-done.19.refs_2_), channel_id=1, source_target_pairs={{16,0},{24,8},{0,16},{8,24},{17,1},{25,9},{1,17},{9,25},{18,2},{26... | collective-permute-start | bytes 393224 | tf_op jit(solution)/shard_map/ppermute | solution.py:26
  219.3 8.1 %collective-permute-start.25 = (bf16[512,128]{1,0:T(8,128)(2,1)S(1)}, bf16[512,128]{1,0:T(8,128)(2,1)S(1)}, u32[]{:S(2)}, u32[]{:S(2)}) collective-permute-start(bf16[512,128]{1,0:T(8,128)(2,1)S(1)} %collective-permute-done.19.refs_2_), channel_id=1, source_target_pairs={{24,0},{0,8},{8,16},{16,24},{25,1},{1,9},{9,17},{17,25},{26,2},{2,... | collective-permute-start | bytes 393224 | tf_op jit(solution)/shard_map/ppermute | solution.py:26
  235.0 11.8 %collective-permute-start.30 = (bf16[512,512]{1,0:T(8,128)(2,1)S(1)}, bf16[512,512]{1,0:T(8,128)(2,1)S(1)}, u32[]{:S(2)}, u32[]{:S(2)}) collective-permute-start(bf16[512,512]{1,0:T(8,128)(2,1)S(1)} %get-tuple-element.102), channel_id=1, source_target_pairs={{1,0},{0,1},{3,2},{2,3},{5,4},{4,5},{7,6},{6,7},{9,8},{8,9},{11,10... | collective-permute-start | bytes 1572872 | tf_op jit(solution)/shard_map/ppermute | solution.py:26
  246.9 43.5 %copy-start.21 = (f32[512,1024]{1,0:T(8,128)S(1)}, f32[512,1024]{1,0:T(8,128)}, u32[]{:S(2)}) copy-start(f32[512,1024]{1,0:T(8,128)} %copy-done.20) | copy-start | bytes 6291460
  247.4 12.8 %collective-permute-start.32 = (bf16[528,512]{1,0:T(8,128)(2,1)S(1)}, bf16[528,512]{1,0:T(8,128)(2,1)S(1)}, u32[]{:S(2)}, u32[]{:S(2)}) collective-permute-start(bf16[528,512]{1,0:T(8,128)(2,1)S(1)} %delta.2.d0.delta_one), channel_id=1, source_target_pairs={{64,0},{0,64},{65,1},{1,65},{66,2},{2,66},{67,3},{3,67},{68,4},{4,... | collective-permute-start | bytes 1622024 | tf_op jit(solution)/shard_map/ppermute | solution.py:26
  249.1 42.7 %collective-permute-start.31 = (bf16[528,512]{1,0:T(8,128)(2,1)S(1)}, bf16[528,512]{1,0:T(8,128)(2,1)S(1)}, u32[]{:S(2)}, u32[]{:S(2)}) collective-permute-start(bf16[528,512]{1,0:T(8,128)(2,1)S(1)} %delta.2.d0.delta_one), channel_id=1, source_target_pairs={{32,0},{0,32},{33,1},{1,33},{34,2},{2,34},{35,3},{3,35},{36,4},{4,... | collective-permute-start | bytes 1622024 | tf_op jit(solution)/shard_map/ppermute | solution.py:26
  260.2 32.9 %copy-start.30 = (bf16[528,512]{1,0:T(8,128)(2,1)}, bf16[528,512]{1,0:T(8,128)(2,1)S(1)}, u32[]{:S(2)}) copy-start(bf16[528,512]{1,0:T(8,128)(2,1)S(1)} %collective-permute-done.32.d2) | copy-start | bytes 1622020
  260.2 32.9 %collective-permute-start.33 = (bf16[528,512]{1,0:T(8,128)(2,1)S(1)}, bf16[528,512]{1,0:T(8,128)(2,1)S(1)}, u32[]{:S(2)}, u32[]{:S(2)}) collective-permute-start(bf16[528,512]{1,0:T(8,128)(2,1)S(1)} %collective-permute-done.32.d2), channel_id=1, source_target_pairs={{32,0},{0,32},{33,1},{1,33},{34,2},{2,34},{35,3},{3,35},{36,4},{4,... | collective-permute-start | bytes 1622024 | tf_op jit(solution)/shard_map/ppermute | solution.py:26
  263.7 13.6 %collective-permute-start.27 = (f32[512,256]{1,0:T(8,128)S(1)}, f32[512,256]{1,0:T(8,128)S(1)}, u32[]{:S(2)}, u32[]{:S(2)}) collective-permute-start(f32[512,256]{1,0:T(8,128)S(1)} %far_gram.1.p0), channel_id=1, source_target_pairs={{8,0},{16,8},{24,16},{0,24},{9,1},{17,9},{25,17},{1,25},{10,2},{18... | collective-permute-start | bytes 1572872 | tf_op jit(solution)/shard_map/ppermute | solution.py:26
  263.7 15.0 %collective-permute-start.28 = (f32[512,256]{1,0:T(8,128)S(1)}, f32[512,256]{1,0:T(8,128)S(1)}, u32[]{:S(2)}, u32[]{:S(2)}) collective-permute-start(f32[512,256]{1,0:T(8,128)S(1)} %far_gram.1.p0), channel_id=1, source_target_pairs={{16,0},{24,8},{0,16},{8,24},{17,1},{25,9},{1,17},{9,25},{18,2},{26... | collective-permute-start | bytes 1572872 | tf_op jit(solution)/shard_map/ppermute | solution.py:26
  264.3 26.1 %collective-permute-start.29 = (f32[512,256]{1,0:T(8,128)S(1)}, f32[512,256]{1,0:T(8,128)S(1)}, u32[]{:S(2)}, u32[]{:S(2)}) collective-permute-start(f32[512,256]{1,0:T(8,128)S(1)} %far_gram.1.p0), channel_id=1, source_target_pairs={{24,0},{0,8},{8,16},{16,24},{25,1},{1,9},{9,17},{17,25},{26,2},{2,... | collective-permute-start | bytes 1572872 | tf_op jit(solution)/shard_map/ppermute | solution.py:26
  295.3 13.4 %collective-permute-start.34 = (bf16[528,512]{1,0:T(8,128)(2,1)S(1)}, bf16[528,512]{1,0:T(8,128)(2,1)S(1)}, u32[]{:S(2)}, u32[]{:S(2)}) collective-permute-start(bf16[528,512]{1,0:T(8,128)(2,1)S(1)} %get-tuple-element.109.own), channel_id=1, source_target_pairs={{1,0},{0,1},{3,2},{2,3},{5,4},{4,5},{7,6},{6,7},{9,8},{8,9},{11,10... | collective-permute-start | bytes 1622024 | tf_op jit(solution)/shard_map/ppermute | solution.py:26
  312.4 31.2 %all-to-all-start.1 = ((bf16[16,528,128]{2,1,0:T(8,128)(2,1)}), bf16[16,528,128]{2,1,0:T(8,128)(2,1)}, u32[]{:S(2)}, u32[]{:S(2)}) async-start(bf16[16,528,128]{2,1,0:T(8,128)(2,1)} %copy-done.17), calls=%async_computation.1 | async-start | bytes 4325376 | tf_op jit(solution)/shard_map/all_to_all | solution.py:357
  320.2 53.3 %collective-permute-start.45 = (bf16[512,2048]{1,0:T(8,128)(2,1)}, bf16[512,2048]{1,0:T(8,128)(2,1)}, u32[]{:S(2)}, u32[]{:S(2)}) collective-permute-start(bf16[512,2048]{1,0:T(8,128)(2,1)} %constant_dynamic-slice_fusion), channel_id=1, source_target_pairs={{64,0},{0,64},{65,1},{1,65},{66,2},{2,66},{67,3},{3,67},{68,4},{4,... | collective-permute-start | bytes 6291464 | tf_op jit(solution)/shard_map/ppermute | solution.py:26
  343.6 26.6 %copy-start.5 = (bf16[512,2048]{1,0:T(8,128)(2,1)S(1)}, bf16[512,2048]{1,0:T(8,128)(2,1)}, u32[]{:S(2)}) copy-start(bf16[512,2048]{1,0:T(8,128)(2,1)} %copy-done.3) | copy-start | bytes 6291460
  346.6 6.1 %collective-permute-start.35 = (bf16[512,128]{1,0:T(8,128)(2,1)S(1)}, bf16[512,128]{1,0:T(8,128)(2,1)S(1)}, u32[]{:S(2)}, u32[]{:S(2)}) collective-permute-start(bf16[512,128]{1,0:T(8,128)(2,1)S(1)} %get-tuple-element.114), channel_id=1, source_target_pairs={{8,0},{16,8},{24,16},{0,24},{9,1},{17,9},{25,17},{1,25},{10,2},{18... | collective-permute-start | bytes 393224 | tf_op jit(solution)/shard_map/ppermute | solution.py:26
  348.5 6.0 %collective-permute-start.36 = (bf16[512,128]{1,0:T(8,128)(2,1)S(1)}, bf16[512,128]{1,0:T(8,128)(2,1)S(1)}, u32[]{:S(2)}, u32[]{:S(2)}) collective-permute-start(bf16[512,128]{1,0:T(8,128)(2,1)S(1)} %get-tuple-element.114), channel_id=1, source_target_pairs={{16,0},{24,8},{0,16},{8,24},{17,1},{25,9},{1,17},{9,25},{18,2},{26... | collective-permute-start | bytes 393224 | tf_op jit(solution)/shard_map/ppermute | solution.py:26
  348.8 6.9 %collective-permute-start.37 = (bf16[512,128]{1,0:T(8,128)(2,1)S(1)}, bf16[512,128]{1,0:T(8,128)(2,1)S(1)}, u32[]{:S(2)}, u32[]{:S(2)}) collective-permute-start(bf16[512,128]{1,0:T(8,128)(2,1)S(1)} %get-tuple-element.114), channel_id=1, source_target_pairs={{24,0},{0,8},{8,16},{16,24},{25,1},{1,9},{9,17},{17,25},{26,2},{2,... | collective-permute-start | bytes 393224 | tf_op jit(solution)/shard_map/ppermute | solution.py:26
  349.6 6.1 %collective-permute-start.38 = (bf16[512,128]{1,0:T(8,128)(2,1)S(1)}, bf16[512,128]{1,0:T(8,128)(2,1)S(1)}, u32[]{:S(2)}, u32[]{:S(2)}) collective-permute-start(bf16[512,128]{1,0:T(8,128)(2,1)S(1)} %get-tuple-element.114), channel_id=1, source_target_pairs={{4,0},{6,2},{0,4},{2,6},{5,1},{7,3},{1,5},{3,7},{12,8},{14,10},{8,... | collective-permute-start | bytes 393224 | tf_op jit(solution)/shard_map/ppermute | solution.py:26
  355.8 14.4 %collective-permute-start.39 = (bf16[4,512,128]{2,1,0:T(8,128)(2,1)S(1)}, bf16[4,512,128]{2,1,0:T(8,128)(2,1)S(1)}, u32[]{:S(2)}, u32[]{:S(2)}) collective-permute-start(bf16[4,512,128]{2,1,0:T(8,128)(2,1)S(1)} %pad_maximum_fusion.2.refs_0_), channel_id=1, source_target_pairs={{2,0},{4,2},{6,4},{0,6},{3,1},{5,3},{7,5},{1,7},{10,8},{12,10},{14... | collective-permute-start | bytes 1572872 | tf_op jit(solution)/shard_map/ppermute | solution.py:26
  359.1 11.1 %collective-permute-start.43 = (bf16[4,512,128]{2,1,0:T(8,128)(2,1)S(1)}, bf16[4,512,128]{2,1,0:T(8,128)(2,1)S(1)}, u32[]{:S(2)}, u32[]{:S(2)}) collective-permute-start(bf16[4,512,128]{2,1,0:T(8,128)(2,1)S(1)} %pad_maximum_fusion.2.refs_0_), channel_id=1, source_target_pairs={{6,0},{0,2},{2,4},{4,6},{7,1},{1,3},{3,5},{5,7},{14,8},{8,10},{10,... | collective-permute-start | bytes 1572872 | tf_op jit(solution)/shard_map/ppermute | solution.py:26
  359.1 4.9 %collective-permute-start.40 = (bf16[512,128]{1,0:T(8,128)(2,1)S(1)}, bf16[512,128]{1,0:T(8,128)(2,1)S(1)}, u32[]{:S(2)}, u32[]{:S(2)}) collective-permute-start(bf16[512,128]{1,0:T(8,128)(2,1)S(1)} %collective-permute-done.38.refs_2_), channel_id=1, source_target_pairs={{8,0},{16,8},{24,16},{0,24},{9,1},{17,9},{25,17},{1,25},{10,2},{18... | collective-permute-start | bytes 393224 | tf_op jit(solution)/shard_map/ppermute | solution.py:26
  360.7 5.7 %collective-permute-start.41 = (bf16[512,128]{1,0:T(8,128)(2,1)S(1)}, bf16[512,128]{1,0:T(8,128)(2,1)S(1)}, u32[]{:S(2)}, u32[]{:S(2)}) collective-permute-start(bf16[512,128]{1,0:T(8,128)(2,1)S(1)} %collective-permute-done.38.refs_2_), channel_id=1, source_target_pairs={{16,0},{24,8},{0,16},{8,24},{17,1},{25,9},{1,17},{9,25},{18,2},{26... | collective-permute-start | bytes 393224 | tf_op jit(solution)/shard_map/ppermute | solution.py:26
  364.0 6.2 %collective-permute-start.42 = (bf16[512,128]{1,0:T(8,128)(2,1)S(1)}, bf16[512,128]{1,0:T(8,128)(2,1)S(1)}, u32[]{:S(2)}, u32[]{:S(2)}) collective-permute-start(bf16[512,128]{1,0:T(8,128)(2,1)S(1)} %collective-permute-done.38.refs_2_), channel_id=1, source_target_pairs={{24,0},{0,8},{8,16},{16,24},{25,1},{1,9},{9,17},{17,25},{26,2},{2,... | collective-permute-start | bytes 393224 | tf_op jit(solution)/shard_map/ppermute | solution.py:26
  372.7 9.0 %collective-permute-start.44 = (bf16[512,512]{1,0:T(8,128)(2,1)S(1)}, bf16[512,512]{1,0:T(8,128)(2,1)S(1)}, u32[]{:S(2)}, u32[]{:S(2)}) collective-permute-start(bf16[512,512]{1,0:T(8,128)(2,1)S(1)} %get-tuple-element.120), channel_id=1, source_target_pairs={{1,0},{0,1},{3,2},{2,3},{5,4},{4,5},{7,6},{6,7},{9,8},{8,9},{11,10... | collective-permute-start | bytes 1572872 | tf_op jit(solution)/shard_map/ppermute | solution.py:26
  381.6 23.5 %collective-permute-start.47 = (bf16[1024,512]{1,0:T(8,128)(2,1)S(1)}, bf16[1024,512]{1,0:T(8,128)(2,1)S(1)}, u32[]{:S(2)}, u32[]{:S(2)}) collective-permute-start(bf16[1024,512]{1,0:T(8,128)(2,1)S(1)} %get-tuple-element.131), channel_id=1, source_target_pairs={{32,0},{0,32},{33,1},{1,33},{34,2},{2,34},{35,3},{3,35},{36,4},{4,... | collective-permute-start | bytes 3145736 | tf_op jit(solution)/shard_map/ppermute | solution.py:26
  387.1 16.8 %copy-start.10 = (bf16[1024,512]{1,0:T(8,128)(2,1)S(1)}, bf16[1024,512]{1,0:T(8,128)(2,1)}, u32[]{:S(2)}) copy-start(bf16[1024,512]{1,0:T(8,128)(2,1)} %copy-done.8) | copy-start | bytes 3145732
  387.1 16.8 %copy-start.13 = (bf16[1024,512]{1,0:T(8,128)(2,1)S(1)}, bf16[1024,512]{1,0:T(8,128)(2,1)}, u32[]{:S(2)}) copy-start(bf16[1024,512]{1,0:T(8,128)(2,1)} %copy-done.11) | copy-start | bytes 3145732
  387.9 17.2 %copy-start.23 = (f32[1024,512]{1,0:T(8,128)S(1)}, f32[1024,512]{1,0:T(8,128)}, u32[]{:S(2)}) copy-start(f32[1024,512]{1,0:T(8,128)} %copy-done.22) | copy-start | bytes 6291460
  387.9 17.2 %copy-start.31 = (bf16[528,512]{1,0:T(8,128)(2,1)S(1)}, bf16[528,512]{1,0:T(8,128)(2,1)}, u32[]{:S(2)}) copy-start(bf16[528,512]{1,0:T(8,128)(2,1)} %copy-done.30) | copy-start | bytes 1622020
  387.9 17.2 %copy-start.33 = (bf16[528,512]{1,0:T(8,128)(2,1)S(1)}, bf16[528,512]{1,0:T(8,128)(2,1)}, u32[]{:S(2)}) copy-start(bf16[528,512]{1,0:T(8,128)(2,1)} %copy-done.32) | copy-start | bytes 1622020
  387.9 15.1 %collective-permute-start.48 = (bf16[512,512]{1,0:T(8,128)(2,1)S(1)}, bf16[512,512]{1,0:T(8,128)(2,1)S(1)}, u32[]{:S(2)}, u32[]{:S(2)}) collective-permute-start(bf16[512,512]{1,0:T(8,128)(2,1)S(1)} %get-tuple-element.127.d0), channel_id=1, source_target_pairs={{64,0},{0,64},{65,1},{1,65},{66,2},{2,66},{67,3},{3,67},{68,4},{4,... | collective-permute-start | bytes 1572872 | tf_op jit(solution)/shard_map/ppermute | solution.py:26
  389.2 14.6 %collective-permute-start.46 = (bf16[512,512]{1,0:T(8,128)(2,1)S(1)}, bf16[512,512]{1,0:T(8,128)(2,1)S(1)}, u32[]{:S(2)}, u32[]{:S(2)}) collective-permute-start(bf16[512,512]{1,0:T(8,128)(2,1)S(1)} %get-tuple-element.127.d0), channel_id=1, source_target_pairs={{32,0},{0,32},{33,1},{1,33},{34,2},{2,34},{35,3},{3,35},{36,4},{4,... | collective-permute-start | bytes 1572872 | tf_op jit(solution)/shard_map/ppermute | solution.py:26
  403.0 3.3 collective-permute-start.49
  406.4 22.5 %copy-start.19 = (f32[1024,512]{1,0:T(8,128)S(1)}, f32[1024,512]{1,0:T(8,128)}, u32[]{:S(2)}) copy-start(f32[1024,512]{1,0:T(8,128)} %start.3) | copy-start | bytes 6291460
  (30 other events, 152.4 us)
